TPU v7x, 256 devices: a whole 4x4x8 slice. The times are simulated.
256 devices in a mesh: grp: 8 (over z), tm: 32 (over x, y, core).
Axes of the slice: x: 4, y: 4, z: 8, core: 2. Of those that a mesh axis runs over, the one named last changes fastest.
Arguments:
- initial_state: float32 [256, 256], replicated, may hold values from -6 to 6
- retain: float32 [2048, 256], P(('grp', 'tm')), may hold values from 0 to 1
- coupling: float32 [2048, 256, 256], P(('grp', 'tm')), may hold values from -1 to 1
- probe: float32 [256], replicated, may hold values from -0.375 to 0.375
- rec_sample: int32 [256, 32, 16], P(('grp', 'tm')), may hold values from 0 to 255
- rec_step: int32 [256, 32, 16], P(('grp', 'tm')), may hold values from 0 to 7
- rec_count: int32 [256, 32], P(('grp', 'tm')), may hold values from 0 to 16, as said below
- rec_load: float32 [256, 32, 16, 256], P(('grp', 'tm')), may hold values from -1.5 to 1.5
Outputs:
- observed: float32 [2048, 256], P(('grp', 'tm'))
- slice_end: float32 [256, 256, 256], P(('grp', 'tm'))
Inputs may be any that keep to these rules, and one draw needn't show every extreme that they name: `rec_count`: A live slot count; in every draw some slice fills all 16 slots to some owner.
All inputs are finite; a program needn't handle non-finite values.
Results may differ from a plain program's by a relative error of at most 0.0003.
Values sent between devices are 32-bit elements; how exact they have to be, the bound alone decides.
No kernel may reach another device: no remote copies, remote signals or barrier semaphores. Data moves between devices by JAX's collectives and lax.ppermute only.
A program may use at most 384 MiB of HBM per device.

v0:
```python
import jax
import jax.numpy as jnp
from jax import lax
from jax.sharding import PartitionSpec as P


def carried_in(part, axis, combine, identity):
    place = lax.axis_index(axis)
    gathered = jax.tree.map(lambda a: lax.all_gather(a, axis), part)
    state = jax.tree.map(lambda a, e: jnp.zeros_like(a) + jnp.asarray(e, a.dtype), part, identity)

    def one(hop, state):
        return combine(
            state, jax.tree.map(lambda a: lax.dynamic_index_in_dim(a, hop, 0, False), gathered)
        )

    return lax.fori_loop(0, place, one, state)


def broadcast(value, axis, source):
    kept = jnp.where(lax.axis_index(axis) == source, value, 0).astype(value.dtype)
    return lax.psum(kept, axis)


def matmul(left, right):
    return jnp.dot(left, right, precision=lax.Precision.HIGHEST, preferred_element_type=jnp.float32)


def advance(field, retain_row, coupling_mat):
    crossed = lax.dot_general(
        field,
        coupling_mat,
        (((1,), (1,)), ((), ())),
        precision=lax.Precision.HIGHEST,
        preferred_element_type=jnp.float32,
    )
    return field * retain_row[None, :] + crossed


def combine(earlier, later):
    return (matmul(earlier[0], later[0]), matmul(earlier[1], later[0]) + later[1])


def body(initial_state, retain, coupling, probe, rec_sample, rec_step, rec_count, rec_load):
    steps = coupling.shape[0]
    modes = coupling.shape[1]
    samples = initial_state.shape[0]
    valid = lax.broadcasted_iota(jnp.int32, rec_sample.shape, 2) < rec_count[:, :, None]
    loads = jnp.where(valid[..., None], rec_load, jnp.float32(0.0))
    codes = rec_step * samples + rec_sample
    arrived_loads, arrived_codes = (
        lax.all_to_all(loads, "tm", split_axis=1, concat_axis=1, tiled=True),
        lax.all_to_all(codes, "tm", split_axis=1, concat_axis=1, tiled=True),
    )
    eye = jnp.eye(modes, dtype=jnp.float32)

    def compose(total, inner):
        retain_row, coupling_mat = inner
        return (advance(total, retain_row, coupling_mat), None)

    whole, _ = lax.scan(compose, eye, (retain, coupling))
    load_rows = arrived_loads.reshape(-1, modes)
    code_rows = arrived_codes.reshape(-1)
    impulse = jnp.zeros((steps * samples, modes), jnp.float32).at[code_rows].add(load_rows)
    impulse = impulse.reshape(steps, samples, modes)

    def drive(field, inner):
        retain_row, coupling_mat, kick = inner
        return (advance(field, retain_row, coupling_mat) + kick, None)

    zeros = jnp.zeros((samples, modes), jnp.float32)
    shifted, _ = lax.scan(drive, zeros, (retain, coupling, impulse))
    identity = (eye, zeros)
    inner_prior = carried_in((whole, shifted), "tm", combine, identity)
    through = combine(inner_prior, (whole, shifted))
    stacked = jnp.concatenate(through, axis=0)
    shared = broadcast(stacked, "tm", lax.axis_size("tm") - 1)
    group_map = (shared[:modes], shared[modes:])
    outer_prior = carried_in(group_map, "grp", combine, identity)
    prior = combine(outer_prior, inner_prior)
    start = matmul(initial_state, prior[0]) + prior[1]

    def replay(field, inner):
        retain_row, coupling_mat, kick = inner
        field = advance(field, retain_row, coupling_mat) + kick
        return (field, jnp.dot(field, probe, precision=lax.Precision.HIGHEST))

    final, observed = lax.scan(replay, start, (retain, coupling, impulse))
    return (observed, final[None])


def solution(mesh):
    in_specs = (
        P(),
        P(("grp", "tm"), None),
        P(("grp", "tm"), None, None),
        P(),
        P(("grp", "tm"), None, None),
        P(("grp", "tm"), None, None),
        P(("grp", "tm"), None),
        P(("grp", "tm"), None, None, None),
    )
    out_specs = (P(("grp", "tm"), None), P(("grp", "tm"), None, None))
    return jax.shard_map(body, mesh=mesh, in_specs=in_specs, out_specs=out_specs, check_vma=False)
```

profile of v0, /device:TPU:225, one launch (start us, length us, event | category | flops | bytes accessed | tf_op | source)
XLA Modules:
  0.0 590.1 jit_solution(18087318474318739095)
XLA Ops:
  7.3 16.8 %while.57 = (s32[]{:T(128)}, f32[256,256]{0,1:T(8,128)S(1)}, f32[8,256]{1,0:T(8,128)}, f32[8,256,256]{2,1,0:T(8,128)}, s32[]{:T(128)}) while((s32[]{:T(128)}, f32[256,256]{0,1:T(8,128)S(1)}, f32[8,256]{1,0:T(8,128)}, f32[8,256,256]{2,1,0:T(8,128)}, s32[]{:T(128)}) %tuple.96), condition=%wide.region_1.2_spmd, body=%wide.region_0.1_spmd.sunk | while | flops 201457664 | bytes 1576513 | solution.py:61
  25.6 7.8 %all-to-all-start = ((s32[1,32,16]{2,0,1:T(1,128)}), s32[1,32,16]{2,0,1:T(1,128)S(1)}, u32[]{:S(2)}, u32[]{:S(2)}) async-start(s32[1,32,16]{2,0,1:T(1,128)} %copy.38), calls=%async_computation | async-start | bytes 32768 | tf_op jit(solution)/shard_map/all_to_all | solution.py:53
  34.4 5.8 all-to-all-done
  40.3 4.2 all-to-all-start.1
  45.9 11.1 %all-to-all-done.1 = f32[1,32,16,256]{3,2,0,1:T(8,128)S(1)} async-done(((f32[1,32,16,256]{3,2,0,1:T(8,128)}), f32[1,32,16,256]{3,2,0,1:T(8,128)S(1)}, u32[]{:S(2)}, u32[]{:S(2)}) %all-to-all-start.1) | async-done | bytes 524320 | tf_op jit(solution)/shard_map/all_to_all | solution.py:52
  56.9 4.8 scatter_custom_fusion
  61.7 1.9 copy.40
  63.6 16.9 %while.61 = (s32[]{:T(128)}, f32[256,256]{0,1:T(8,128)S(1)}, f32[8,256]{1,0:T(8,128)}, f32[8,256,256]{2,1,0:T(8,128)}, f32[8,256,256]{1,2,0:T(8,128)S(1)}, /*index=5*/s32[]{:T(128)}, s32[]{:T(128)}) while((s32[]{:T(128)}, f32[256,256]{0,1:T(8,128)S(1)}, f32[8,256]{1,0:T(8,128)}, f32[8,256,256]{2,1,0:T(8,128)}, ...), condition=%wide.region_4.5_spmd.clone, body=%wide.region_3.4_spmd.clone.sunk | while | flops 201654272 | bytes 1840218 | solution.py:72
  68.5 1.4 fusion.101
  76.9 1.4 fusion.101
  79.1 1.4 fusion.101
  82.3 13.3 %all-gather.9.cloned.1.call-done = f32[8192,256]{0,1:T(8,128)} async-done(((f32[256,256]{0,1:T(8,128)}), f32[8192,256]{0,1:T(8,128)}) %all-gather.9.cloned.1.call-update) | async-done | bytes 8388624 | tf_op jit(solution)/shard_map/all_gather | solution.py:9
  95.6 9.0 %copy.37 = f32[8192,256]{1,0:T(8,128)} copy(f32[8192,256]{0,1:T(8,128)} %all-gather.9.cloned.1.call-done) | data formatting | bytes 16777216 | tf_op jit(solution)/shard_map/all_gather | solution.py:9
  104.6 57.8 %all-gather.11.cloned.1.call-done = f32[8192,256]{0,1:T(8,128)} async-done(((f32[256,256]{0,1:T(8,128)}), f32[8192,256]{0,1:T(8,128)}) %all-gather.11.cloned.1.call-update) | async-done | bytes 8388624 | tf_op jit(solution)/shard_map/all_gather | solution.py:9
  162.4 10.1 %copy.50 = f32[32,8,32,256]{3,2,1,0:T(8,128)} copy(f32[32,8,32,256]{3,1,2,0:T(8,128)} %bitcast.159) | data formatting | bytes 16777216
  172.6 5.2 while.58
  172.6 1.8 constant_dynamic-slice_fusion.11
  174.5 1.6 fusion.87
  176.1 1.6 convolution_bitcast_fusion.10
  180.7 261.5 %all-reduce.2.cloned.1.call-done = f32[512,256]{1,0:T(8,128)} async-done(((f32[512,256]{1,0:T(8,128)}), f32[512,256]{1,0:T(8,128)}) %all-reduce.2.cloned.1.call-update) | async-done | bytes 524304 | tf_op jit(solution)/shard_map/psum | solution.py:22
  442.2 1.9 fusion.36
  444.7 34.9 %all-gather.13.cloned.1.call-done = f32[2048,256]{1,0:T(8,128)} async-done(((f32[256,256]{1,0:T(8,128)}), f32[2048,256]{1,0:T(8,128)}) %all-gather.13.cloned.1.call-update) | async-done | bytes 2097168 | tf_op jit(solution)/shard_map/all_gather | solution.py:9
  479.6 41.5 %all-gather.15.cloned.1.call-done = f32[2048,256]{1,0:T(8,128)} async-done(((f32[256,256]{1,0:T(8,128)}), f32[2048,256]{1,0:T(8,128)}) %all-gather.15.cloned.1.call-update) | async-done | bytes 2097168 | tf_op jit(solution)/shard_map/all_gather | solution.py:9
  521.1 30.2 %while.59 = (s32[]{:T(128)}, f32[256,256]{0,1:T(8,128)S(1)}, f32[256,256]{0,1:T(8,128)S(1)}, s32[]{:T(128)}, f32[8,256,256]{2,1,0:T(8,128)}, /*index=5*/f32[8,256,256]{2,1,0:T(8,128)}, s32[]{:T(128)}, s32[]{:T(128)}, s32[]{:T(128)}) while((s32[]{:T(128)}, f32[256,256]{0,1:T(8,128)S(1)}, f32[256,256]{0,1:T(8,128)S(1)}, s32[]{:T(128)}, ...), condition=%wide.region_9.10_spmd, body=%wide.region_8.9_spmd.sunk | while | flops 402718720 | bytes 3932299 | solution.py:17
  522.3 1.6 fusion.92
  523.9 1.6 convolution_bitcast_fusion.11
  526.7 1.6 fusion.92
  528.2 1.6 convolution_bitcast_fusion.11
  531.0 1.6 fusion.92
  532.6 1.6 convolution_bitcast_fusion.11
  535.3 1.6 fusion.92
  536.9 1.6 convolution_bitcast_fusion.11
  539.6 1.6 fusion.92
  541.2 1.6 convolution_bitcast_fusion.11
  543.9 1.6 fusion.92
  545.5 1.6 convolution_bitcast_fusion.11
  548.2 1.6 fusion.92
  549.8 1.6 convolution_bitcast_fusion.11
  553.0 29.7 %while.60 = (s32[]{:T(128)}, f32[256,256]{0,1:T(8,128)S(1)}, f32[8,256]{1,0:T(8,128)}, f32[8,256]{1,0:T(8,128)}, f32[8,256,256]{2,1,0:T(8,128)}, /*index=5*/f32[...) while((s32[]{:T(128)}, f32[256,256]{0,1:T(8,128)S(1)}, f32[8,256]{1,0:T(8,128)}, ...), condition=%wide.region_11.12_spmd, body=%wide.region_10.11_spmd.sunk | while | flops 202309632 | bytes 2105445 | solution.py:88
  553.8 1.4 fusion.97
  557.5 1.4 fusion.97
  561.2 1.4 fusion.97
  562.8 1.3 dynamic_update_slice.5
  564.9 1.4 fusion.97
  568.6 1.4 fusion.97
  572.3 1.4 fusion.97
  576.0 1.4 fusion.97
  579.7 1.4 fusion.97
  (168 shorter events, 65.7 us)
Async XLA Ops:
  7.2 544.8 %copy-start = (f32[256,256]{1,0:T(8,128)S(1)}, f32[256,256]{1,0:T(8,128)}, u32[]{:S(2)}) copy-start(f32[256,256]{1,0:T(8,128)} %param.18) | copy-start | bytes 786436
  7.2 88.4 %all-gather.9.cloned.1.call-start = ((), (), s32[]{:S(2)}) async-start(), calls=%async_computation.3 | async-start | bytes 8650752 | tf_op jit(solution)/shard_map/all_gather | solution.py:9
  7.2 74.0 %copy-start.1 = (f32[256,256]{0,1:T(8,128)}, f32[256,256]{0,1:T(8,128)S(1)}, u32[]{:S(2)}) copy-start(f32[256,256]{0,1:T(8,128)S(1)} %fusion.35) | copy-start | bytes 786436
  7.3 17.6 %copy-start.12 = (s32[1,32,16]{1,2,0:T(8,128)S(1)}, s32[1,32,16]{1,2,0:T(8,128)}, u32[]{:S(2)}) copy-start(s32[1,32,16]{1,2,0:T(8,128)} %param.22) | copy-start | bytes 6148
  7.3 17.6 %copy-start.13 = (s32[1,32,16]{1,2,0:T(8,128)S(1)}, s32[1,32,16]{1,2,0:T(8,128)}, u32[]{:S(2)}) copy-start(s32[1,32,16]{1,2,0:T(8,128)} %param.23) | copy-start | bytes 6148
  7.3 26.0 %copy-start.14 = (s32[1,32]{1,0:T(1,128)S(1)}, s32[1,32]{1,0:T(1,128)}, u32[]{:S(2)}) copy-start(s32[1,32]{1,0:T(1,128)} %param.24) | copy-start | bytes 388
  7.3 26.1 %copy-start.10 = (f32[1,32,16,256]{3,2,1,0:T(8,128)S(1)}, f32[1,32,16,256]{3,2,1,0:T(8,128)}, u32[]{:S(2)}) copy-start(f32[1,32,16,256]{3,2,1,0:T(8,128)} %param.25) | copy-start | bytes 1572868
  24.1 0.7 copy-start.6
  25.6 14.7 %all-to-all-start = ((s32[1,32,16]{2,0,1:T(1,128)}), s32[1,32,16]{2,0,1:T(1,128)S(1)}, u32[]{:S(2)}, u32[]{:S(2)}) async-start(s32[1,32,16]{2,0,1:T(1,128)} %copy.38), calls=%async_computation | async-start | bytes 32768 | tf_op jit(solution)/shard_map/all_to_all | solution.py:53
  40.3 16.6 %all-to-all-start.1 = ((f32[1,32,16,256]{3,2,0,1:T(8,128)}), f32[1,32,16,256]{3,2,0,1:T(8,128)S(1)}, u32[]{:S(2)}, u32[]{:S(2)}) async-start(f32[1,32,16,256]{3,2,0,1:T(8,128)} %bitcast_select_fusion), calls=%async_computation.1 | async-start | bytes 1048576 | tf_op jit(solution)/shard_map/all_to_all | solution.py:52
  44.5 118.0 %all-gather.11.cloned.1.call-start = ((), (), s32[]{:S(2)}) async-start(), calls=%async_computation.4 | async-start | bytes 8650752 | tf_op jit(solution)/shard_map/all_gather | solution.py:9
  80.5 0.7 copy-start.8
  80.5 24.1 %copy-start.9 = (f32[8,256,256]{1,2,0:T(8,128)}, f32[8,256,256]{1,2,0:T(8,128)S(1)}, u32[]{:S(2)}) copy-start(f32[8,256,256]{1,2,0:T(8,128)S(1)} %get-tuple-element.626) | copy-start | bytes 6291460
  81.2 361.0 %all-reduce.2.cloned.1.call-start = ((), (), s32[]{:S(2)}) async-start(), calls=%async_computation.2 | async-start | bytes 1048576 | tf_op jit(solution)/shard_map/psum | solution.py:22
  162.4 10.2 %copy-start.5 = (f32[256,256]{0,1:T(8,128)S(1)}, f32[256,256]{0,1:T(8,128)}, u32[]{:S(2)}) copy-start(f32[256,256]{0,1:T(8,128)} %copy-done.1) | copy-start | bytes 786436
  172.6 5.9 %copy-start.7 = (f32[256,256]{0,1:T(8,128)S(1)}, f32[256,256]{0,1:T(8,128)}, u32[]{:S(2)}) copy-start(f32[256,256]{0,1:T(8,128)} %copy-done.6) | copy-start | bytes 786436
  177.8 0.7 copy-start.3
  179.1 342.0 %copy-start.2 = (f32[256,256]{0,1:T(8,128)S(1)}, f32[256,256]{0,1:T(8,128)}, u32[]{:S(2)}) copy-start(f32[256,256]{0,1:T(8,128)} %copy-done.1) | copy-start | bytes 786436
  180.6 299.0 %all-gather.13.cloned.1.call-start = ((), (), s32[]{:S(2)}) async-start(), calls=%async_computation.5 | async-start | bytes 2359296 | tf_op jit(solution)/shard_map/all_gather | solution.py:9
  444.1 77.0 %all-gather.15.cloned.1.call-start = ((), (), s32[]{:S(2)}) async-start(), calls=%async_computation.6 | async-start | bytes 2359296 | tf_op jit(solution)/shard_map/all_gather | solution.py:9
  521.1 30.2 %copy-start.4 = (f32[256,256]{0,1:T(8,128)S(1)}, f32[256,256]{0,1:T(8,128)}, u32[]{:S(2)}) copy-start(f32[256,256]{0,1:T(8,128)} %copy-done.3) | copy-start | bytes 786436
  551.4 1.6 copy-start.11
Sparse Core Ops, SparseCore 0:
  25.0 70.5 all-gather.8
  98.1 64.3 all-gather.10
  180.8 261.4 all-reduce.1
  444.2 35.3 all-gather.12
  481.4 39.6 all-gather.14
where the time goes:
time: 600 us; the launch traced here: 590 us
  waiting for transfers between devices  426 us (71%)
  local copies, waits for them, and re-layouts  66.4 us (11%)
  matrix products  62.2 us (10%)
  between operations  14.1 us (2%)
  starting transfers between devices  12.2 us (2%)
  other arithmetic  7.4 us (1%)
    psum x1, waiting for transfers between devices, broadcast(): return lax.psum(kept, axis)  262 us
    all_gather x4, waiting for transfers between devices, carried_in(): gathered = jax.tree.map(lambda a: lax.all_gather(a, axis), part)  147 us
    dot_general x24, matrix products, advance(): lax.dot_general(field, coupling_mat, (((1,), (1,)), ((), ())), precision=...  32.9 us
    dot_general x21, matrix products, matmul(): jnp.dot(left, right, precision=lax.Precision.HIGHEST, preferred_element_t...  27.6 us
    dynamic_slice x24, local copies, waits for them, and re-layouts, body(): whole, _ = lax.scan(compose, eye, (retain, coupling))  17 us
    unnamed x33, local copies, waits for them, and re-layouts  14.2 us
  transfers between devices with their start and end apart: 7, of which 7 were waited for; matrix products, arithmetic and copies ran while one was open for 6% of the time, Pallas kernels for 0%

commit v1 on v0

v1 whole, which is shorter than its diff:
```python
import functools

import jax
import jax.numpy as jnp
from jax import lax
from jax.experimental import pallas as pl
from jax.experimental.pallas import tpu as pltpu
from jax.sharding import PartitionSpec as P

F32 = jnp.float32
BF16 = jnp.bfloat16
NY = 4
NX = 4
SHIFTS = (1, 3, 2)


def split(a):
    hi = a.astype(BF16)
    return hi, (a - hi.astype(F32)).astype(BF16)


def dot(a, b, transposed=False):
    dims = (((1,), (1 if transposed else 0,)), ((), ()))
    return lax.dot_general(a, b, dims, preferred_element_type=F32)


def mm(left, right, transposed=False):
    ah, al = left
    bh, bl = right
    return dot(ah, bh, transposed) + (dot(ah, bl, transposed) + dot(al, bh, transposed))


def call(kernel, name, outs, *args, scratch=(), flops=0):
    shapes = [jax.ShapeDtypeStruct(s, F32) for s in outs]
    smem = pl.BlockSpec(memory_space=pltpu.SMEM)
    vmem = pl.BlockSpec(memory_space=pltpu.VMEM)
    moved = sum(4 * a.size for a in args) + sum(4 * s.size for s in shapes)
    return pl.pallas_call(
        kernel,
        out_shape=shapes,
        in_specs=[smem] + [vmem] * (len(args) - 1),
        out_specs=[vmem] * len(shapes),
        scratch_shapes=list(scratch),
        name=name,
        cost_estimate=pl.CostEstimate(flops=flops, bytes_accessed=moved, transcendentals=0),
        compiler_params=pltpu.CompilerParams(vmem_limit_bytes=32 * 1024 * 1024),
    )(*args)


def compose_kernel(pos, retain, coupling, whole):
    steps, modes = retain.shape
    rows = lax.broadcasted_iota(jnp.int32, (modes, modes), 0)
    cols = lax.broadcasted_iota(jnp.int32, (modes, modes), 1)
    total = coupling[0].T + jnp.where(rows == cols, retain[0:1, :], 0.0)
    for t in range(1, steps):
        total = total * retain[t : t + 1, :] + mm(split(total), split(coupling[t]), True)
    whole[...] = total


def weights_kernel(pos, retain, coupling, probe, seen):
    steps, modes = retain.shape
    rows = lax.broadcasted_iota(jnp.int32, (steps, modes), 0)
    state = jnp.zeros((steps, modes), F32)
    for t in range(steps - 1, -1, -1):
        state = jnp.where(rows == t, probe[...], state)
        state = state * retain[t : t + 1, :] + mm(split(state), split(coupling[t]))
    seen[...] = state


def drive_kernel(pos, arrived, retain, coupling, probe, shifted, kept, sent, seen):
    steps, modes = retain.shape
    sources, half, _ = arrived.shape
    n = sources * half
    samples = shifted.shape[0]
    loads = jnp.concatenate(
        [
            arrived[:, :, 0:modes].reshape(n, modes),
            arrived[:, :, modes : 2 * modes].reshape(n, modes),
        ],
        axis=0,
    )
    lh, ll = split(loads)
    codes = arrived[:, :, 2 * modes : 2 * modes + 128].reshape(n, 128).T
    codes = jnp.concatenate([codes[0:1, :], codes[1:2, :]], axis=1).astype(jnp.int32)
    place = lax.broadcasted_iota(jnp.int32, (samples, 2 * n), 0)
    ph, pw = split(jnp.broadcast_to(probe[...], (8, modes)))
    rows = lax.broadcasted_iota(jnp.int32, (8, samples), 0)
    shown = jnp.zeros((8, samples), F32)
    field = None
    for t in range(steps):
        hit = jnp.where(place + t * samples == codes, 1.0, 0.0).astype(BF16)
        kick = dot(hit, lh) + dot(hit, ll)
        if t > 0:
            kick = kick + field * retain[t : t + 1, :] + mm(parts, split(coupling[t]), True)
        field = kick
        parts = split(field)
        shown = jnp.where(rows == t, mm((ph, pw), parts, True), shown)
    shifted[...] = field
    seen[...] = shown
    c = pos[0]
    h = samples // 2

    @pl.when(c == 0)
    def _():
        kept[...] = field[:h]
        sent[...] = field[h:]

    @pl.when(c != 0)
    def _():
        kept[...] = field[h:]
        sent[...] = field[:h]


def pair_kernel(pos, mine, other, both, chip):
    c = pos[0]

    @pl.when(c == 0)
    def _():
        both[0] = mine[...]
        both[1] = other[...]

    @pl.when(c != 0)
    def _():
        both[0] = other[...]
        both[1] = mine[...]

    chip[...] = mm(split(both[0]), split(both[1]))


def order(place, count, ordered, refs):
    ordered[place] = refs[0][...]
    for s, ref in zip(SHIFTS, refs[1:]):
        ordered[lax.rem(place + count - s, count)] = ref[...]


def line_map_kernel(pos, a0, a1, a3, a2, ordered, prefix, line):
    order(pos[1], NY, ordered, (a0, a1, a3, a2))
    total = ordered[0]
    for k in range(1, NY):
        prefix[k - 1] = total
        total = mm(split(total), split(ordered[k]))
    line[...] = total


def group_map_kernel(pos, a0, a1, a3, a2, prefix, ordered, through, group, before):
    x = pos[2]
    order(x, NX, ordered, (a0, a1, a3, a2))
    modes = group.shape[0]
    rows = lax.broadcasted_iota(jnp.int32, (modes, modes), 0)
    cols = lax.broadcasted_iota(jnp.int32, (modes, modes), 1)
    before[0] = jnp.where(rows == cols, 1.0, 0.0)
    total = ordered[0]
    for k in range(1, NX):
        before[k] = total
        total = mm(split(total), split(ordered[k]))
    group[...] = total
    own = before[x]
    through[0] = own
    own = split(own)
    for k in range(1, NY):
        through[k] = mm(own, split(prefix[k - 1]))


def product_kernel(pos, left, right, out):
    out[...] = mm(split(left[...]), split(right[...]))


def pair_shift_kernel(pos, kept, got, both, first, s0, s1, s3, s2, chip):
    c = pos[0]
    y = pos[1]
    r = s0.shape[0]
    mine = kept[...]
    theirs = got[...]
    zero = jnp.where(c == 0, mine, theirs)
    one = jnp.where(c == 0, theirs, mine)
    first[...] = zero
    chip[...] = mm(split(zero), split(both[1])) + one
    for s, out in zip((0,) + SHIFTS, (s0, s1, s3, s2)):
        start = pl.multiple_of(lax.rem(y + s, NY) * r, r)
        out[...] = chip[pl.ds(start, r), :]


def line_shift_kernel(pos, b0, b1, b3, b2, maps, before, line, ordered):
    order(pos[1], NY, ordered, (b0, b1, b3, b2))
    total = ordered[0]
    for k in range(1, NY):
        before[k - 1] = total
        total = mm(split(total), split(maps[k])) + ordered[k]
    line[...] = total


def group_shift_kernel(pos, b0, b1, b3, b2, maps, prefix, before, through, group, ordered, own):
    x = pos[2]
    order(x, NX, ordered, (b0, b1, b3, b2))
    own[0] = jnp.zeros_like(ordered[0])
    total = ordered[0]
    for k in range(1, NX):
        own[k] = total
        total = mm(split(total), split(maps[k])) + ordered[k]
    group[...] = total
    prior = own[x]
    through[0] = prior
    prior = split(prior)
    for k in range(1, NY):
        through[k] = mm(prior, split(prefix[k - 1])) + before[k - 1]


def first_hop_kernel(pos, initial, got1, got2, before, out):
    c, y, g = pos[0], pos[1], pos[3]
    r = out.shape[0]
    start = pl.multiple_of(c * (NY * r) + y * r, r)
    released = initial[pl.ds(start, r), :]
    near = jnp.where(g == 0, released, got1[...])
    far = jnp.where(g == 1, released, got2[...])
    far = jnp.where(g == 0, 0.0, far)
    out[...] = near + mm(split(far), split(before[...]))


def hop_kernel(pos, mine, got, before, out):
    out[...] = mine[...] + mm(split(got[...]), split(before[...]))


def last_hop_kernel(pos, mine, got, before, maps, shifts, s0, s1, s3, s2, chips):
    y = pos[1]
    group = split(mine[...] + mm(split(got[...]), split(before[...])))
    for k in range(NY):
        chips[k] = mm(group, split(maps[k])) + shifts[k]
    for s, out in zip((0,) + SHIFTS, (s0, s1, s3, s2)):
        out[...] = chips[lax.rem(y + s, NY)]


def chip_kernel(pos, e0, e1, e3, e2, both, first, kept, sent, chip):
    c, y = pos[0], pos[1]
    r = e0.shape[0]
    for s, ref in zip((0,) + SHIFTS, (e0, e1, e3, e2)):
        start = pl.multiple_of(lax.rem(y + NY - s, NY) * r, r)
        chip[pl.ds(start, r), :] = ref[...]
    zero = chip[...]
    one = mm(split(zero), split(both[0])) + first[...]
    kept[...] = jnp.where(c == 0, zero, one)
    sent[...] = jnp.where(c == 0, one, zero)


def finish_kernel(pos, kept, got, whole, shifted, weights, driven, observed, final, start):
    c = pos[0]
    h = kept.shape[0]

    @pl.when(c == 0)
    def _():
        start[:h] = kept[...]
        start[h:] = got[...]

    @pl.when(c != 0)
    def _():
        start[:h] = got[...]
        start[h:] = kept[...]

    parts = split(start[...])
    final[...] = mm(parts, split(whole[...])) + shifted[...]
    observed[...] = mm(split(weights[...]), parts, True) + driven[...]


def body(initial_state, retain, coupling, probe, rec_sample, rec_step, rec_count, rec_load):
    steps, modes, _ = coupling.shape
    samples = initial_state.shape[0]
    owners, cap = rec_sample.shape[1:]
    half = samples // 2
    part = half // NY
    mat = (modes, modes)
    vm = lambda *s: pltpu.VMEM(s, F32)

    t = lax.axis_index("tm")
    g = lax.axis_index("grp")
    pos = jnp.stack([t % 2, (t // 2) % NY, t // (2 * NY), g]).astype(jnp.int32)

    def at(x, y, c):
        return (x * NY + y) * 2 + c

    spots = [(x, y, c) for x in range(NX) for y in range(NY) for c in range(2)]
    swap = [(at(x, y, c), at(x, y, 1 - c)) for x, y, c in spots]

    def along_y(s):
        return [(at(x, y, c), at(x, (y + s) % NY, c)) for x, y, c in spots]

    def along_x(s):
        return [(at(x, y, c), at((x + s) % NX, y, c)) for x, y, c in spots]

    n_grp = lax.axis_size("grp")

    def later(a, s):
        return lax.ppermute(a, "grp", [(i, i + s) for i in range(n_grp - s)])

    slot = lax.broadcasted_iota(jnp.int32, rec_sample.shape, 2)
    codes = jnp.where(slot < rec_count[:, :, None], rec_step * samples + rec_sample, -1)
    codes = codes[0].astype(F32)
    lane = lax.broadcasted_iota(jnp.int32, (owners, cap // 2, 128), 2)
    tags = jnp.where(
        lane == 0,
        codes[:, : cap // 2, None],
        jnp.where(lane == 1, codes[:, cap // 2 :, None], 0.0),
    )
    packed = jnp.concatenate(
        [rec_load[0, :, : cap // 2], rec_load[0, :, cap // 2 :], tags], axis=-1
    )
    arrived = lax.all_to_all(packed, "tm", split_axis=0, concat_axis=0)

    cube = 2 * modes * modes * modes
    probe_row = probe[None, :]
    (whole,) = call(compose_kernel, "compose", [mat], pos, retain, coupling, flops=21 * cube)
    other = lax.ppermute(whole, "tm", swap)
    both, chip = call(pair_kernel, "pair_map", [(2,) + mat, mat], pos, whole, other, flops=3 * cube)
    got = [lax.ppermute(chip, "tm", along_y(s)) for s in SHIFTS]
    y_maps, y_before, line = call(
        line_map_kernel,
        "line_map",
        [(NY,) + mat, (NY - 1,) + mat, mat],
        pos,
        chip,
        *got,
        flops=9 * cube,
    )
    got = [lax.ppermute(line, "tm", along_x(s)) for s in SHIFTS]
    x_maps, through, group = call(
        group_map_kernel,
        "group_map",
        [(NX,) + mat, (NY,) + mat, mat],
        pos,
        line,
        *got,
        y_before,
        scratch=[vm(NX, *mat)],
        flops=18 * cube,
    )
    g1 = later(group, 1)
    g2 = later(group, 2)
    (h1,) = call(product_kernel, "two_groups", [mat], pos, g2, g1, flops=3 * cube)
    h1_far = later(h1, 2)
    (h2,) = call(product_kernel, "four_groups", [mat], pos, h1_far, h1, flops=3 * cube)

    (weights,) = call(
        weights_kernel, "weights", [(steps, modes)], pos, retain, coupling, probe_row, flops=cube
    )
    shifted, kept, sent, driven = call(
        drive_kernel,
        "drive",
        [mat, (half, modes), (half, modes), (steps, samples)],
        pos,
        arrived,
        retain,
        coupling,
        probe_row,
        flops=60 * cube,
    )
    back = lax.ppermute(sent, "tm", swap)
    small = (part, modes)
    first, *rows = call(
        pair_shift_kernel,
        "pair_shift",
        [(half, modes)] + [small] * 4,
        pos,
        kept,
        back,
        both,
        scratch=[vm(half, modes)],
        flops=cube,
    )
    got = [lax.ppermute(r, "tm", along_y(s)) for r, s in zip(rows[1:], SHIFTS)]
    b_before, b_line = call(
        line_shift_kernel,
        "line_shift",
        [(NY - 1,) + small, small],
        pos,
        rows[0],
        *got,
        y_maps,
        scratch=[vm(NY, *small)],
        flops=cube,
    )
    got = [lax.ppermute(b_line, "tm", along_x(s)) for s in SHIFTS]
    b_through, b_group = call(
        group_shift_kernel,
        "group_shift",
        [(NY,) + small, small],
        pos,
        b_line,
        *got,
        x_maps,
        y_before,
        b_before,
        scratch=[vm(NX, *small), vm(NX, *small)],
        flops=2 * cube,
    )
    (e,) = call(
        first_hop_kernel,
        "hop1",
        [small],
        pos,
        initial_state,
        later(b_group, 1),
        later(b_group, 2),
        g1,
        flops=cube,
    )
    (e,) = call(hop_kernel, "hop2", [small], pos, e, later(e, 2), h1, flops=cube)
    rows = call(
        last_hop_kernel,
        "hop4",
        [small] * 4,
        pos,
        e,
        later(e, 4),
        h2,
        through,
        b_through,
        scratch=[vm(NY, *small)],
        flops=2 * cube,
    )
    got = [lax.ppermute(r, "tm", along_y(s)) for r, s in zip(rows[1:], SHIFTS)]
    kept, sent = call(
        chip_kernel,
        "chip_start",
        [(half, modes)] * 2,
        pos,
        rows[0],
        *got,
        both,
        first,
        scratch=[vm(half, modes)],
        flops=cube,
    )
    back = lax.ppermute(sent, "tm", swap)
    observed, final = call(
        finish_kernel,
        "finish",
        [(steps, samples), mat],
        pos,
        kept,
        back,
        whole,
        shifted,
        weights,
        driven,
        scratch=[vm(samples, modes)],
        flops=3 * cube,
    )
    return observed, final[None]


def solution(mesh):
    in_specs = (
        P(),
        P(("grp", "tm"), None),
        P(("grp", "tm"), None, None),
        P(),
        P(("grp", "tm"), None, None),
        P(("grp", "tm"), None, None),
        P(("grp", "tm"), None),
        P(("grp", "tm"), None, None, None),
    )
    out_specs = (P(("grp", "tm"), None), P(("grp", "tm"), None, None))
    return jax.shard_map(body, mesh=mesh, in_specs=in_specs, out_specs=out_specs, check_vma=False)
```

time: 600 us -> 138 us (0.23)
  the two profiles are of different devices: /device:TPU:225 before, /device:TPU:1 now
where the time goes in v1:
time: 138 us; the launch traced here: 137 us
  starting transfers between devices  80 us (58%)
  Pallas kernels  26.2 us (19%)
  waiting for transfers between devices  23.5 us (17%)
  local copies, waits for them, and re-layouts  5.52 us (4%)
    ppermute x7, starting transfers between devices, later(): return lax.ppermute(a, 'grp', [(i, i + s) for i in range(n_grp - s)])  33.8 us
    pallas_call x16, Pallas kernels, call(): pl.pallas_call(kernel, out_shape=shapes, in_specs=[smem] + [vmem] * (len(...  26.2 us
    ppermute x2, starting transfers between devices, body(): back = lax.ppermute(sent, 'tm', swap)  16.4 us
    ppermute x6, starting transfers between devices, body(): got = [lax.ppermute(r, 'tm', along_y(s)) for r, s in zip(rows[1:], SHIFTS)]  9.26 us
    ppermute x3, waiting for transfers between devices, body(): got = [lax.ppermute(line, 'tm', along_x(s)) for s in SHIFTS]  8.15 us
    all_to_all x1, starting transfers between devices, body(): arrived = lax.all_to_all(packed, 'tm', split_axis=0, concat_axis=0)  6.8 us
    unnamed x36, local copies, waits for them, and re-layouts  5.33 us
    ppermute x6, waiting for transfers between devices, body(): got = [lax.ppermute(r, 'tm', along_y(s)) for r, s in zip(rows[1:], SHIFTS)]  5.18 us
  transfers between devices with their start and end apart: 26, of which 14 were waited for; matrix products, arithmetic and copies ran while one was open for 1% of the time, Pallas kernels for 14%

profile of v1, /device:TPU:1, one launch (start us, length us, event | category | flops | bytes accessed | tf_op | source)
XLA Modules:
  0.0 137.4 jit_solution(4478132359714585257)
XLA Ops:
  0.8 1.6 %copy-done = f32[8,256,256]{2,1,0:T(8,128)S(1)} copy-done((f32[8,256,256]{2,1,0:T(8,128)S(1)}, f32[8,256,256]{2,1,0:T(8,128)}, u32[]{:S(2)}) %copy-start) | copy-done | bytes 2097176
  3.1 2.4 %compose.1.mine.whole = f32[256,256]{1,0:T(8,128)S(1)} custom-call(s32[4]{0:T(128)S(1)} %pad_add_fusion.pos, f32[8,256]{1,0:T(8,128)S(1)} %copy-done.11, f32[8,256,256]{2,1,0:T(8,128)S(1)} %copy-done), custom_call_target="tpu_custom_call" | custom-call | flops 704643072 | bytes 2367504 | tf_op jit(solution)/shard_map/compose/pallas_call | solution.py:38
  5.5 3.3 %collective-permute-start.1 = (f32[256,256]{1,0:T(8,128)S(1)}, f32[256,256]{1,0:T(8,128)S(1)}, u32[]{:S(2)}, u32[]{:S(2)}) collective-permute-start(f32[256,256]{1,0:T(8,128)S(1)} %compose.1.mine.whole), channel_id=1, source_target_pairs={{0,1},{1,0},{2,3},{3,2},{4,5},{5,4},{6,7},{7,6},{8,9},{9,8},{10,11... | collective-permute-start | bytes 786440 | tf_op jit(solution)/shard_map/ppermute | solution.py:310
  10.0 0.9 pair_map.1
  11.0 2.7 %collective-permute-start.6 = (f32[256,256]{1,0:T(8,128)S(1)}, f32[256,256]{1,0:T(8,128)}, u32[]{:S(2)}, u32[]{:S(2)}) collective-permute-start(f32[256,256]{1,0:T(8,128)S(1)} %get-tuple-element.38.a0), channel_id=1, source_target_pairs={{0,6},{1,7},{2,0},{3,1},{4,2},{5,3},{6,4},{7,5},{8,14},{9,15},{10,... | collective-permute-start | bytes 786440 | tf_op jit(solution)/shard_map/ppermute | solution.py:312
  13.6 0.9 pad_maximum_fusion
  14.5 6.8 %all-to-all-start = ((f32[32,8,640]{2,1,0:T(8,128)}), f32[32,8,640]{2,1,0:T(8,128)}, u32[]{:S(2)}, u32[]{:S(2)}) async-start(f32[32,8,640]{2,1,0:T(8,128)} %pad_maximum_fusion), calls=%async_computation | async-start | bytes 1310720 | tf_op jit(solution)/shard_map/all_to_all | solution.py:305
  21.4 3.6 %collective-permute-done.7.a2 = f32[256,256]{1,0:T(8,128)} collective-permute-done((f32[256,256]{1,0:T(8,128)S(1)}, f32[256,256]{1,0:T(8,128)}, u32[]{:S(2)}, u32[]{:S(2)}) %collective-permute-start.7) | collective-permute-done | bytes 262176 | tf_op jit(solution)/shard_map/ppermute | solution.py:312
  24.9 2.0 %line_map.1 = (f32[4,256,256]{2,1,0:T(8,128)S(1)}, f32[3,256,256]{2,1,0:T(8,128)S(1)}, f32[256,256]{1,0:T(8,128)S(1)}) custom-call(s32[4]{0:T(128)S(1)} %pad_add_fusion.pos, f32[256,256]{1,0:T(8,128)S(1)} %get-tuple-element.38.a0, f32[256,256]{1,0:T(8,128)S(1)} %collective-permute-done.5.a1, f32[256,256]{1,0:T(8,128)} %collective-permute-done.6.a3, ...), custom_call_target="tpu_custom_call" | custom-call | flops 301989888 | bytes 3145744 | tf_op jit(solution)/shard_map/line_map/pallas_call | solution.py:38
  26.9 1.0 copy-done.6
  27.9 1.2 collective-permute-start.11
  29.1 1.5 %collective-permute-start.12 = (f32[256,256]{1,0:T(8,128)S(1)}, f32[256,256]{1,0:T(8,128)S(1)}, u32[]{:S(2)}, u32[]{:S(2)}) collective-permute-start(f32[256,256]{1,0:T(8,128)S(1)} %get-tuple-element.41.a0), channel_id=1, source_target_pairs={{0,24},{1,25},{2,26},{3,27},{4,28},{5,29},{6,30},{7,31},{8,0},{9,1... | collective-permute-start | bytes 786440 | tf_op jit(solution)/shard_map/ppermute | solution.py:322
  30.6 1.5 %collective-permute-start.13 = (f32[256,256]{1,0:T(8,128)S(1)}, f32[256,256]{1,0:T(8,128)S(1)}, u32[]{:S(2)}, u32[]{:S(2)}) collective-permute-start(f32[256,256]{1,0:T(8,128)S(1)} %get-tuple-element.41.a0), channel_id=1, source_target_pairs={{0,16},{1,17},{2,18},{3,19},{4,20},{5,21},{6,22},{7,23},{8,24},{9,... | collective-permute-start | bytes 786440 | tf_op jit(solution)/shard_map/ppermute | solution.py:322
  32.1 2.8 %collective-permute-done.11.a1 = f32[256,256]{1,0:T(8,128)S(1)} collective-permute-done((f32[256,256]{1,0:T(8,128)S(1)}, f32[256,256]{1,0:T(8,128)S(1)}, u32[]{:S(2)}, u32[]{:S(2)}) %collective-permute-start.11) | collective-permute-done | bytes 262176 | tf_op jit(solution)/shard_map/ppermute | solution.py:322
  34.9 1.8 %collective-permute-done.12.a3 = f32[256,256]{1,0:T(8,128)S(1)} collective-permute-done((f32[256,256]{1,0:T(8,128)S(1)}, f32[256,256]{1,0:T(8,128)S(1)}, u32[]{:S(2)}, u32[]{:S(2)}) %collective-permute-start.12) | collective-permute-done | bytes 262176 | tf_op jit(solution)/shard_map/ppermute | solution.py:322
  36.7 3.5 %collective-permute-done.13.a2 = f32[256,256]{1,0:T(8,128)S(1)} collective-permute-done((f32[256,256]{1,0:T(8,128)S(1)}, f32[256,256]{1,0:T(8,128)S(1)}, u32[]{:S(2)}, u32[]{:S(2)}) %collective-permute-start.13) | collective-permute-done | bytes 262176 | tf_op jit(solution)/shard_map/ppermute | solution.py:322
  40.2 2.3 %group_map.1 = (f32[4,256,256]{2,1,0:T(8,128)S(1)}, f32[4,256,256]{2,1,0:T(8,128)S(1)}, f32[256,256]{1,0:T(8,128)}) custom-call(s32[4]{0:T(128)S(1)} %pad_add_fusion.pos, f32[256,256]{1,0:T(8,128)S(1)} %get-tuple-element.41.a0, f32[256,256]{1,0:T(8,128)S(1)} %collective-permute-done.11.a1, f32[256,256]{1,0:T(8,128)S(1)} %collective-permute-done.12.a3, ...), custom_call_target="tpu_custom_call" | custom-call | flops 603979776 | bytes 4194320 | tf_op jit(solution)/shard_map/group_map/pallas_call | solution.py:38
  42.5 1.0 copy-done.2
  43.5 1.0 copy-done.4
  44.5 3.5 %collective-permute-start.16 = (f32[256,256]{1,0:T(8,128)}, f32[256,256]{1,0:T(8,128)S(1)}, u32[]{:S(2)}, u32[]{:S(2)}) collective-permute-start(f32[256,256]{1,0:T(8,128)} %get-tuple-element.46), channel_id=1, source_target_pairs={{0,32},{32,64},{64,96},{96,128},{128,160},{160,192},{192,224},{1,3... | collective-permute-start | bytes 786440 | tf_op jit(solution)/shard_map/ppermute | solution.py:291
  48.0 5.1 %collective-permute-start.18 = (f32[256,256]{1,0:T(8,128)}, f32[256,256]{1,0:T(8,128)S(1)}, u32[]{:S(2)}, u32[]{:S(2)}) collective-permute-start(f32[256,256]{1,0:T(8,128)} %get-tuple-element.46), channel_id=1, source_target_pairs={{0,64},{32,96},{64,128},{96,160},{128,192},{160,224},{1,65},{33,97... | collective-permute-start | bytes 786440 | tf_op jit(solution)/shard_map/ppermute | solution.py:291
  53.2 7.2 %drive.1 = (f32[256,256]{1,0:T(8,128)S(1)}, f32[128,256]{1,0:T(8,128)S(1)}, f32[128,256]{1,0:T(8,128)S(1)}, f32[8,256]{1,0:T(8,128)S(1)}) custom-call(s32[4]{0:T(128)S(1)} %pad_add_fusion.pos, f32[32,8,640]{2,1,0:T(8,128)} %all-to-all-done.arrived, f32[8,256]{1,0:T(8,128)S(1)} %copy-done.12, f32[8,256,256]{2,1,0:T(8,128)S(1)} %copy-done.1, f32[1,256]{1,0:T(1,128)S(1)} %bitcast.13), custom_call_target="tpu_custom_call" | custom-call | flops 2013265920 | bytes 3294224 | tf_op jit(solution)/shard_map/drive/pallas_call | solution.py:38
  60.4 4.7 %collective-permute-start = (f32[128,256]{1,0:T(8,128)S(1)}, f32[128,256]{1,0:T(8,128)S(1)}, u32[]{:S(2)}, u32[]{:S(2)}) collective-permute-start(f32[128,256]{1,0:T(8,128)S(1)} %get-tuple-element.32), channel_id=1, source_target_pairs={{0,1},{1,0},{2,3},{3,2},{4,5},{5,4},{6,7},{7,6},{8,9},{9,8},{10,11... | collective-permute-start | bytes 393224 | tf_op jit(solution)/shard_map/ppermute | solution.py:354
  65.2 0.8 two_groups.1.before.right
  66.0 5.3 %collective-permute-start.20 = (f32[256,256]{1,0:T(8,128)S(1)}, f32[256,256]{1,0:T(8,128)S(1)}, u32[]{:S(2)}, u32[]{:S(2)}) collective-permute-start(f32[256,256]{1,0:T(8,128)S(1)} %two_groups.1.before.right), channel_id=1, source_target_pairs={{0,64},{32,96},{64,128},{96,160},{128,192},{160,224},{1,65},{33,97... | collective-permute-start | bytes 786440 | tf_op jit(solution)/shard_map/ppermute | solution.py:291
  72.1 1.7 %collective-permute-start.2 = (f32[32,256]{1,0:T(8,128)S(1)}, f32[32,256]{1,0:T(8,128)S(1)}, u32[]{:S(2)}, u32[]{:S(2)}) collective-permute-start(f32[32,256]{1,0:T(8,128)S(1)} %get-tuple-element.35), channel_id=1, source_target_pairs={{0,2},{1,3},{2,4},{3,5},{4,6},{5,7},{6,0},{7,1},{8,10},{9,11},{10,... | collective-permute-start | bytes 98312 | tf_op jit(solution)/shard_map/ppermute | solution.py:367
  73.9 1.3 collective-permute-start.3
  75.2 1.1 collective-permute-start.4
  76.6 2.9 %collective-permute-done.4.b2 = f32[32,256]{1,0:T(8,128)S(1)} collective-permute-done((f32[32,256]{1,0:T(8,128)S(1)}, f32[32,256]{1,0:T(8,128)S(1)}, u32[]{:S(2)}, u32[]{:S(2)}) %collective-permute-start.4) | collective-permute-done | bytes 32800 | tf_op jit(solution)/shard_map/ppermute | solution.py:367
  79.6 1.1 line_shift.1
  80.7 1.2 collective-permute-start.8
  81.9 1.5 %collective-permute-start.9 = (f32[32,256]{1,0:T(8,128)S(1)}, f32[32,256]{1,0:T(8,128)S(1)}, u32[]{:S(2)}, u32[]{:S(2)}) collective-permute-start(f32[32,256]{1,0:T(8,128)S(1)} %get-tuple-element.40.b0), channel_id=1, source_target_pairs={{0,24},{1,25},{2,26},{3,27},{4,28},{5,29},{6,30},{7,31},{8,0},{9,1... | collective-permute-start | bytes 98312 | tf_op jit(solution)/shard_map/ppermute | solution.py:379
  84.7 3.0 %collective-permute-done.10.b2 = f32[32,256]{1,0:T(8,128)S(1)} collective-permute-done((f32[32,256]{1,0:T(8,128)S(1)}, f32[32,256]{1,0:T(8,128)S(1)}, u32[]{:S(2)}, u32[]{:S(2)}) %collective-permute-start.10) | collective-permute-done | bytes 32800 | tf_op jit(solution)/shard_map/ppermute | solution.py:379
  87.7 1.3 group_shift.1
  89.0 3.3 %collective-permute-start.14 = (f32[32,256]{1,0:T(8,128)S(1)}, f32[32,256]{1,0:T(8,128)S(1)}, u32[]{:S(2)}, u32[]{:S(2)}) collective-permute-start(f32[32,256]{1,0:T(8,128)S(1)} %get-tuple-element.45), channel_id=1, source_target_pairs={{0,32},{32,64},{64,96},{96,128},{128,160},{160,192},{192,224},{1,3... | collective-permute-start | bytes 98312 | tf_op jit(solution)/shard_map/ppermute | solution.py:291
  92.3 4.6 %collective-permute-start.15 = (f32[32,256]{1,0:T(8,128)S(1)}, f32[32,256]{1,0:T(8,128)S(1)}, u32[]{:S(2)}, u32[]{:S(2)}) collective-permute-start(f32[32,256]{1,0:T(8,128)S(1)} %get-tuple-element.45), channel_id=1, source_target_pairs={{0,64},{32,96},{64,128},{96,160},{128,192},{160,224},{1,65},{33,97... | collective-permute-start | bytes 98312 | tf_op jit(solution)/shard_map/ppermute | solution.py:291
  96.9 1.0 collective-permute-done.15.got2
  98.6 4.6 %collective-permute-start.17 = (f32[32,256]{1,0:T(8,128)S(1)}, f32[32,256]{1,0:T(8,128)S(1)}, u32[]{:S(2)}, u32[]{:S(2)}) collective-permute-start(f32[32,256]{1,0:T(8,128)S(1)} %hop1.1.mine), channel_id=1, source_target_pairs={{0,64},{32,96},{64,128},{96,160},{128,192},{160,224},{1,65},{33,97... | collective-permute-start | bytes 98312 | tf_op jit(solution)/shard_map/ppermute | solution.py:291
  103.2 1.0 collective-permute-done.17.got
  104.9 7.3 %collective-permute-start.19 = (f32[32,256]{1,0:T(8,128)S(1)}, f32[32,256]{1,0:T(8,128)S(1)}, u32[]{:S(2)}, u32[]{:S(2)}) collective-permute-start(f32[32,256]{1,0:T(8,128)S(1)} %hop2.1.mine), channel_id=1, source_target_pairs={{0,128},{32,160},{64,192},{96,224},{1,129},{33,161},{65,193},{97,2... | collective-permute-start | bytes 98312 | tf_op jit(solution)/shard_map/ppermute | solution.py:291
  113.4 1.1 hop4.1
  114.5 1.9 %collective-permute-start.21 = (f32[32,256]{1,0:T(8,128)S(1)}, f32[32,256]{1,0:T(8,128)S(1)}, u32[]{:S(2)}, u32[]{:S(2)}) collective-permute-start(f32[32,256]{1,0:T(8,128)S(1)} %get-tuple-element.50), channel_id=1, source_target_pairs={{0,2},{1,3},{2,4},{3,5},{4,6},{5,7},{6,0},{7,1},{8,10},{9,11},{10,... | collective-permute-start | bytes 98312 | tf_op jit(solution)/shard_map/ppermute | solution.py:418
  116.4 0.9 collective-permute-start.22
  117.3 2.4 %collective-permute-start.23 = (f32[32,256]{1,0:T(8,128)S(1)}, f32[32,256]{1,0:T(8,128)S(1)}, u32[]{:S(2)}, u32[]{:S(2)}) collective-permute-start(f32[32,256]{1,0:T(8,128)S(1)} %get-tuple-element.52), channel_id=1, source_target_pairs={{0,4},{1,5},{2,6},{3,7},{4,0},{5,1},{6,2},{7,3},{8,12},{9,13},{10,... | collective-permute-start | bytes 98312 | tf_op jit(solution)/shard_map/ppermute | solution.py:418
  119.6 1.9 %collective-permute-done.23.e2 = f32[32,256]{1,0:T(8,128)S(1)} collective-permute-done((f32[32,256]{1,0:T(8,128)S(1)}, f32[32,256]{1,0:T(8,128)S(1)}, u32[]{:S(2)}, u32[]{:S(2)}) %collective-permute-start.23) | collective-permute-done | bytes 32800 | tf_op jit(solution)/shard_map/ppermute | solution.py:418
  122.3 11.7 %collective-permute-start.24 = (f32[128,256]{1,0:T(8,128)S(1)}, f32[128,256]{1,0:T(8,128)S(1)}, u32[]{:S(2)}, u32[]{:S(2)}) collective-permute-start(f32[128,256]{1,0:T(8,128)S(1)} %get-tuple-element.55), channel_id=1, source_target_pairs={{0,1},{1,0},{2,3},{3,2},{4,5},{5,4},{6,7},{7,6},{8,9},{9,8},{10,11... | collective-permute-start | bytes 393224 | tf_op jit(solution)/shard_map/ppermute | solution.py:431
  134.0 1.8 %weights.1 = f32[8,256]{1,0:T(8,128)S(1)} custom-call(s32[4]{0:T(128)S(1)} %pad_add_fusion.pos, f32[8,256]{1,0:T(8,128)S(1)} %copy-done.12, f32[8,256,256]{2,1,0:T(8,128)S(1)} %copy-done.1, f32[1,256]{1,0:T(1,128)S(1)} %bitcast.14), custom_call_target="tpu_custom_call" | custom-call | flops 33554432 | bytes 2114576 | tf_op jit(solution)/shard_map/weights/pallas_call | solution.py:38
  135.8 1.7 %finish.1 = (f32[8,256]{1,0:T(8,128)}, f32[256,256]{1,0:T(8,128)}) custom-call(s32[4]{0:T(128)S(1)} %pad_add_fusion.pos, f32[128,256]{1,0:T(8,128)S(1)} %get-tuple-element.54.kept, f32[128,256]{1,0:T(8,128)S(1)} %collective-permute-done.24.got, f32[256,256]{1,0:T(8,128)S(1)} %compose.1.mine.whole, f32[256,256]{1,0:T(8,128)S(1)} %get-tuple-element.56.shifted, ...), custom_call_target="tpu_custom_call" | custom-call | flops 100663296 | bytes 1073168 | tf_op jit(solution)/shard_map/finish/pallas_call | solution.py:38
  (65 shorter events, 7.8 us)
Async XLA Ops:
  0.6 8.2 %copy-start.15 = (s32[1,32,16]{1,2,0:T(8,128)S(1)}, s32[1,32,16]{1,2,0:T(8,128)}, u32[]{:S(2)}) copy-start(s32[1,32,16]{1,2,0:T(8,128)} %param.12) | copy-start | bytes 6148
  0.6 8.2 %copy-start.16 = (s32[1,32,16]{1,2,0:T(8,128)S(1)}, s32[1,32,16]{1,2,0:T(8,128)}, u32[]{:S(2)}) copy-start(s32[1,32,16]{1,2,0:T(8,128)} %param.13) | copy-start | bytes 6148
  0.7 8.2 %copy-start.17 = (s32[1,32]{1,0:T(1,128)S(1)}, s32[1,32]{1,0:T(1,128)}, u32[]{:S(2)}) copy-start(s32[1,32]{1,0:T(1,128)} %param.14) | copy-start | bytes 388
  0.8 1.6 %copy-start = (f32[8,256,256]{2,1,0:T(8,128)S(1)}, f32[8,256,256]{2,1,0:T(8,128)}, u32[]{:S(2)}) copy-start(f32[8,256,256]{2,1,0:T(8,128)} %coupling.5) | copy-start | bytes 6291460
  2.4 0.7 copy-start.11
  3.1 6.1 %copy-start.14 = (f32[1,32,16,256]{3,2,1,0:T(8,128)S(1)}, f32[1,32,16,256]{3,2,1,0:T(8,128)}, u32[]{:S(2)}) copy-start(f32[1,32,16,256]{3,2,1,0:T(8,128)} %param.15) | copy-start | bytes 1572868
  5.5 4.5 %collective-permute-start.1 = (f32[256,256]{1,0:T(8,128)S(1)}, f32[256,256]{1,0:T(8,128)S(1)}, u32[]{:S(2)}, u32[]{:S(2)}) collective-permute-start(f32[256,256]{1,0:T(8,128)S(1)} %compose.1.mine.whole), channel_id=1, source_target_pairs={{0,1},{1,0},{2,3},{3,2},{4,5},{5,4},{6,7},{7,6},{8,9},{9,8},{10,11... | collective-permute-start | bytes 786440 | tf_op jit(solution)/shard_map/ppermute | solution.py:310
  10.9 10.5 %collective-permute-start.5 = (f32[256,256]{1,0:T(8,128)S(1)}, f32[256,256]{1,0:T(8,128)S(1)}, u32[]{:S(2)}, u32[]{:S(2)}) collective-permute-start(f32[256,256]{1,0:T(8,128)S(1)} %get-tuple-element.38.a0), channel_id=1, source_target_pairs={{0,2},{1,3},{2,4},{3,5},{4,6},{5,7},{6,0},{7,1},{8,10},{9,11},{10,... | collective-permute-start | bytes 786440 | tf_op jit(solution)/shard_map/ppermute | solution.py:312
  11.0 10.4 %collective-permute-start.6 = (f32[256,256]{1,0:T(8,128)S(1)}, f32[256,256]{1,0:T(8,128)}, u32[]{:S(2)}, u32[]{:S(2)}) collective-permute-start(f32[256,256]{1,0:T(8,128)S(1)} %get-tuple-element.38.a0), channel_id=1, source_target_pairs={{0,6},{1,7},{2,0},{3,1},{4,2},{5,3},{6,4},{7,5},{8,14},{9,15},{10,... | collective-permute-start | bytes 786440 | tf_op jit(solution)/shard_map/ppermute | solution.py:312
  13.6 11.3 %collective-permute-start.7 = (f32[256,256]{1,0:T(8,128)S(1)}, f32[256,256]{1,0:T(8,128)}, u32[]{:S(2)}, u32[]{:S(2)}) collective-permute-start(f32[256,256]{1,0:T(8,128)S(1)} %get-tuple-element.38.a0), channel_id=1, source_target_pairs={{0,4},{1,5},{2,6},{3,7},{4,0},{5,1},{6,2},{7,3},{8,12},{9,13},{10,... | collective-permute-start | bytes 786440 | tf_op jit(solution)/shard_map/ppermute | solution.py:312
  14.5 38.6 %copy-start.1 = (f32[8,256,256]{2,1,0:T(8,128)S(1)}, f32[8,256,256]{2,1,0:T(8,128)}, u32[]{:S(2)}) copy-start(f32[8,256,256]{2,1,0:T(8,128)} %coupling.5) | copy-start | bytes 6291460
  14.5 38.7 %copy-start.12 = (f32[8,256]{1,0:T(8,128)S(1)}, f32[8,256]{1,0:T(8,128)}, u32[]{:S(2)}) copy-start(f32[8,256]{1,0:T(8,128)} %retain.5) | copy-start | bytes 24580
  14.5 38.7 %copy-start.13 = (f32[256]{0:T(256)S(1)}, f32[256]{0:T(256)}, u32[]{:S(2)}) copy-start(f32[256]{0:T(256)} %param.11) | copy-start | bytes 3076
  14.5 38.6 %all-to-all-start = ((f32[32,8,640]{2,1,0:T(8,128)}), f32[32,8,640]{2,1,0:T(8,128)}, u32[]{:S(2)}, u32[]{:S(2)}) async-start(f32[32,8,640]{2,1,0:T(8,128)} %pad_maximum_fusion), calls=%async_computation | async-start | bytes 1310720 | tf_op jit(solution)/shard_map/all_to_all | solution.py:305
  26.9 1.0 copy-start.6
  27.9 14.6 %copy-start.8 = (f32[3,256,256]{2,1,0:T(8,128)}, f32[3,256,256]{2,1,0:T(8,128)S(1)}, u32[]{:S(2)}) copy-start(f32[3,256,256]{2,1,0:T(8,128)S(1)} %get-tuple-element.42.prefix) | copy-start | bytes 2359300
  27.9 7.0 %collective-permute-start.11 = (f32[256,256]{1,0:T(8,128)S(1)}, f32[256,256]{1,0:T(8,128)S(1)}, u32[]{:S(2)}, u32[]{:S(2)}) collective-permute-start(f32[256,256]{1,0:T(8,128)S(1)} %get-tuple-element.41.a0), channel_id=1, source_target_pairs={{0,8},{1,9},{2,10},{3,11},{4,12},{5,13},{6,14},{7,15},{8,16},{9,17... | collective-permute-start | bytes 786440 | tf_op jit(solution)/shard_map/ppermute | solution.py:322
  29.1 7.6 %collective-permute-start.12 = (f32[256,256]{1,0:T(8,128)S(1)}, f32[256,256]{1,0:T(8,128)S(1)}, u32[]{:S(2)}, u32[]{:S(2)}) collective-permute-start(f32[256,256]{1,0:T(8,128)S(1)} %get-tuple-element.41.a0), channel_id=1, source_target_pairs={{0,24},{1,25},{2,26},{3,27},{4,28},{5,29},{6,30},{7,31},{8,0},{9,1... | collective-permute-start | bytes 786440 | tf_op jit(solution)/shard_map/ppermute | solution.py:322
  30.6 9.6 %collective-permute-start.13 = (f32[256,256]{1,0:T(8,128)S(1)}, f32[256,256]{1,0:T(8,128)S(1)}, u32[]{:S(2)}, u32[]{:S(2)}) collective-permute-start(f32[256,256]{1,0:T(8,128)S(1)} %get-tuple-element.41.a0), channel_id=1, source_target_pairs={{0,16},{1,17},{2,18},{3,19},{4,20},{5,21},{6,22},{7,23},{8,24},{9,... | collective-permute-start | bytes 786440 | tf_op jit(solution)/shard_map/ppermute | solution.py:322
  42.5 1.0 copy-start.2
  43.5 1.0 copy-start.4
  44.5 20.7 %collective-permute-start.16 = (f32[256,256]{1,0:T(8,128)}, f32[256,256]{1,0:T(8,128)S(1)}, u32[]{:S(2)}, u32[]{:S(2)}) collective-permute-start(f32[256,256]{1,0:T(8,128)} %get-tuple-element.46), channel_id=1, source_target_pairs={{0,32},{32,64},{64,96},{96,128},{128,160},{160,192},{192,224},{1,3... | collective-permute-start | bytes 786440 | tf_op jit(solution)/shard_map/ppermute | solution.py:291
  48.0 17.1 %collective-permute-start.18 = (f32[256,256]{1,0:T(8,128)}, f32[256,256]{1,0:T(8,128)S(1)}, u32[]{:S(2)}, u32[]{:S(2)}) collective-permute-start(f32[256,256]{1,0:T(8,128)} %get-tuple-element.46), channel_id=1, source_target_pairs={{0,64},{32,96},{64,128},{96,160},{128,192},{160,224},{1,65},{33,97... | collective-permute-start | bytes 786440 | tf_op jit(solution)/shard_map/ppermute | solution.py:291
  53.2 26.4 %copy-start.7 = (f32[4,256,256]{2,1,0:T(8,128)S(1)}, f32[4,256,256]{2,1,0:T(8,128)}, u32[]{:S(2)}) copy-start(f32[4,256,256]{2,1,0:T(8,128)} %copy-done.6) | copy-start | bytes 3145732
  60.4 27.3 %copy-start.5 = (f32[4,256,256]{2,1,0:T(8,128)S(1)}, f32[4,256,256]{2,1,0:T(8,128)}, u32[]{:S(2)}) copy-start(f32[4,256,256]{2,1,0:T(8,128)} %copy-done.4) | copy-start | bytes 3145732
  60.4 27.3 %copy-start.9 = (f32[3,256,256]{2,1,0:T(8,128)S(1)}, f32[3,256,256]{2,1,0:T(8,128)}, u32[]{:S(2)}) copy-start(f32[3,256,256]{2,1,0:T(8,128)} %copy-done.8) | copy-start | bytes 2359300
  60.4 10.9 %collective-permute-start = (f32[128,256]{1,0:T(8,128)S(1)}, f32[128,256]{1,0:T(8,128)S(1)}, u32[]{:S(2)}, u32[]{:S(2)}) collective-permute-start(f32[128,256]{1,0:T(8,128)S(1)} %get-tuple-element.32), channel_id=1, source_target_pairs={{0,1},{1,0},{2,3},{3,2},{4,5},{5,4},{6,7},{7,6},{8,9},{9,8},{10,11... | collective-permute-start | bytes 393224 | tf_op jit(solution)/shard_map/ppermute | solution.py:354
  66.0 31.9 %copy-start.10 = (f32[256,256]{1,0:T(8,128)S(1)}, f32[256,256]{1,0:T(8,128)}, u32[]{:S(2)}) copy-start(f32[256,256]{1,0:T(8,128)} %initial.1) | copy-start | bytes 786436
  66.0 46.2 %collective-permute-start.20 = (f32[256,256]{1,0:T(8,128)S(1)}, f32[256,256]{1,0:T(8,128)S(1)}, u32[]{:S(2)}, u32[]{:S(2)}) collective-permute-start(f32[256,256]{1,0:T(8,128)S(1)} %two_groups.1.before.right), channel_id=1, source_target_pairs={{0,64},{32,96},{64,128},{96,160},{128,192},{160,224},{1,65},{33,97... | collective-permute-start | bytes 786440 | tf_op jit(solution)/shard_map/ppermute | solution.py:291
  72.1 4.3 %collective-permute-start.2 = (f32[32,256]{1,0:T(8,128)S(1)}, f32[32,256]{1,0:T(8,128)S(1)}, u32[]{:S(2)}, u32[]{:S(2)}) collective-permute-start(f32[32,256]{1,0:T(8,128)S(1)} %get-tuple-element.35), channel_id=1, source_target_pairs={{0,2},{1,3},{2,4},{3,5},{4,6},{5,7},{6,0},{7,1},{8,10},{9,11},{10,... | collective-permute-start | bytes 98312 | tf_op jit(solution)/shard_map/ppermute | solution.py:367
  73.9 2.8 %collective-permute-start.3 = (f32[32,256]{1,0:T(8,128)S(1)}, f32[32,256]{1,0:T(8,128)S(1)}, u32[]{:S(2)}, u32[]{:S(2)}) collective-permute-start(f32[32,256]{1,0:T(8,128)S(1)} %get-tuple-element.36), channel_id=1, source_target_pairs={{0,6},{1,7},{2,0},{3,1},{4,2},{5,3},{6,4},{7,5},{8,14},{9,15},{10,... | collective-permute-start | bytes 98312 | tf_op jit(solution)/shard_map/ppermute | solution.py:367
  75.2 4.4 %collective-permute-start.4 = (f32[32,256]{1,0:T(8,128)S(1)}, f32[32,256]{1,0:T(8,128)S(1)}, u32[]{:S(2)}, u32[]{:S(2)}) collective-permute-start(f32[32,256]{1,0:T(8,128)S(1)} %get-tuple-element.37), channel_id=1, source_target_pairs={{0,4},{1,5},{2,6},{3,7},{4,0},{5,1},{6,2},{7,3},{8,12},{9,13},{10,... | collective-permute-start | bytes 98312 | tf_op jit(solution)/shard_map/ppermute | solution.py:367
  80.6 32.7 %copy-start.3 = (f32[4,256,256]{2,1,0:T(8,128)S(1)}, f32[4,256,256]{2,1,0:T(8,128)}, u32[]{:S(2)}) copy-start(f32[4,256,256]{2,1,0:T(8,128)} %copy-done.2) | copy-start | bytes 3145732
  80.7 4.1 %collective-permute-start.8 = (f32[32,256]{1,0:T(8,128)S(1)}, f32[32,256]{1,0:T(8,128)S(1)}, u32[]{:S(2)}, u32[]{:S(2)}) collective-permute-start(f32[32,256]{1,0:T(8,128)S(1)} %get-tuple-element.40.b0), channel_id=1, source_target_pairs={{0,8},{1,9},{2,10},{3,11},{4,12},{5,13},{6,14},{7,15},{8,16},{9,17... | collective-permute-start | bytes 98312 | tf_op jit(solution)/shard_map/ppermute | solution.py:379
  81.9 2.8 %collective-permute-start.9 = (f32[32,256]{1,0:T(8,128)S(1)}, f32[32,256]{1,0:T(8,128)S(1)}, u32[]{:S(2)}, u32[]{:S(2)}) collective-permute-start(f32[32,256]{1,0:T(8,128)S(1)} %get-tuple-element.40.b0), channel_id=1, source_target_pairs={{0,24},{1,25},{2,26},{3,27},{4,28},{5,29},{6,30},{7,31},{8,0},{9,1... | collective-permute-start | bytes 98312 | tf_op jit(solution)/shard_map/ppermute | solution.py:379
  83.4 4.3 %collective-permute-start.10 = (f32[32,256]{1,0:T(8,128)S(1)}, f32[32,256]{1,0:T(8,128)S(1)}, u32[]{:S(2)}, u32[]{:S(2)}) collective-permute-start(f32[32,256]{1,0:T(8,128)S(1)} %get-tuple-element.40.b0), channel_id=1, source_target_pairs={{0,16},{1,17},{2,18},{3,19},{4,20},{5,21},{6,22},{7,23},{8,24},{9,... | collective-permute-start | bytes 98312 | tf_op jit(solution)/shard_map/ppermute | solution.py:379
  89.0 7.9 %collective-permute-start.14 = (f32[32,256]{1,0:T(8,128)S(1)}, f32[32,256]{1,0:T(8,128)S(1)}, u32[]{:S(2)}, u32[]{:S(2)}) collective-permute-start(f32[32,256]{1,0:T(8,128)S(1)} %get-tuple-element.45), channel_id=1, source_target_pairs={{0,32},{32,64},{64,96},{96,128},{128,160},{160,192},{192,224},{1,3... | collective-permute-start | bytes 98312 | tf_op jit(solution)/shard_map/ppermute | solution.py:291
  92.3 5.6 %collective-permute-start.15 = (f32[32,256]{1,0:T(8,128)S(1)}, f32[32,256]{1,0:T(8,128)S(1)}, u32[]{:S(2)}, u32[]{:S(2)}) collective-permute-start(f32[32,256]{1,0:T(8,128)S(1)} %get-tuple-element.45), channel_id=1, source_target_pairs={{0,64},{32,96},{64,128},{96,160},{128,192},{160,224},{1,65},{33,97... | collective-permute-start | bytes 98312 | tf_op jit(solution)/shard_map/ppermute | solution.py:291
  98.6 5.6 %collective-permute-start.17 = (f32[32,256]{1,0:T(8,128)S(1)}, f32[32,256]{1,0:T(8,128)S(1)}, u32[]{:S(2)}, u32[]{:S(2)}) collective-permute-start(f32[32,256]{1,0:T(8,128)S(1)} %hop1.1.mine), channel_id=1, source_target_pairs={{0,64},{32,96},{64,128},{96,160},{128,192},{160,224},{1,65},{33,97... | collective-permute-start | bytes 98312 | tf_op jit(solution)/shard_map/ppermute | solution.py:291
  104.9 8.4 %collective-permute-start.19 = (f32[32,256]{1,0:T(8,128)S(1)}, f32[32,256]{1,0:T(8,128)S(1)}, u32[]{:S(2)}, u32[]{:S(2)}) collective-permute-start(f32[32,256]{1,0:T(8,128)S(1)} %hop2.1.mine), channel_id=1, source_target_pairs={{0,128},{32,160},{64,192},{96,224},{1,129},{33,161},{65,193},{97,2... | collective-permute-start | bytes 98312 | tf_op jit(solution)/shard_map/ppermute | solution.py:291
  114.5 5.1 %collective-permute-start.21 = (f32[32,256]{1,0:T(8,128)S(1)}, f32[32,256]{1,0:T(8,128)S(1)}, u32[]{:S(2)}, u32[]{:S(2)}) collective-permute-start(f32[32,256]{1,0:T(8,128)S(1)} %get-tuple-element.50), channel_id=1, source_target_pairs={{0,2},{1,3},{2,4},{3,5},{4,6},{5,7},{6,0},{7,1},{8,10},{9,11},{10,... | collective-permute-start | bytes 98312 | tf_op jit(solution)/shard_map/ppermute | solution.py:418
  116.4 3.3 %collective-permute-start.22 = (f32[32,256]{1,0:T(8,128)S(1)}, f32[32,256]{1,0:T(8,128)S(1)}, u32[]{:S(2)}, u32[]{:S(2)}) collective-permute-start(f32[32,256]{1,0:T(8,128)S(1)} %get-tuple-element.51), channel_id=1, source_target_pairs={{0,6},{1,7},{2,0},{3,1},{4,2},{5,3},{6,4},{7,5},{8,14},{9,15},{10,... | collective-permute-start | bytes 98312 | tf_op jit(solution)/shard_map/ppermute | solution.py:418
  117.3 4.3 %collective-permute-start.23 = (f32[32,256]{1,0:T(8,128)S(1)}, f32[32,256]{1,0:T(8,128)S(1)}, u32[]{:S(2)}, u32[]{:S(2)}) collective-permute-start(f32[32,256]{1,0:T(8,128)S(1)} %get-tuple-element.52), channel_id=1, source_target_pairs={{0,4},{1,5},{2,6},{3,7},{4,0},{5,1},{6,2},{7,3},{8,12},{9,13},{10,... | collective-permute-start | bytes 98312 | tf_op jit(solution)/shard_map/ppermute | solution.py:418
  122.3 13.5 %collective-permute-start.24 = (f32[128,256]{1,0:T(8,128)S(1)}, f32[128,256]{1,0:T(8,128)S(1)}, u32[]{:S(2)}, u32[]{:S(2)}) collective-permute-start(f32[128,256]{1,0:T(8,128)S(1)} %get-tuple-element.55), channel_id=1, source_target_pairs={{0,1},{1,0},{2,3},{3,2},{4,5},{5,4},{6,7},{7,6},{8,9},{9,8},{10,11... | collective-permute-start | bytes 393224 | tf_op jit(solution)/shard_map/ppermute | solution.py:431

commit v2 on v1

--- a/solution.py
+++ b/solution.py
@@ -30,40 +30,70 @@
     return dot(ah, bh, transposed) + (dot(ah, bl, transposed) + dot(al, bh, transposed))
 
 
-def call(kernel, name, outs, *args, scratch=(), flops=0):
-    shapes = [jax.ShapeDtypeStruct(s, F32) for s in outs]
+def call(kernel, name, outs, *args, scratch=(), flops=0, after=()):
+    shapes = [s if hasattr(s, "dtype") else jax.ShapeDtypeStruct(s, F32) for s in outs]
     smem = pl.BlockSpec(memory_space=pltpu.SMEM)
     vmem = pl.BlockSpec(memory_space=pltpu.VMEM)
     moved = sum(4 * a.size for a in args) + sum(4 * s.size for s in shapes)
+    n_args, n_after = len(args), len(after)
+
+    def run(*refs):
+        kernel(*refs[:n_args], *refs[n_args + n_after :])
+
     return pl.pallas_call(
-        kernel,
+        run,
         out_shape=shapes,
-        in_specs=[smem] + [vmem] * (len(args) - 1),
+        in_specs=[smem] + [vmem] * (n_args - 1) + [pl.BlockSpec(memory_space=pl.ANY)] * n_after,
         out_specs=[vmem] * len(shapes),
         scratch_shapes=list(scratch),
         name=name,
         cost_estimate=pl.CostEstimate(flops=flops, bytes_accessed=moved, transcendentals=0),
-        compiler_params=pltpu.CompilerParams(vmem_limit_bytes=32 * 1024 * 1024),
-    )(*args)
-
-
-def compose_kernel(pos, retain, coupling, whole):
+        compiler_params=pltpu.CompilerParams(vmem_limit_bytes=16 * 1024 * 1024),
+    )(*args, *after)
+
+
+def pack_kernel(loads, samples_of, steps_of, counts, *refs, samples):
+    out, samples_buf, steps_buf, counts_buf, tags, sems = refs[-6:]
+    owners, cap, modes = loads.shape
+    half = cap // 2
+    copies = [
+        pltpu.make_async_copy(samples_of, samples_buf, sems.at[0]),
+        pltpu.make_async_copy(steps_of, steps_buf, sems.at[1]),
+        pltpu.make_async_copy(counts, counts_buf, sems.at[2]),
+        pltpu.make_async_copy(loads.at[:, :half, :], out.at[:, :, 0:modes], sems.at[3]),
+        pltpu.make_async_copy(loads.at[:, half:, :], out.at[:, :, modes : 2 * modes], sems.at[4]),
+    ]
+    for copy in copies:
+        copy.start()
+    for copy in copies[:3]:
+        copy.wait()
+    slot = lax.broadcasted_iota(jnp.int32, (cap, owners), 0)
+    codes = jnp.where(slot < counts_buf[...], steps_buf[...] * samples + samples_buf[...], -1)
+    codes = codes.astype(F32)
+    lane = lax.broadcasted_iota(jnp.int32, (half, 128), 1)
+    for j in range(owners):
+        tags[j] = jnp.where(lane == 0, codes[:half, j : j + 1], codes[half:, j : j + 1])
+    last = pltpu.make_async_copy(tags, out.at[:, :, 2 * modes : 2 * modes + 128], sems.at[5])
+    last.start()
+    for copy in copies[3:]:
+        copy.wait()
+    last.wait()
+
+
+def compose_kernel(pos, retain, coupling, probe, whole, seen):
     steps, modes = retain.shape
     rows = lax.broadcasted_iota(jnp.int32, (modes, modes), 0)
     cols = lax.broadcasted_iota(jnp.int32, (modes, modes), 1)
     total = coupling[0].T + jnp.where(rows == cols, retain[0:1, :], 0.0)
-    for t in range(1, steps):
-        total = total * retain[t : t + 1, :] + mm(split(total), split(coupling[t]), True)
+    step = lax.broadcasted_iota(jnp.int32, (steps, modes), 0)
+    state = jnp.zeros((steps, modes), F32)
+    for t in range(steps):
+        u = steps - 1 - t
+        state = jnp.where(step == u, probe[...], state)
+        state = state * retain[u : u + 1, :] + mm(split(state), split(coupling[u]))
+        if t > 0:
+            total = total * retain[t : t + 1, :] + mm(split(total), split(coupling[t]), True)
     whole[...] = total
-
-
-def weights_kernel(pos, retain, coupling, probe, seen):
-    steps, modes = retain.shape
-    rows = lax.broadcasted_iota(jnp.int32, (steps, modes), 0)
-    state = jnp.zeros((steps, modes), F32)
-    for t in range(steps - 1, -1, -1):
-        state = jnp.where(rows == t, probe[...], state)
-        state = state * retain[t : t + 1, :] + mm(split(state), split(coupling[t]))
     seen[...] = state
 
 
@@ -83,9 +113,8 @@
     codes = arrived[:, :, 2 * modes : 2 * modes + 128].reshape(n, 128).T
     codes = jnp.concatenate([codes[0:1, :], codes[1:2, :]], axis=1).astype(jnp.int32)
     place = lax.broadcasted_iota(jnp.int32, (samples, 2 * n), 0)
-    ph, pw = split(jnp.broadcast_to(probe[...], (8, modes)))
-    rows = lax.broadcasted_iota(jnp.int32, (8, samples), 0)
-    shown = jnp.zeros((8, samples), F32)
+    lane = lax.broadcasted_iota(jnp.int32, (samples, 128), 1)
+    shown = jnp.zeros((samples, 128), F32)
     field = None
     for t in range(steps):
         hit = jnp.where(place + t * samples == codes, 1.0, 0.0).astype(BF16)
@@ -94,9 +123,9 @@
             kick = kick + field * retain[t : t + 1, :] + mm(parts, split(coupling[t]), True)
         field = kick
         parts = split(field)
-        shown = jnp.where(rows == t, mm((ph, pw), parts, True), shown)
+        shown = jnp.where(lane == t, jnp.sum(field * probe[...], axis=1, keepdims=True), shown)
     shifted[...] = field
-    seen[...] = shown
+    seen[...] = shown.T[:steps]
     c = pos[0]
     h = samples // 2
 
@@ -142,10 +171,10 @@
     line[...] = total
 
 
-def group_map_kernel(pos, a0, a1, a3, a2, prefix, ordered, through, group, before):
+def group_map_kernel(pos, a0, a1, a3, a2, prefix, ordered, through, high, low, before):
     x = pos[2]
     order(x, NX, ordered, (a0, a1, a3, a2))
-    modes = group.shape[0]
+    modes = high.shape[0]
     rows = lax.broadcasted_iota(jnp.int32, (modes, modes), 0)
     cols = lax.broadcasted_iota(jnp.int32, (modes, modes), 1)
     before[0] = jnp.where(rows == cols, 1.0, 0.0)
@@ -153,16 +182,12 @@
     for k in range(1, NX):
         before[k] = total
         total = mm(split(total), split(ordered[k]))
-    group[...] = total
+    high[...], low[...] = split(total)
     own = before[x]
     through[0] = own
     own = split(own)
     for k in range(1, NY):
         through[k] = mm(own, split(prefix[k - 1]))
-
-
-def product_kernel(pos, left, right, out):
-    out[...] = mm(split(left[...]), split(right[...]))
 
 
 def pair_shift_kernel(pos, kept, got, both, first, s0, s1, s3, s2, chip):
@@ -205,24 +230,28 @@
         through[k] = mm(prior, split(prefix[k - 1])) + before[k - 1]
 
 
-def first_hop_kernel(pos, initial, got1, got2, before, out):
-    c, y, g = pos[0], pos[1], pos[3]
-    r = out.shape[0]
-    start = pl.multiple_of(c * (NY * r) + y * r, r)
-    released = initial[pl.ds(start, r), :]
-    near = jnp.where(g == 0, released, got1[...])
-    far = jnp.where(g == 1, released, got2[...])
-    far = jnp.where(g == 0, 0.0, far)
-    out[...] = near + mm(split(far), split(before[...]))
-
-
-def hop_kernel(pos, mine, got, before, out):
-    out[...] = mine[...] + mm(split(got[...]), split(before[...]))
-
-
-def last_hop_kernel(pos, mine, got, before, maps, shifts, s0, s1, s3, s2, chips):
+def released_rows(pos, initial, part):
+    start = pl.multiple_of(pos[0] * (NY * part) + pos[1] * part, part)
+    return initial[pl.ds(start, part), :]
+
+
+def first_hop_kernel(pos, initial, high, low, shift, out):
+    state = released_rows(pos, initial, out.shape[0])
+    out[...] = mm(split(state), (high[...], low[...])) + shift[...]
+
+
+def hop_kernel(pos, got, high, low, shift, out):
+    out[...] = mm(split(got[...]), (high[...], low[...])) + shift[...]
+
+
+def last_hop_kernel(pos, initial, *refs):
+    gots, (maps, shifts, s0, s1, s3, s2, chips) = refs[:-7], refs[-7:]
     y = pos[1]
-    group = split(mine[...] + mm(split(got[...]), split(before[...])))
+    g = pos[3]
+    state = released_rows(pos, initial, s0.shape[0])
+    for k, got in enumerate(gots):
+        state = jnp.where(g == k + 1, got[...], state)
+    group = split(state)
     for k in range(NY):
         chips[k] = mm(group, split(maps[k])) + shifts[k]
     for s, out in zip((0,) + SHIFTS, (s0, s1, s3, s2)):
@@ -287,29 +316,39 @@
 
     n_grp = lax.axis_size("grp")
 
-    def later(a, s):
-        return lax.ppermute(a, "grp", [(i, i + s) for i in range(n_grp - s)])
-
-    slot = lax.broadcasted_iota(jnp.int32, rec_sample.shape, 2)
-    codes = jnp.where(slot < rec_count[:, :, None], rec_step * samples + rec_sample, -1)
-    codes = codes[0].astype(F32)
-    lane = lax.broadcasted_iota(jnp.int32, (owners, cap // 2, 128), 2)
-    tags = jnp.where(
-        lane == 0,
-        codes[:, : cap // 2, None],
-        jnp.where(lane == 1, codes[:, cap // 2 :, None], 0.0),
-    )
-    packed = jnp.concatenate(
-        [rec_load[0, :, : cap // 2], rec_load[0, :, cap // 2 :], tags], axis=-1
-    )
-    arrived = lax.all_to_all(packed, "tm", split_axis=0, concat_axis=0)
-
     cube = 2 * modes * modes * modes
     probe_row = probe[None, :]
-    (whole,) = call(compose_kernel, "compose", [mat], pos, retain, coupling, flops=21 * cube)
+    whole, weights = call(
+        compose_kernel,
+        "compose",
+        [mat, (steps, modes)],
+        pos,
+        retain,
+        coupling,
+        probe_row,
+        flops=22 * cube,
+    )
     other = lax.ppermute(whole, "tm", swap)
     both, chip = call(pair_kernel, "pair_map", [(2,) + mat, mat], pos, whole, other, flops=3 * cube)
     got = [lax.ppermute(chip, "tm", along_y(s)) for s in SHIFTS]
+    anywhere = pl.BlockSpec(memory_space=pl.ANY)
+    shape = (owners, cap // 2, 2 * modes + 128)
+    packed = pl.pallas_call(
+        functools.partial(pack_kernel, samples=samples),
+        out_shape=jax.ShapeDtypeStruct(shape, F32),
+        in_specs=[anywhere] * 5,
+        out_specs=anywhere,
+        scratch_shapes=[
+            pltpu.VMEM((cap, owners), jnp.int32),
+            pltpu.VMEM((cap, owners), jnp.int32),
+            pltpu.VMEM((1, owners), jnp.int32),
+            vm(owners, cap // 2, 128),
+            pltpu.SemaphoreType.DMA((6,)),
+        ],
+        name="pack",
+        cost_estimate=pl.CostEstimate(flops=0, bytes_accessed=2**20, transcendentals=0),
+    )(rec_load[0], rec_sample[0].T, rec_step[0].T, rec_count, chip)
+    arrived = lax.all_to_all(packed, "tm", split_axis=0, concat_axis=0)
     y_maps, y_before, line = call(
         line_map_kernel,
         "line_map",
@@ -318,38 +357,32 @@
         chip,
         *got,
         flops=9 * cube,
+        after=(packed,),
     )
     got = [lax.ppermute(line, "tm", along_x(s)) for s in SHIFTS]
-    x_maps, through, group = call(
+    shifted, kept, sent, driven = call(
+        drive_kernel,
+        "drive",
+        [mat, (half, modes), (half, modes), (steps, samples)],
+        pos,
+        arrived,
+        retain,
+        coupling,
+        probe_row,
+        flops=60 * cube,
+        after=(line,),
+    )
+    half_mat = jax.ShapeDtypeStruct(mat, BF16)
+    x_maps, through, high, low = call(
         group_map_kernel,
         "group_map",
-        [(NX,) + mat, (NY,) + mat, mat],
+        [(NX,) + mat, (NY,) + mat, half_mat, half_mat],
         pos,
         line,
         *got,
         y_before,
         scratch=[vm(NX, *mat)],
         flops=18 * cube,
-    )
-    g1 = later(group, 1)
-    g2 = later(group, 2)
-    (h1,) = call(product_kernel, "two_groups", [mat], pos, g2, g1, flops=3 * cube)
-    h1_far = later(h1, 2)
-    (h2,) = call(product_kernel, "four_groups", [mat], pos, h1_far, h1, flops=3 * cube)
-
-    (weights,) = call(
-        weights_kernel, "weights", [(steps, modes)], pos, retain, coupling, probe_row, flops=cube
-    )
-    shifted, kept, sent, driven = call(
-        drive_kernel,
-        "drive",
-        [mat, (half, modes), (half, modes), (steps, samples)],
-        pos,
-        arrived,
-        retain,
-        coupling,
-        probe_row,
-        flops=60 * cube,
     )
     back = lax.ppermute(sent, "tm", swap)
     small = (part, modes)
@@ -391,25 +424,19 @@
         flops=2 * cube,
     )
     (e,) = call(
-        first_hop_kernel,
-        "hop1",
-        [small],
-        pos,
-        initial_state,
-        later(b_group, 1),
-        later(b_group, 2),
-        g1,
-        flops=cube,
-    )
-    (e,) = call(hop_kernel, "hop2", [small], pos, e, later(e, 2), h1, flops=cube)
+        first_hop_kernel, "hop0", [small], pos, initial_state, high, low, b_group, flops=cube
+    )
+    carried = [lax.ppermute(e, "grp", [(0, 1)])]
+    for k in range(1, n_grp - 1):
+        (e,) = call(hop_kernel, "hop", [small], pos, carried[-1], high, low, b_group, flops=cube)
+        carried.append(lax.ppermute(e, "grp", [(k, k + 1)]))
     rows = call(
         last_hop_kernel,
-        "hop4",
+        "chips",
         [small] * 4,
         pos,
-        e,
-        later(e, 4),
-        h2,
+        initial_state,
+        *carried,
         through,
         b_through,
         scratch=[vm(NY, *small)],

time: 138 us -> 141 us (1.022)
  the two profiles are of different devices: /device:TPU:1 before, /device:TPU:225 now
where the time goes in v2:
time: 141 us
  waiting for transfers between devices  48.1 us (34%)
  starting transfers between devices  44.9 us (32%)
  Pallas kernels  39.7 us (28%)
  local copies, waits for them, and re-layouts  7.05 us (5%)
    pallas_call x18, Pallas kernels, call(): pl.pallas_call(run, out_shape=shapes, in_specs=[smem] + [vmem] * (n_args...  22.7 us
    ppermute x3, waiting for transfers between devices, body(): got = [lax.ppermute(chip, 'tm', along_y(s)) for s in SHIFTS]  17.3 us
    pallas_call x1, Pallas kernels, body(): pl.pallas_call(functools.partial(pack_kernel, samples=samples), out_shape...  17 us
    ppermute x6, waiting for transfers between devices, body(): carried.append(lax.ppermute(e, 'grp', [(k, k + 1)]))  16.4 us
    ppermute x2, starting transfers between devices, body(): back = lax.ppermute(sent, 'tm', swap)  13.9 us
    ppermute x6, waiting for transfers between devices, body(): got = [lax.ppermute(r, 'tm', along_y(s)) for r, s in zip(rows[1:], SHIFTS)]  9.82 us
    all_to_all x1, starting transfers between devices, body(): arrived = lax.all_to_all(packed, 'tm', split_axis=0, concat_axis=0)  7.47 us
    unnamed x20, local copies, waits for them, and re-layouts  7.05 us
  transfers between devices with their start and end apart: 26, of which 12 were waited for; matrix products, arithmetic and copies ran while one was open for 0% of the time, Pallas kernels for 7%

profile of v2, /device:TPU:225, one launch (start us, length us, event | category | flops | bytes accessed | tf_op | source)
XLA Modules:
  0.0 140.9 jit_solution(9135277494095446772)
XLA Ops:
  0.8 1.6 %copy-done.4 = f32[8,256,256]{2,1,0:T(8,128)S(1)} copy-done((f32[8,256,256]{2,1,0:T(8,128)S(1)}, f32[8,256,256]{2,1,0:T(8,128)}, u32[]{:S(2)}) %copy-start.4) | copy-done | bytes 2097176
  2.3 0.7 copy-done.6
  3.7 2.7 %compose.1 = (f32[256,256]{1,0:T(8,128)S(1)}, f32[8,256]{1,0:T(8,128)S(1)}) custom-call(s32[4]{0:T(128)S(1)} %pad_add_fusion.refs_0_, f32[8,256]{1,0:T(8,128)S(1)} %copy-done.6, f32[8,256,256]{2,1,0:T(8,128)S(1)} %copy-done.4, f32[1,256]{1,0:T(1,128)S(1)} %bitcast.13), custom_call_target="tpu_custom_call" | custom-call | flops 738197504 | bytes 2376720 | tf_op jit(solution)/shard_map/compose/pallas_call | solution.py:43
  6.4 0.8 collective-permute-start
  7.2 1.2 collective-permute-done.refs_2_
  8.3 0.9 pair_map.1
  9.9 17.0 %pack.1.refs_5_ = f32[32,8,640]{2,1,0:T(8,128)} custom-call(f32[32,16,256]{2,1,0:T(8,128)} %bitcast.15, s32[16,32]{1,0:T(8,128)} %bitcast.16, s32[16,32]{1,0:T(8,128)} %bitcast.17, s32[1,32]{1,0:T(1,128)} %counts.1, f32[256,256]{1,0:T(8,128)} %copy-done.1), custom_call_target="tpu_custom_call" | custom-call | bytes 1048576 | tf_op jit(solution)/shard_map/pack/pallas_call | solution.py:336
  26.9 7.5 %all-to-all-start = ((f32[32,8,640]{2,1,0:T(8,128)}), f32[32,8,640]{2,1,0:T(8,128)S(1)}, u32[]{:S(2)}, u32[]{:S(2)}) async-start(f32[32,8,640]{2,1,0:T(8,128)} %pack.1.refs_5_), calls=%async_computation | async-start | bytes 1310720 | tf_op jit(solution)/shard_map/all_to_all | solution.py:351
  34.4 3.0 %collective-permute-start.3 = (f32[256,256]{1,0:T(8,128)S(1)}, f32[256,256]{1,0:T(8,128)S(1)}, u32[]{:S(2)}, u32[]{:S(2)}) collective-permute-start(f32[256,256]{1,0:T(8,128)S(1)} %copy-done.2), channel_id=1, source_target_pairs={{0,4},{1,5},{2,6},{3,7},{4,0},{5,1},{6,2},{7,3},{8,12},{9,13},{10,... | collective-permute-start | bytes 786440 | tf_op jit(solution)/shard_map/ppermute | solution.py:333
  37.4 0.9 collective-permute-start.2
  38.9 12.1 %collective-permute-done.3.refs_4_ = f32[256,256]{1,0:T(8,128)S(1)} collective-permute-done((f32[256,256]{1,0:T(8,128)S(1)}, f32[256,256]{1,0:T(8,128)S(1)}, u32[]{:S(2)}, u32[]{:S(2)}) %collective-permute-start.3) | collective-permute-done | bytes 262176 | tf_op jit(solution)/shard_map/ppermute | solution.py:333
  51.0 4.2 %collective-permute-done.2.refs_3_ = f32[256,256]{1,0:T(8,128)S(1)} collective-permute-done((f32[256,256]{1,0:T(8,128)S(1)}, f32[256,256]{1,0:T(8,128)S(1)}, u32[]{:S(2)}, u32[]{:S(2)}) %collective-permute-start.2) | collective-permute-done | bytes 262176 | tf_op jit(solution)/shard_map/ppermute | solution.py:333
  55.2 1.0 collective-permute-done.1.refs_2_
  56.2 1.1 copy-done
  57.3 2.2 %line_map.1 = (f32[4,256,256]{2,1,0:T(8,128)S(1)}, f32[3,256,256]{2,1,0:T(8,128)S(1)}, f32[256,256]{1,0:T(8,128)}) custom-call(s32[4]{0:T(128)S(1)} %pad_add_fusion.refs_0_, f32[256,256]{1,0:T(8,128)S(1)} %copy-done.2, f32[256,256]{1,0:T(8,128)S(1)} %collective-permute-done.1.refs_2_, f32[256,256]{1,0:T(8,128)S(1)} %collective-permute-done.2.refs_3_, ...), custom_call_target="tpu_custom_call" | custom-call | flops 301989888 | bytes 3145744 | tf_op jit(solution)/shard_map/line_map/pallas_call | solution.py:43
  59.5 3.2 %collective-permute-start.6 = (f32[256,256]{1,0:T(8,128)}, f32[256,256]{1,0:T(8,128)}, u32[]{:S(2)}, u32[]{:S(2)}) collective-permute-start(f32[256,256]{1,0:T(8,128)} %get-tuple-element.36.refs_1_.refs_5_), channel_id=1, source_target_pairs={{0,16},{1,17},{2,18},{3,19},{4,20},{5,21},{6,22},{7,23},{8,24},{9,... | collective-permute-start | bytes 786440 | tf_op jit(solution)/shard_map/ppermute | solution.py:362
  62.6 0.8 collective-permute-start.5
  64.1 1.6 %copy-done.5 = f32[8,256,256]{2,1,0:T(8,128)S(1)} copy-done((f32[8,256,256]{2,1,0:T(8,128)S(1)}, f32[8,256,256]{2,1,0:T(8,128)}, u32[]{:S(2)}) %copy-start.5) | copy-done | bytes 2097176
  65.7 0.7 copy-done.7
  66.4 3.2 %drive.1 = (f32[256,256]{1,0:T(8,128)S(1)}, f32[128,256]{1,0:T(8,128)S(1)}, f32[128,256]{1,0:T(8,128)S(1)}, f32[8,256]{1,0:T(8,128)S(1)}) custom-call(s32[4]{0:T(128)S(1)} %pad_add_fusion.refs_0_, f32[32,8,640]{2,1,0:T(8,128)S(1)} %all-to-all-done.refs_1_, f32[8,256]{1,0:T(8,128)S(1)} %copy-done.7, f32[8,256,256]{2,1,0:T(8,128)S(1)} %copy-done.5, ...), custom_call_target="tpu_custom_call" | custom-call | flops 2013265920 | bytes 3294224 | tf_op jit(solution)/shard_map/drive/pallas_call | solution.py:43
  69.6 1.3 collective-permute-start.7
  70.9 1.0 collective-permute-done.7.refs_2_
  71.9 0.8 pair_shift.1
  72.8 2.7 %collective-permute-start.9 = (f32[32,256]{1,0:T(8,128)S(1)}, f32[32,256]{1,0:T(8,128)S(1)}, u32[]{:S(2)}, u32[]{:S(2)}) collective-permute-start(f32[32,256]{1,0:T(8,128)S(1)} %get-tuple-element.45), channel_id=1, source_target_pairs={{0,6},{1,7},{2,0},{3,1},{4,2},{5,3},{6,4},{7,5},{8,14},{9,15},{10,... | collective-permute-start | bytes 98312 | tf_op jit(solution)/shard_map/ppermute | solution.py:400
  75.4 1.3 collective-permute-done.8.refs_2_
  76.7 4.3 %collective-permute-done.10.refs_4_ = f32[32,256]{1,0:T(8,128)S(1)} collective-permute-done((f32[32,256]{1,0:T(8,128)S(1)}, f32[32,256]{1,0:T(8,128)S(1)}, u32[]{:S(2)}, u32[]{:S(2)}) %collective-permute-start.10) | collective-permute-done | bytes 32800 | tf_op jit(solution)/shard_map/ppermute | solution.py:400
  81.0 1.1 line_shift.1
  82.5 2.3 %collective-permute-start.12 = (f32[32,256]{1,0:T(8,128)S(1)}, f32[32,256]{1,0:T(8,128)S(1)}, u32[]{:S(2)}, u32[]{:S(2)}) collective-permute-start(f32[32,256]{1,0:T(8,128)S(1)} %get-tuple-element.48.refs_1_), channel_id=1, source_target_pairs={{0,24},{1,25},{2,26},{3,27},{4,28},{5,29},{6,30},{7,31},{8,0},{9,1... | collective-permute-start | bytes 98312 | tf_op jit(solution)/shard_map/ppermute | solution.py:412
  84.9 2.5 %group_map.1 = (f32[4,256,256]{2,1,0:T(8,128)S(1)}, f32[4,256,256]{2,1,0:T(8,128)S(1)}, bf16[256,256]{1,0:T(8,128)(2,1)S(1)}, bf16[256,256]{1,0:T(8,128)(2,1)S(1)}) custom-call(s32[4]{0:T(128)S(1)} %pad_add_fusion.refs_0_, f32[256,256]{1,0:T(8,128)} %get-tuple-element.36.refs_1_.refs_5_, f32[256,256]{1,0:T(8,128)} %collective-permute-done.4.refs_2_, ...), custom_call_target="tpu_custom_call" | custom-call | flops 603979776 | bytes 4456464 | tf_op jit(solution)/shard_map/group_map/pallas_call | solution.py:43
  87.4 1.4 collective-permute-done.11.refs_2_
  88.8 1.3 group_shift.1
  90.1 0.7 hop0.1
  91.5 0.7 hop.6
  92.9 0.7 hop.7
  94.3 0.7 hop.8
  95.7 0.7 hop.9
  97.2 0.7 hop.10
  98.6 0.7 hop.11
  99.3 1.3 collective-permute-start.20
  100.6 16.4 %collective-permute-done.20.refs_8_ = f32[32,256]{1,0:T(8,128)S(1)} collective-permute-done((f32[32,256]{1,0:T(8,128)S(1)}, f32[32,256]{1,0:T(8,128)S(1)}, u32[]{:S(2)}, u32[]{:S(2)}) %collective-permute-start.20) | collective-permute-done | bytes 32800 | tf_op jit(solution)/shard_map/ppermute | solution.py:432
  117.0 1.0 chips.1
  118.1 2.7 %collective-permute-start.22 = (f32[32,256]{1,0:T(8,128)S(1)}, f32[32,256]{1,0:T(8,128)S(1)}, u32[]{:S(2)}, u32[]{:S(2)}) collective-permute-start(f32[32,256]{1,0:T(8,128)S(1)} %get-tuple-element.56), channel_id=1, source_target_pairs={{0,6},{1,7},{2,0},{3,1},{4,2},{5,3},{6,4},{7,5},{8,14},{9,15},{10,... | collective-permute-start | bytes 98312 | tf_op jit(solution)/shard_map/ppermute | solution.py:445
  120.7 1.3 collective-permute-done.21.refs_2_
  122.0 3.0 %collective-permute-done.23.refs_4_ = f32[32,256]{1,0:T(8,128)S(1)} collective-permute-done((f32[32,256]{1,0:T(8,128)S(1)}, f32[32,256]{1,0:T(8,128)S(1)}, u32[]{:S(2)}, u32[]{:S(2)}) %collective-permute-start.23) | collective-permute-done | bytes 32800 | tf_op jit(solution)/shard_map/ppermute | solution.py:445
  125.0 0.8 chip_start.1
  125.8 12.5 %collective-permute-start.24 = (f32[128,256]{1,0:T(8,128)S(1)}, f32[128,256]{1,0:T(8,128)S(1)}, u32[]{:S(2)}, u32[]{:S(2)}) collective-permute-start(f32[128,256]{1,0:T(8,128)S(1)} %get-tuple-element.60), channel_id=1, source_target_pairs={{0,1},{1,0},{2,3},{3,2},{4,5},{5,4},{6,7},{7,6},{8,9},{9,8},{10,11... | collective-permute-start | bytes 393224 | tf_op jit(solution)/shard_map/ppermute | solution.py:458
  138.3 1.0 collective-permute-done.24.refs_2_
  139.3 1.6 %finish.1 = (f32[8,256]{1,0:T(8,128)}, f32[256,256]{1,0:T(8,128)}) custom-call(s32[4]{0:T(128)S(1)} %pad_add_fusion.refs_0_, f32[128,256]{1,0:T(8,128)S(1)} %get-tuple-element.59.refs_1_, f32[128,256]{1,0:T(8,128)S(1)} %collective-permute-done.24.refs_2_, f32[256,256]{1,0:T(8,128)S(1)} %get-tuple-element.34.refs_1_.refs_3_, ...), custom_call_target="tpu_custom_call" | custom-call | flops 100663296 | bytes 1073168 | tf_op jit(solution)/shard_map/finish/pallas_call | solution.py:43
  (44 shorter events, 7.5 us)
Async XLA Ops:
  0.7 1.6 %copy-start.4 = (f32[8,256,256]{2,1,0:T(8,128)S(1)}, f32[8,256,256]{2,1,0:T(8,128)}, u32[]{:S(2)}) copy-start(f32[8,256,256]{2,1,0:T(8,128)} %refs_3_.1) | copy-start | bytes 6291460
  2.3 0.7 copy-start.6
  3.0 0.7 copy-start.8
  6.4 1.9 %collective-permute-start = (f32[256,256]{1,0:T(8,128)S(1)}, f32[256,256]{1,0:T(8,128)S(1)}, u32[]{:S(2)}, u32[]{:S(2)}) collective-permute-start(f32[256,256]{1,0:T(8,128)S(1)} %get-tuple-element.34.refs_1_.refs_3_), channel_id=1, source_target_pairs={{0,1},{1,0},{2,3},{3,2},{4,5},{5,4},{6,7},{7,6},{8,9},{9,8},{10,11... | collective-permute-start | bytes 786440 | tf_op jit(solution)/shard_map/ppermute | solution.py:331
  9.2 0.7 copy-start.1
  9.9 24.5 %copy-start.2 = (f32[256,256]{1,0:T(8,128)S(1)}, f32[256,256]{1,0:T(8,128)}, u32[]{:S(2)}) copy-start(f32[256,256]{1,0:T(8,128)} %copy-done.1) | copy-start | bytes 786436
  9.9 54.2 %copy-start.9 = (f32[256]{0:T(256)S(1)}, f32[256]{0:T(256)}, u32[]{:S(2)}) copy-start(f32[256]{0:T(256)} %param.11) | copy-start | bytes 3076
  26.9 37.2 %all-to-all-start = ((f32[32,8,640]{2,1,0:T(8,128)}), f32[32,8,640]{2,1,0:T(8,128)S(1)}, u32[]{:S(2)}, u32[]{:S(2)}) async-start(f32[32,8,640]{2,1,0:T(8,128)} %pack.1.refs_5_), calls=%async_computation | async-start | bytes 1310720 | tf_op jit(solution)/shard_map/all_to_all | solution.py:351
  34.4 16.6 %collective-permute-start.3 = (f32[256,256]{1,0:T(8,128)S(1)}, f32[256,256]{1,0:T(8,128)S(1)}, u32[]{:S(2)}, u32[]{:S(2)}) collective-permute-start(f32[256,256]{1,0:T(8,128)S(1)} %copy-done.2), channel_id=1, source_target_pairs={{0,4},{1,5},{2,6},{3,7},{4,0},{5,1},{6,2},{7,3},{8,12},{9,13},{10,... | collective-permute-start | bytes 786440 | tf_op jit(solution)/shard_map/ppermute | solution.py:333
  37.4 17.8 %collective-permute-start.2 = (f32[256,256]{1,0:T(8,128)S(1)}, f32[256,256]{1,0:T(8,128)S(1)}, u32[]{:S(2)}, u32[]{:S(2)}) collective-permute-start(f32[256,256]{1,0:T(8,128)S(1)} %copy-done.2), channel_id=1, source_target_pairs={{0,6},{1,7},{2,0},{3,1},{4,2},{5,3},{6,4},{7,5},{8,14},{9,15},{10,... | collective-permute-start | bytes 786440 | tf_op jit(solution)/shard_map/ppermute | solution.py:333
  38.3 17.9 %collective-permute-start.1 = (f32[256,256]{1,0:T(8,128)S(1)}, f32[256,256]{1,0:T(8,128)S(1)}, u32[]{:S(2)}, u32[]{:S(2)}) collective-permute-start(f32[256,256]{1,0:T(8,128)S(1)} %copy-done.2), channel_id=1, source_target_pairs={{0,2},{1,3},{2,4},{3,5},{4,6},{5,7},{6,0},{7,1},{8,10},{9,11},{10,... | collective-permute-start | bytes 786440 | tf_op jit(solution)/shard_map/ppermute | solution.py:333
  56.2 1.1 copy-start
  59.5 25.4 %collective-permute-start.6 = (f32[256,256]{1,0:T(8,128)}, f32[256,256]{1,0:T(8,128)}, u32[]{:S(2)}, u32[]{:S(2)}) collective-permute-start(f32[256,256]{1,0:T(8,128)} %get-tuple-element.36.refs_1_.refs_5_), channel_id=1, source_target_pairs={{0,16},{1,17},{2,18},{3,19},{4,20},{5,21},{6,22},{7,23},{8,24},{9,... | collective-permute-start | bytes 786440 | tf_op jit(solution)/shard_map/ppermute | solution.py:362
  62.6 22.2 %collective-permute-start.5 = (f32[256,256]{1,0:T(8,128)}, f32[256,256]{1,0:T(8,128)}, u32[]{:S(2)}, u32[]{:S(2)}) collective-permute-start(f32[256,256]{1,0:T(8,128)} %get-tuple-element.36.refs_1_.refs_5_), channel_id=1, source_target_pairs={{0,24},{1,25},{2,26},{3,27},{4,28},{5,29},{6,30},{7,31},{8,0},{9,1... | collective-permute-start | bytes 786440 | tf_op jit(solution)/shard_map/ppermute | solution.py:362
  63.5 21.4 %collective-permute-start.4 = (f32[256,256]{1,0:T(8,128)}, f32[256,256]{1,0:T(8,128)}, u32[]{:S(2)}, u32[]{:S(2)}) collective-permute-start(f32[256,256]{1,0:T(8,128)} %get-tuple-element.36.refs_1_.refs_5_), channel_id=1, source_target_pairs={{0,8},{1,9},{2,10},{3,11},{4,12},{5,13},{6,14},{7,15},{8,16},{9,17... | collective-permute-start | bytes 786440 | tf_op jit(solution)/shard_map/ppermute | solution.py:362
  64.1 1.6 %copy-start.5 = (f32[8,256,256]{2,1,0:T(8,128)S(1)}, f32[8,256,256]{2,1,0:T(8,128)}, u32[]{:S(2)}) copy-start(f32[8,256,256]{2,1,0:T(8,128)} %refs_3_.1) | copy-start | bytes 6291460
  65.7 0.7 copy-start.7
  69.6 2.3 %collective-permute-start.7 = (f32[128,256]{1,0:T(8,128)S(1)}, f32[128,256]{1,0:T(8,128)S(1)}, u32[]{:S(2)}, u32[]{:S(2)}) collective-permute-start(f32[128,256]{1,0:T(8,128)S(1)} %get-tuple-element.41), channel_id=1, source_target_pairs={{0,1},{1,0},{2,3},{3,2},{4,5},{5,4},{6,7},{7,6},{8,9},{9,8},{10,11... | collective-permute-start | bytes 393224 | tf_op jit(solution)/shard_map/ppermute | solution.py:387
  72.7 4.1 %collective-permute-start.8 = (f32[32,256]{1,0:T(8,128)S(1)}, f32[32,256]{1,0:T(8,128)S(1)}, u32[]{:S(2)}, u32[]{:S(2)}) collective-permute-start(f32[32,256]{1,0:T(8,128)S(1)} %get-tuple-element.44), channel_id=1, source_target_pairs={{0,2},{1,3},{2,4},{3,5},{4,6},{5,7},{6,0},{7,1},{8,10},{9,11},{10,... | collective-permute-start | bytes 98312 | tf_op jit(solution)/shard_map/ppermute | solution.py:400
  72.8 4.0 %collective-permute-start.9 = (f32[32,256]{1,0:T(8,128)S(1)}, f32[32,256]{1,0:T(8,128)S(1)}, u32[]{:S(2)}, u32[]{:S(2)}) collective-permute-start(f32[32,256]{1,0:T(8,128)S(1)} %get-tuple-element.45), channel_id=1, source_target_pairs={{0,6},{1,7},{2,0},{3,1},{4,2},{5,3},{6,4},{7,5},{8,14},{9,15},{10,... | collective-permute-start | bytes 98312 | tf_op jit(solution)/shard_map/ppermute | solution.py:400
  76.7 4.3 %collective-permute-start.10 = (f32[32,256]{1,0:T(8,128)S(1)}, f32[32,256]{1,0:T(8,128)S(1)}, u32[]{:S(2)}, u32[]{:S(2)}) collective-permute-start(f32[32,256]{1,0:T(8,128)S(1)} %get-tuple-element.46), channel_id=1, source_target_pairs={{0,4},{1,5},{2,6},{3,7},{4,0},{5,1},{6,2},{7,3},{8,12},{9,13},{10,... | collective-permute-start | bytes 98312 | tf_op jit(solution)/shard_map/ppermute | solution.py:400
  82.0 5.4 %collective-permute-start.13 = (f32[32,256]{1,0:T(8,128)S(1)}, f32[32,256]{1,0:T(8,128)S(1)}, u32[]{:S(2)}, u32[]{:S(2)}) collective-permute-start(f32[32,256]{1,0:T(8,128)S(1)} %get-tuple-element.48.refs_1_), channel_id=1, source_target_pairs={{0,16},{1,17},{2,18},{3,19},{4,20},{5,21},{6,22},{7,23},{8,24},{9,... | collective-permute-start | bytes 98312 | tf_op jit(solution)/shard_map/ppermute | solution.py:412
  82.5 4.9 %collective-permute-start.12 = (f32[32,256]{1,0:T(8,128)S(1)}, f32[32,256]{1,0:T(8,128)S(1)}, u32[]{:S(2)}, u32[]{:S(2)}) collective-permute-start(f32[32,256]{1,0:T(8,128)S(1)} %get-tuple-element.48.refs_1_), channel_id=1, source_target_pairs={{0,24},{1,25},{2,26},{3,27},{4,28},{5,29},{6,30},{7,31},{8,0},{9,1... | collective-permute-start | bytes 98312 | tf_op jit(solution)/shard_map/ppermute | solution.py:412
  84.8 4.0 %collective-permute-start.11 = (f32[32,256]{1,0:T(8,128)S(1)}, f32[32,256]{1,0:T(8,128)S(1)}, u32[]{:S(2)}, u32[]{:S(2)}) collective-permute-start(f32[32,256]{1,0:T(8,128)S(1)} %get-tuple-element.48.refs_1_), channel_id=1, source_target_pairs={{0,8},{1,9},{2,10},{3,11},{4,12},{5,13},{6,14},{7,15},{8,16},{9,17... | collective-permute-start | bytes 98312 | tf_op jit(solution)/shard_map/ppermute | solution.py:412
  84.9 5.2 %copy-start.3 = (f32[256,256]{1,0:T(8,128)S(1)}, f32[256,256]{1,0:T(8,128)}, u32[]{:S(2)}) copy-start(f32[256,256]{1,0:T(8,128)} %refs_1_.5) | copy-start | bytes 786436
  90.8 0.7 collective-permute-start.14
  92.2 0.7 collective-permute-start.15
  93.6 0.7 collective-permute-start.16
  95.0 0.7 collective-permute-start.17
  96.5 0.7 collective-permute-start.18
  97.9 0.7 collective-permute-start.19
  99.3 17.7 %collective-permute-start.20 = (f32[32,256]{1,0:T(8,128)S(1)}, f32[32,256]{1,0:T(8,128)S(1)}, u32[]{:S(2)}, u32[]{:S(2)}) collective-permute-start(f32[32,256]{1,0:T(8,128)S(1)} %hop.11), channel_id=1, source_target_pairs={{192,224},{193,225},{194,226},{195,227},{196,228},{197,229},{198,2... | collective-permute-start | bytes 98312 | tf_op jit(solution)/shard_map/ppermute | solution.py:432
  118.0 4.1 %collective-permute-start.21 = (f32[32,256]{1,0:T(8,128)S(1)}, f32[32,256]{1,0:T(8,128)S(1)}, u32[]{:S(2)}, u32[]{:S(2)}) collective-permute-start(f32[32,256]{1,0:T(8,128)S(1)} %get-tuple-element.55), channel_id=1, source_target_pairs={{0,2},{1,3},{2,4},{3,5},{4,6},{5,7},{6,0},{7,1},{8,10},{9,11},{10,... | collective-permute-start | bytes 98312 | tf_op jit(solution)/shard_map/ppermute | solution.py:445
  118.1 4.0 %collective-permute-start.22 = (f32[32,256]{1,0:T(8,128)S(1)}, f32[32,256]{1,0:T(8,128)S(1)}, u32[]{:S(2)}, u32[]{:S(2)}) collective-permute-start(f32[32,256]{1,0:T(8,128)S(1)} %get-tuple-element.56), channel_id=1, source_target_pairs={{0,6},{1,7},{2,0},{3,1},{4,2},{5,3},{6,4},{7,5},{8,14},{9,15},{10,... | collective-permute-start | bytes 98312 | tf_op jit(solution)/shard_map/ppermute | solution.py:445
  120.7 4.3 %collective-permute-start.23 = (f32[32,256]{1,0:T(8,128)S(1)}, f32[32,256]{1,0:T(8,128)S(1)}, u32[]{:S(2)}, u32[]{:S(2)}) collective-permute-start(f32[32,256]{1,0:T(8,128)S(1)} %get-tuple-element.57), channel_id=1, source_target_pairs={{0,4},{1,5},{2,6},{3,7},{4,0},{5,1},{6,2},{7,3},{8,12},{9,13},{10,... | collective-permute-start | bytes 98312 | tf_op jit(solution)/shard_map/ppermute | solution.py:445
  125.8 13.5 %collective-permute-start.24 = (f32[128,256]{1,0:T(8,128)S(1)}, f32[128,256]{1,0:T(8,128)S(1)}, u32[]{:S(2)}, u32[]{:S(2)}) collective-permute-start(f32[128,256]{1,0:T(8,128)S(1)} %get-tuple-element.60), channel_id=1, source_target_pairs={{0,1},{1,0},{2,3},{3,2},{4,5},{5,4},{6,7},{7,6},{8,9},{9,8},{10,11... | collective-permute-start | bytes 393224 | tf_op jit(solution)/shard_map/ppermute | solution.py:458

commit v3 on v2

--- a/solution.py
+++ b/solution.py
@@ -52,8 +52,7 @@
     )(*args, *after)
 
 
-def pack_kernel(loads, samples_of, steps_of, counts, *refs, samples):
-    out, samples_buf, steps_buf, counts_buf, tags, sems = refs[-6:]
+def pack_kernel(loads, samples_of, steps_of, counts, out, samples_buf, steps_buf, counts_buf, sems, *, samples):
     owners, cap, modes = loads.shape
     half = cap // 2
     copies = [
@@ -72,12 +71,11 @@
     codes = codes.astype(F32)
     lane = lax.broadcasted_iota(jnp.int32, (half, 128), 1)
     for j in range(owners):
-        tags[j] = jnp.where(lane == 0, codes[:half, j : j + 1], codes[half:, j : j + 1])
-    last = pltpu.make_async_copy(tags, out.at[:, :, 2 * modes : 2 * modes + 128], sems.at[5])
-    last.start()
+        out[j, :, 2 * modes :] = jnp.where(
+            lane == 0, codes[:half, j : j + 1], codes[half:, j : j + 1]
+        )
     for copy in copies[3:]:
         copy.wait()
-    last.wait()
 
 
 def compose_kernel(pos, retain, coupling, probe, whole, seen):
@@ -316,6 +314,22 @@
 
     n_grp = lax.axis_size("grp")
 
+    packed = pl.pallas_call(
+        functools.partial(pack_kernel, samples=samples),
+        out_shape=jax.ShapeDtypeStruct((owners, cap // 2, 2 * modes + 128), F32),
+        in_specs=[pl.BlockSpec(memory_space=pltpu.HBM)] * 4,
+        out_specs=pl.BlockSpec(memory_space=pltpu.VMEM),
+        scratch_shapes=[
+            pltpu.VMEM((cap, owners), jnp.int32),
+            pltpu.VMEM((cap, owners), jnp.int32),
+            pltpu.VMEM((1, owners), jnp.int32),
+            pltpu.SemaphoreType.DMA((5,)),
+        ],
+        name="pack",
+        cost_estimate=pl.CostEstimate(flops=0, bytes_accessed=2**20, transcendentals=0),
+    )(rec_load[0], rec_sample[0].T, rec_step[0].T, rec_count)
+    arrived = lax.all_to_all(packed, "tm", split_axis=0, concat_axis=0)
+
     cube = 2 * modes * modes * modes
     probe_row = probe[None, :]
     whole, weights = call(
@@ -327,39 +341,11 @@
         coupling,
         probe_row,
         flops=22 * cube,
+        after=(packed,),
     )
     other = lax.ppermute(whole, "tm", swap)
     both, chip = call(pair_kernel, "pair_map", [(2,) + mat, mat], pos, whole, other, flops=3 * cube)
-    got = [lax.ppermute(chip, "tm", along_y(s)) for s in SHIFTS]
-    anywhere = pl.BlockSpec(memory_space=pl.ANY)
-    shape = (owners, cap // 2, 2 * modes + 128)
-    packed = pl.pallas_call(
-        functools.partial(pack_kernel, samples=samples),
-        out_shape=jax.ShapeDtypeStruct(shape, F32),
-        in_specs=[anywhere] * 5,
-        out_specs=anywhere,
-        scratch_shapes=[
-            pltpu.VMEM((cap, owners), jnp.int32),
-            pltpu.VMEM((cap, owners), jnp.int32),
-            pltpu.VMEM((1, owners), jnp.int32),
-            vm(owners, cap // 2, 128),
-            pltpu.SemaphoreType.DMA((6,)),
-        ],
-        name="pack",
-        cost_estimate=pl.CostEstimate(flops=0, bytes_accessed=2**20, transcendentals=0),
-    )(rec_load[0], rec_sample[0].T, rec_step[0].T, rec_count, chip)
-    arrived = lax.all_to_all(packed, "tm", split_axis=0, concat_axis=0)
-    y_maps, y_before, line = call(
-        line_map_kernel,
-        "line_map",
-        [(NY,) + mat, (NY - 1,) + mat, mat],
-        pos,
-        chip,
-        *got,
-        flops=9 * cube,
-        after=(packed,),
-    )
-    got = [lax.ppermute(line, "tm", along_x(s)) for s in SHIFTS]
+    chips = [lax.ppermute(chip, "tm", along_y(s)) for s in SHIFTS]
     shifted, kept, sent, driven = call(
         drive_kernel,
         "drive",
@@ -370,19 +356,6 @@
         coupling,
         probe_row,
         flops=60 * cube,
-        after=(line,),
-    )
-    half_mat = jax.ShapeDtypeStruct(mat, BF16)
-    x_maps, through, high, low = call(
-        group_map_kernel,
-        "group_map",
-        [(NX,) + mat, (NY,) + mat, half_mat, half_mat],
-        pos,
-        line,
-        *got,
-        y_before,
-        scratch=[vm(NX, *mat)],
-        flops=18 * cube,
     )
     back = lax.ppermute(sent, "tm", swap)
     small = (part, modes)
@@ -398,6 +371,29 @@
         flops=cube,
     )
     got = [lax.ppermute(r, "tm", along_y(s)) for r, s in zip(rows[1:], SHIFTS)]
+    y_maps, y_before, line = call(
+        line_map_kernel,
+        "line_map",
+        [(NY,) + mat, (NY - 1,) + mat, mat],
+        pos,
+        chip,
+        *chips,
+        flops=9 * cube,
+        after=got,
+    )
+    lines = [lax.ppermute(line, "tm", along_x(s)) for s in SHIFTS]
+    half_mat = jax.ShapeDtypeStruct(mat, BF16)
+    x_maps, through, high, low = call(
+        group_map_kernel,
+        "group_map",
+        [(NX,) + mat, (NY,) + mat, half_mat, half_mat],
+        pos,
+        line,
+        *lines,
+        y_before,
+        scratch=[vm(NX, *mat)],
+        flops=18 * cube,
+    )
     b_before, b_line = call(
         line_shift_kernel,
         "line_shift",

time: 141 us -> 105 us (0.74)
  Pallas kernels: 39.7 us -> 24.8 us
  waiting for transfers between devices: 48.1 us -> 36.3 us
  local copies, waits for them, and re-layouts: 7.05 us -> 1.11 us
  starting transfers between devices: 44.9 us -> 41.2 us
    pallas_call x1, Pallas kernels: 17 us -> 2.1 us  [body(): pl.pallas_call(functools.partial(pack_kernel, samples=samples), out_shape...]
    ppermute x6, waiting for transfers between devices: 17.3 us -> 10 us  [the longest x3 6.88 us: body(): lines = [lax.ppermute(line, 'tm', along_x(s)) for s in SHIFTS]]
    unnamed x20 -> x14, local copies, waits for them, and re-layouts: 7.05 us -> 1.11 us
    ppermute x6, waiting for transfers between devices: 9.82 us -> 4.65 us  [body(): got = [lax.ppermute(r, 'tm', along_y(s)) for r, s in zip(rows[1:], SHIFTS)]]
    ppermute x2, starting transfers between devices: 13.9 us -> 10.3 us  [body(): back = lax.ppermute(sent, 'tm', swap)]
    all_to_all x1, waiting for transfers between devices: 0.01 us -> 1.54 us  [body(): arrived = lax.all_to_all(packed, 'tm', split_axis=0, concat_axis=0)]
  transfers between devices with their start and end apart: 26 -> 26, of which waited for: 12 -> 14; matrix products, arithmetic and copies ran while one was open for 0% -> 0% of each run, Pallas kernels for 7% -> 11%
where the time goes in v3:
time: 105 us; the launch traced here: 104 us
  starting transfers between devices  41.2 us (39%)
  waiting for transfers between devices  36.3 us (35%)
  Pallas kernels  24.8 us (24%)
  local copies, waits for them, and re-layouts  1.11 us (1%)
    pallas_call x18, Pallas kernels, call(): pl.pallas_call(run, out_shape=shapes, in_specs=[smem] + [vmem] * (n_args...  22.7 us
    ppermute x6, waiting for transfers between devices, body(): carried.append(lax.ppermute(e, 'grp', [(k, k + 1)]))  16.4 us
    ppermute x2, starting transfers between devices, body(): back = lax.ppermute(sent, 'tm', swap)  10.3 us
    all_to_all x1, starting transfers between devices, body(): arrived = lax.all_to_all(packed, 'tm', split_axis=0, concat_axis=0)  7.77 us
    ppermute x3, waiting for transfers between devices, body(): lines = [lax.ppermute(line, 'tm', along_x(s)) for s in SHIFTS]  6.88 us
    ppermute x6, starting transfers between devices, body(): got = [lax.ppermute(r, 'tm', along_y(s)) for r, s in zip(rows[1:], SHIFTS)]  6.23 us
    ppermute x6, starting transfers between devices, body(): carried.append(lax.ppermute(e, 'grp', [(k, k + 1)]))  4.88 us
    ppermute x6, waiting for transfers between devices, body(): got = [lax.ppermute(r, 'tm', along_y(s)) for r, s in zip(rows[1:], SHIFTS)]  4.65 us
  transfers between devices with their start and end apart: 26, of which 14 were waited for; matrix products, arithmetic and copies ran while one was open for 0% of the time, Pallas kernels for 11%

profile of v3, /device:TPU:225, one launch (start us, length us, event | category | flops | bytes accessed | tf_op | source)
XLA Modules:
  0.0 104.5 jit_solution(5441374213647824922)
XLA Ops:
  0.7 2.1 %pack.1.refs_4_ = f32[32,8,640]{2,1,0:T(8,128)} custom-call(f32[32,16,256]{2,1,0:T(8,128)} %bitcast.15, s32[16,32]{1,0:T(8,128)} %bitcast.16, s32[16,32]{1,0:T(8,128)} %bitcast.17, s32[1,32]{1,0:T(1,128)} %counts.1), custom_call_target="tpu_custom_call" | custom-call | bytes 1048576 | tf_op jit(solution)/shard_map/pack/pallas_call | solution.py:317
  2.8 7.8 %all-to-all-start = ((f32[32,8,640]{2,1,0:T(8,128)}), f32[32,8,640]{2,1,0:T(8,128)S(1)}, u32[]{:S(2)}, u32[]{:S(2)}) async-start(f32[32,8,640]{2,1,0:T(8,128)} %pack.1.refs_4_), calls=%async_computation | async-start | bytes 1310720 | tf_op jit(solution)/shard_map/all_to_all | solution.py:331
  10.7 1.1 %copy-done = f32[32,8,640]{2,1,0:T(8,128)S(1)} copy-done((f32[32,8,640]{2,1,0:T(8,128)S(1)}, f32[32,8,640]{2,1,0:T(8,128)}, u32[]{:S(2)}) %copy-start) | copy-done | bytes 655384
  11.8 2.7 %compose.1 = (f32[256,256]{1,0:T(8,128)S(1)}, f32[8,256]{1,0:T(8,128)S(1)}) custom-call(s32[4]{0:T(128)S(1)} %pad_add_fusion.refs_0_, f32[8,256]{1,0:T(8,128)S(1)} %copy-done.3, f32[8,256,256]{2,1,0:T(8,128)S(1)} %copy-done.1, f32[1,256]{1,0:T(1,128)S(1)} %bitcast.13, f32[32,8,640]{2,1,0:T(8,128)S(1)} %copy-done), custom_call_target="tpu_custom_call" | custom-call | flops 738197504 | bytes 2376720 | tf_op jit(solution)/shard_map/compose/pallas_call | solution.py:43
  14.8 1.3 %collective-permute-done.refs_2_ = f32[256,256]{1,0:T(8,128)S(1)} collective-permute-done((f32[256,256]{1,0:T(8,128)S(1)}, f32[256,256]{1,0:T(8,128)S(1)}, u32[]{:S(2)}, u32[]{:S(2)}) %collective-permute-start) | collective-permute-done | bytes 262176 | tf_op jit(solution)/shard_map/ppermute | solution.py:346
  16.1 1.6 %pair_map.1 = (f32[2,256,256]{2,1,0:T(8,128)S(1)}, f32[256,256]{1,0:T(8,128)}) custom-call(s32[4]{0:T(128)S(1)} %pad_add_fusion.refs_0_, f32[256,256]{1,0:T(8,128)S(1)} %get-tuple-element.34.refs_1_.refs_3_, f32[256,256]{1,0:T(8,128)S(1)} %collective-permute-done.refs_2_), custom_call_target="tpu_custom_call" | custom-call | flops 100663296 | bytes 1310736 | tf_op jit(solution)/shard_map/pair_map/pallas_call | solution.py:43
  17.6 2.9 %collective-permute-start.3 = (f32[256,256]{1,0:T(8,128)}, f32[256,256]{1,0:T(8,128)}, u32[]{:S(2)}, u32[]{:S(2)}) collective-permute-start(f32[256,256]{1,0:T(8,128)} %get-tuple-element.35.refs_1_), channel_id=1, source_target_pairs={{0,4},{1,5},{2,6},{3,7},{4,0},{5,1},{6,2},{7,3},{8,12},{9,13},{10,... | collective-permute-start | bytes 786440 | tf_op jit(solution)/shard_map/ppermute | solution.py:348
  20.5 0.9 collective-permute-start.2
  22.0 1.5 %all-to-all-done.refs_1_ = f32[32,8,640]{2,1,0:T(8,128)S(1)} async-done(((f32[32,8,640]{2,1,0:T(8,128)}), f32[32,8,640]{2,1,0:T(8,128)S(1)}, u32[]{:S(2)}, u32[]{:S(2)}) %all-to-all-start) | async-done | bytes 655392 | tf_op jit(solution)/shard_map/all_to_all | solution.py:331
  23.6 3.2 %drive.1 = (f32[256,256]{1,0:T(8,128)S(1)}, f32[128,256]{1,0:T(8,128)S(1)}, f32[128,256]{1,0:T(8,128)S(1)}, f32[8,256]{1,0:T(8,128)S(1)}) custom-call(s32[4]{0:T(128)S(1)} %pad_add_fusion.refs_0_, f32[32,8,640]{2,1,0:T(8,128)S(1)} %all-to-all-done.refs_1_, f32[8,256]{1,0:T(8,128)S(1)} %copy-done.3, f32[8,256,256]{2,1,0:T(8,128)S(1)} %copy-done.1, ...), custom_call_target="tpu_custom_call" | custom-call | flops 2013265920 | bytes 3294224 | tf_op jit(solution)/shard_map/drive/pallas_call | solution.py:43
  26.8 1.3 %collective-permute-done.4.refs_2_ = f32[128,256]{1,0:T(8,128)S(1)} collective-permute-done((f32[128,256]{1,0:T(8,128)S(1)}, f32[128,256]{1,0:T(8,128)S(1)}, u32[]{:S(2)}, u32[]{:S(2)}) %collective-permute-start.4) | collective-permute-done | bytes 131104 | tf_op jit(solution)/shard_map/ppermute | solution.py:360
  28.1 0.8 pair_shift.1
  29.0 2.7 %collective-permute-start.6 = (f32[32,256]{1,0:T(8,128)S(1)}, f32[32,256]{1,0:T(8,128)S(1)}, u32[]{:S(2)}, u32[]{:S(2)}) collective-permute-start(f32[32,256]{1,0:T(8,128)S(1)} %get-tuple-element.40), channel_id=1, source_target_pairs={{0,6},{1,7},{2,0},{3,1},{4,2},{5,3},{6,4},{7,5},{8,14},{9,15},{10,... | collective-permute-start | bytes 98312 | tf_op jit(solution)/shard_map/ppermute | solution.py:373
  31.7 1.6 %collective-permute-done.2.refs_3_ = f32[256,256]{1,0:T(8,128)} collective-permute-done((f32[256,256]{1,0:T(8,128)}, f32[256,256]{1,0:T(8,128)}, u32[]{:S(2)}, u32[]{:S(2)}) %collective-permute-start.2) | collective-permute-done | bytes 262176 | tf_op jit(solution)/shard_map/ppermute | solution.py:348
  33.3 1.5 %collective-permute-done.1.refs_2_ = f32[256,256]{1,0:T(8,128)} collective-permute-done((f32[256,256]{1,0:T(8,128)}, f32[256,256]{1,0:T(8,128)}, u32[]{:S(2)}, u32[]{:S(2)}) %collective-permute-start.1) | collective-permute-done | bytes 262176 | tf_op jit(solution)/shard_map/ppermute | solution.py:348
  36.0 2.1 %line_map.1 = (f32[4,256,256]{2,1,0:T(8,128)S(1)}, f32[3,256,256]{2,1,0:T(8,128)S(1)}, f32[256,256]{1,0:T(8,128)S(1)}) custom-call(s32[4]{0:T(128)S(1)} %pad_add_fusion.refs_0_, f32[256,256]{1,0:T(8,128)} %get-tuple-element.35.refs_1_, f32[256,256]{1,0:T(8,128)} %collective-permute-done.1.refs_2_, f32[256,256]{1,0:T(8,128)} %collective-permute-done.2.refs_3_, ...), custom_call_target="tpu_custom_call" | custom-call | flops 301989888 | bytes 3145744 | tf_op jit(solution)/shard_map/line_map/pallas_call | solution.py:43
  38.1 2.0 %collective-permute-start.10 = (f32[256,256]{1,0:T(8,128)S(1)}, f32[256,256]{1,0:T(8,128)S(1)}, u32[]{:S(2)}, u32[]{:S(2)}) collective-permute-start(f32[256,256]{1,0:T(8,128)S(1)} %get-tuple-element.42.refs_1_), channel_id=1, source_target_pairs={{0,16},{1,17},{2,18},{3,19},{4,20},{5,21},{6,22},{7,23},{8,24},{9,... | collective-permute-start | bytes 786440 | tf_op jit(solution)/shard_map/ppermute | solution.py:384
  40.1 0.9 collective-permute-start.9
  41.6 1.1 %line_shift.1 = (f32[3,32,256]{2,1,0:T(8,128)S(1)}, f32[32,256]{1,0:T(8,128)S(1)}) custom-call(s32[4]{0:T(128)S(1)} %pad_add_fusion.refs_0_, f32[32,256]{1,0:T(8,128)S(1)} %get-tuple-element.46.refs_1_, f32[32,256]{1,0:T(8,128)S(1)} %collective-permute-done.5.refs_5_.refs_2_, f32[32,256]{1,0:T(8,128)S(1)} %collective-permute-done.6.refs_6_.refs_3_, ...), custom_call_target="tpu_custom_call" | custom-call | flops 33554432 | bytes 1310736 | tf_op jit(solution)/shard_map/line_shift/pallas_call | solution.py:43
  42.7 1.1 %collective-permute-start.13 = (f32[32,256]{1,0:T(8,128)S(1)}, f32[32,256]{1,0:T(8,128)S(1)}, u32[]{:S(2)}, u32[]{:S(2)}) collective-permute-start(f32[32,256]{1,0:T(8,128)S(1)} %get-tuple-element.48.refs_1_), channel_id=1, source_target_pairs={{0,16},{1,17},{2,18},{3,19},{4,20},{5,21},{6,22},{7,23},{8,24},{9,... | collective-permute-start | bytes 98312 | tf_op jit(solution)/shard_map/ppermute | solution.py:408
  43.8 1.7 %collective-permute-start.12 = (f32[32,256]{1,0:T(8,128)S(1)}, f32[32,256]{1,0:T(8,128)S(1)}, u32[]{:S(2)}, u32[]{:S(2)}) collective-permute-start(f32[32,256]{1,0:T(8,128)S(1)} %get-tuple-element.48.refs_1_), channel_id=1, source_target_pairs={{0,24},{1,25},{2,26},{3,27},{4,28},{5,29},{6,30},{7,31},{8,0},{9,1... | collective-permute-start | bytes 98312 | tf_op jit(solution)/shard_map/ppermute | solution.py:408
  45.9 6.0 %collective-permute-done.9.refs_3_ = f32[256,256]{1,0:T(8,128)S(1)} collective-permute-done((f32[256,256]{1,0:T(8,128)S(1)}, f32[256,256]{1,0:T(8,128)S(1)}, u32[]{:S(2)}, u32[]{:S(2)}) %collective-permute-start.9) | collective-permute-done | bytes 262176 | tf_op jit(solution)/shard_map/ppermute | solution.py:384
  52.0 0.7 collective-permute-done.8.refs_2_
  52.7 1.8 %group_map.1 = (f32[4,256,256]{2,1,0:T(8,128)S(1)}, f32[4,256,256]{2,1,0:T(8,128)S(1)}, bf16[256,256]{1,0:T(8,128)(2,1)S(1)}, bf16[256,256]{1,0:T(8,128)(2,1)S(1)}) custom-call(s32[4]{0:T(128)S(1)} %pad_add_fusion.refs_0_, f32[256,256]{1,0:T(8,128)S(1)} %get-tuple-element.42.refs_1_, f32[256,256]{1,0:T(8,128)S(1)} %collective-permute-done.8.refs_2_, ...), custom_call_target="tpu_custom_call" | custom-call | flops 603979776 | bytes 4456464 | tf_op jit(solution)/shard_map/group_map/pallas_call | solution.py:43
  54.6 1.3 %group_shift.1 = (f32[4,32,256]{2,1,0:T(8,128)S(1)}, f32[32,256]{1,0:T(8,128)S(1)}) custom-call(s32[4]{0:T(128)S(1)} %pad_add_fusion.refs_0_, f32[32,256]{1,0:T(8,128)S(1)} %get-tuple-element.48.refs_1_, f32[32,256]{1,0:T(8,128)S(1)} %collective-permute-done.11.refs_2_, f32[32,256]{1,0:T(8,128)S(1)} %collective-permute-done.12.refs_3_, ...), custom_call_target="tpu_custom_call" | custom-call | flops 67108864 | bytes 2228240 | tf_op jit(solution)/shard_map/group_shift/pallas_call | solution.py:43
  55.9 0.7 hop0.1
  56.6 0.7 collective-permute-start.14
  57.3 0.7 hop.6
  58.0 0.8 collective-permute-start.15
  58.8 0.7 hop.7
  59.5 0.7 collective-permute-start.16
  60.2 0.7 hop.8
  60.9 0.7 collective-permute-start.17
  61.7 0.7 hop.9
  63.1 0.7 hop.10
  63.8 0.7 collective-permute-start.19
  64.5 0.7 hop.11
  65.2 1.3 %collective-permute-start.20 = (f32[32,256]{1,0:T(8,128)S(1)}, f32[32,256]{1,0:T(8,128)S(1)}, u32[]{:S(2)}, u32[]{:S(2)}) collective-permute-start(f32[32,256]{1,0:T(8,128)S(1)} %hop.11), channel_id=1, source_target_pairs={{192,224},{193,225},{194,226},{195,227},{196,228},{197,229},{198,2... | collective-permute-start | bytes 98312 | tf_op jit(solution)/shard_map/ppermute | solution.py:428
  66.5 16.4 %collective-permute-done.20.refs_8_ = f32[32,256]{1,0:T(8,128)S(1)} collective-permute-done((f32[32,256]{1,0:T(8,128)S(1)}, f32[32,256]{1,0:T(8,128)S(1)}, u32[]{:S(2)}, u32[]{:S(2)}) %collective-permute-start.20) | collective-permute-done | bytes 32800 | tf_op jit(solution)/shard_map/ppermute | solution.py:428
  82.9 1.0 chips.1
  83.9 0.8 collective-permute-start.21
  84.6 2.0 %collective-permute-start.22 = (f32[32,256]{1,0:T(8,128)S(1)}, f32[32,256]{1,0:T(8,128)S(1)}, u32[]{:S(2)}, u32[]{:S(2)}) collective-permute-start(f32[32,256]{1,0:T(8,128)S(1)} %get-tuple-element.56), channel_id=1, source_target_pairs={{0,6},{1,7},{2,0},{3,1},{4,2},{5,3},{6,4},{7,5},{8,14},{9,15},{10,... | collective-permute-start | bytes 98312 | tf_op jit(solution)/shard_map/ppermute | solution.py:441
  86.6 0.7 collective-permute-start.23
  87.9 3.0 %collective-permute-done.23.refs_4_ = f32[32,256]{1,0:T(8,128)S(1)} collective-permute-done((f32[32,256]{1,0:T(8,128)S(1)}, f32[32,256]{1,0:T(8,128)S(1)}, u32[]{:S(2)}, u32[]{:S(2)}) %collective-permute-start.23) | collective-permute-done | bytes 32800 | tf_op jit(solution)/shard_map/ppermute | solution.py:441
  90.9 0.8 chip_start.1
  91.7 10.2 %collective-permute-start.24 = (f32[128,256]{1,0:T(8,128)S(1)}, f32[128,256]{1,0:T(8,128)S(1)}, u32[]{:S(2)}, u32[]{:S(2)}) collective-permute-start(f32[128,256]{1,0:T(8,128)S(1)} %get-tuple-element.60), channel_id=1, source_target_pairs={{0,1},{1,0},{2,3},{3,2},{4,5},{5,4},{6,7},{7,6},{8,9},{9,8},{10,11... | collective-permute-start | bytes 393224 | tf_op jit(solution)/shard_map/ppermute | solution.py:454
  101.8 1.0 collective-permute-done.24.refs_2_
  102.8 1.6 %finish.1 = (f32[8,256]{1,0:T(8,128)}, f32[256,256]{1,0:T(8,128)}) custom-call(s32[4]{0:T(128)S(1)} %pad_add_fusion.refs_0_, f32[128,256]{1,0:T(8,128)S(1)} %get-tuple-element.59.refs_1_, f32[128,256]{1,0:T(8,128)S(1)} %collective-permute-done.24.refs_2_, f32[256,256]{1,0:T(8,128)S(1)} %get-tuple-element.34.refs_1_.refs_3_, ...), custom_call_target="tpu_custom_call" | custom-call | flops 100663296 | bytes 1073168 | tf_op jit(solution)/shard_map/finish/pallas_call | solution.py:43
  (38 shorter events, 4.6 us)
Async XLA Ops:
  0.6 10.0 %copy-start.1 = (f32[8,256,256]{2,1,0:T(8,128)S(1)}, f32[8,256,256]{2,1,0:T(8,128)}, u32[]{:S(2)}) copy-start(f32[8,256,256]{2,1,0:T(8,128)} %refs_3_.1) | copy-start | bytes 6291460
  0.6 10.0 %copy-start.3 = (f32[8,256]{1,0:T(8,128)S(1)}, f32[8,256]{1,0:T(8,128)}, u32[]{:S(2)}) copy-start(f32[8,256]{1,0:T(8,128)} %refs_2_.3) | copy-start | bytes 24580
  0.7 10.0 %copy-start.6 = (f32[256]{0:T(256)S(1)}, f32[256]{0:T(256)}, u32[]{:S(2)}) copy-start(f32[256]{0:T(256)} %param.11) | copy-start | bytes 3076
  2.8 20.8 %all-to-all-start = ((f32[32,8,640]{2,1,0:T(8,128)}), f32[32,8,640]{2,1,0:T(8,128)S(1)}, u32[]{:S(2)}, u32[]{:S(2)}) async-start(f32[32,8,640]{2,1,0:T(8,128)} %pack.1.refs_4_), calls=%async_computation | async-start | bytes 1310720 | tf_op jit(solution)/shard_map/all_to_all | solution.py:331
  10.7 1.1 %copy-start = (f32[32,8,640]{2,1,0:T(8,128)S(1)}, f32[32,8,640]{2,1,0:T(8,128)}, u32[]{:S(2)}) copy-start(f32[32,8,640]{2,1,0:T(8,128)} %pack.1.refs_4_) | copy-start | bytes 1966084
  14.4 7.0 %copy-start.4 = (f32[8,256]{1,0:T(8,128)}, f32[8,256]{1,0:T(8,128)S(1)}, u32[]{:S(2)}) copy-start(f32[8,256]{1,0:T(8,128)S(1)} %get-tuple-element.62.refs_5_) | copy-start | bytes 24580
  14.5 1.6 %collective-permute-start = (f32[256,256]{1,0:T(8,128)S(1)}, f32[256,256]{1,0:T(8,128)S(1)}, u32[]{:S(2)}, u32[]{:S(2)}) collective-permute-start(f32[256,256]{1,0:T(8,128)S(1)} %get-tuple-element.34.refs_1_.refs_3_), channel_id=1, source_target_pairs={{0,1},{1,0},{2,3},{3,2},{4,5},{5,4},{6,7},{7,6},{8,9},{9,8},{10,11... | collective-permute-start | bytes 786440 | tf_op jit(solution)/shard_map/ppermute | solution.py:346
  17.6 14.0 %collective-permute-start.3 = (f32[256,256]{1,0:T(8,128)}, f32[256,256]{1,0:T(8,128)}, u32[]{:S(2)}, u32[]{:S(2)}) collective-permute-start(f32[256,256]{1,0:T(8,128)} %get-tuple-element.35.refs_1_), channel_id=1, source_target_pairs={{0,4},{1,5},{2,6},{3,7},{4,0},{5,1},{6,2},{7,3},{8,12},{9,13},{10,... | collective-permute-start | bytes 786440 | tf_op jit(solution)/shard_map/ppermute | solution.py:348
  20.5 12.8 %collective-permute-start.2 = (f32[256,256]{1,0:T(8,128)}, f32[256,256]{1,0:T(8,128)}, u32[]{:S(2)}, u32[]{:S(2)}) collective-permute-start(f32[256,256]{1,0:T(8,128)} %get-tuple-element.35.refs_1_), channel_id=1, source_target_pairs={{0,6},{1,7},{2,0},{3,1},{4,2},{5,3},{6,4},{7,5},{8,14},{9,15},{10,... | collective-permute-start | bytes 786440 | tf_op jit(solution)/shard_map/ppermute | solution.py:348
  21.4 13.4 %collective-permute-start.1 = (f32[256,256]{1,0:T(8,128)}, f32[256,256]{1,0:T(8,128)}, u32[]{:S(2)}, u32[]{:S(2)}) collective-permute-start(f32[256,256]{1,0:T(8,128)} %get-tuple-element.35.refs_1_), channel_id=1, source_target_pairs={{0,2},{1,3},{2,4},{3,5},{4,6},{5,7},{6,0},{7,1},{8,10},{9,11},{10,... | collective-permute-start | bytes 786440 | tf_op jit(solution)/shard_map/ppermute | solution.py:348
  26.7 1.4 %collective-permute-start.4 = (f32[128,256]{1,0:T(8,128)S(1)}, f32[128,256]{1,0:T(8,128)S(1)}, u32[]{:S(2)}, u32[]{:S(2)}) collective-permute-start(f32[128,256]{1,0:T(8,128)S(1)} %get-tuple-element.37), channel_id=1, source_target_pairs={{0,1},{1,0},{2,3},{3,2},{4,5},{5,4},{6,7},{7,6},{8,9},{9,8},{10,11... | collective-permute-start | bytes 393224 | tf_op jit(solution)/shard_map/ppermute | solution.py:360
  28.9 6.5 %collective-permute-start.5 = (f32[32,256]{1,0:T(8,128)S(1)}, f32[32,256]{1,0:T(8,128)S(1)}, u32[]{:S(2)}, u32[]{:S(2)}) collective-permute-start(f32[32,256]{1,0:T(8,128)S(1)} %get-tuple-element.39), channel_id=1, source_target_pairs={{0,2},{1,3},{2,4},{3,5},{4,6},{5,7},{6,0},{7,1},{8,10},{9,11},{10,... | collective-permute-start | bytes 98312 | tf_op jit(solution)/shard_map/ppermute | solution.py:373
  29.0 6.4 %collective-permute-start.6 = (f32[32,256]{1,0:T(8,128)S(1)}, f32[32,256]{1,0:T(8,128)S(1)}, u32[]{:S(2)}, u32[]{:S(2)}) collective-permute-start(f32[32,256]{1,0:T(8,128)S(1)} %get-tuple-element.40), channel_id=1, source_target_pairs={{0,6},{1,7},{2,0},{3,1},{4,2},{5,3},{6,4},{7,5},{8,14},{9,15},{10,... | collective-permute-start | bytes 98312 | tf_op jit(solution)/shard_map/ppermute | solution.py:373
  31.7 4.3 %collective-permute-start.7 = (f32[32,256]{1,0:T(8,128)S(1)}, f32[32,256]{1,0:T(8,128)S(1)}, u32[]{:S(2)}, u32[]{:S(2)}) collective-permute-start(f32[32,256]{1,0:T(8,128)S(1)} %get-tuple-element.41), channel_id=1, source_target_pairs={{0,4},{1,5},{2,6},{3,7},{4,0},{5,1},{6,2},{7,3},{8,12},{9,13},{10,... | collective-permute-start | bytes 98312 | tf_op jit(solution)/shard_map/ppermute | solution.py:373
  38.1 7.5 %collective-permute-start.10 = (f32[256,256]{1,0:T(8,128)S(1)}, f32[256,256]{1,0:T(8,128)S(1)}, u32[]{:S(2)}, u32[]{:S(2)}) collective-permute-start(f32[256,256]{1,0:T(8,128)S(1)} %get-tuple-element.42.refs_1_), channel_id=1, source_target_pairs={{0,16},{1,17},{2,18},{3,19},{4,20},{5,21},{6,22},{7,23},{8,24},{9,... | collective-permute-start | bytes 786440 | tf_op jit(solution)/shard_map/ppermute | solution.py:384
  40.1 11.8 %collective-permute-start.9 = (f32[256,256]{1,0:T(8,128)S(1)}, f32[256,256]{1,0:T(8,128)S(1)}, u32[]{:S(2)}, u32[]{:S(2)}) collective-permute-start(f32[256,256]{1,0:T(8,128)S(1)} %get-tuple-element.42.refs_1_), channel_id=1, source_target_pairs={{0,24},{1,25},{2,26},{3,27},{4,28},{5,29},{6,30},{7,31},{8,0},{9,1... | collective-permute-start | bytes 786440 | tf_op jit(solution)/shard_map/ppermute | solution.py:384
  41.0 11.7 %collective-permute-start.8 = (f32[256,256]{1,0:T(8,128)S(1)}, f32[256,256]{1,0:T(8,128)S(1)}, u32[]{:S(2)}, u32[]{:S(2)}) collective-permute-start(f32[256,256]{1,0:T(8,128)S(1)} %get-tuple-element.42.refs_1_), channel_id=1, source_target_pairs={{0,8},{1,9},{2,10},{3,11},{4,12},{5,13},{6,14},{7,15},{8,16},{9,17... | collective-permute-start | bytes 786440 | tf_op jit(solution)/shard_map/ppermute | solution.py:384
  42.7 11.9 %collective-permute-start.13 = (f32[32,256]{1,0:T(8,128)S(1)}, f32[32,256]{1,0:T(8,128)S(1)}, u32[]{:S(2)}, u32[]{:S(2)}) collective-permute-start(f32[32,256]{1,0:T(8,128)S(1)} %get-tuple-element.48.refs_1_), channel_id=1, source_target_pairs={{0,16},{1,17},{2,18},{3,19},{4,20},{5,21},{6,22},{7,23},{8,24},{9,... | collective-permute-start | bytes 98312 | tf_op jit(solution)/shard_map/ppermute | solution.py:408
  43.8 10.8 %collective-permute-start.12 = (f32[32,256]{1,0:T(8,128)S(1)}, f32[32,256]{1,0:T(8,128)S(1)}, u32[]{:S(2)}, u32[]{:S(2)}) collective-permute-start(f32[32,256]{1,0:T(8,128)S(1)} %get-tuple-element.48.refs_1_), channel_id=1, source_target_pairs={{0,24},{1,25},{2,26},{3,27},{4,28},{5,29},{6,30},{7,31},{8,0},{9,1... | collective-permute-start | bytes 98312 | tf_op jit(solution)/shard_map/ppermute | solution.py:408
  45.6 9.0 %collective-permute-start.11 = (f32[32,256]{1,0:T(8,128)S(1)}, f32[32,256]{1,0:T(8,128)S(1)}, u32[]{:S(2)}, u32[]{:S(2)}) collective-permute-start(f32[32,256]{1,0:T(8,128)S(1)} %get-tuple-element.48.refs_1_), channel_id=1, source_target_pairs={{0,8},{1,9},{2,10},{3,11},{4,12},{5,13},{6,14},{7,15},{8,16},{9,17... | collective-permute-start | bytes 98312 | tf_op jit(solution)/shard_map/ppermute | solution.py:408
  52.7 3.2 %copy-start.2 = (f32[256,256]{1,0:T(8,128)S(1)}, f32[256,256]{1,0:T(8,128)}, u32[]{:S(2)}) copy-start(f32[256,256]{1,0:T(8,128)} %refs_1_.5) | copy-start | bytes 786436
  56.6 0.7 collective-permute-start.14
  58.0 44.8 %copy-start.5 = (f32[8,256]{1,0:T(8,128)S(1)}, f32[8,256]{1,0:T(8,128)}, u32[]{:S(2)}) copy-start(f32[8,256]{1,0:T(8,128)} %copy-done.4) | copy-start | bytes 24580
  58.0 0.8 collective-permute-start.15
  59.5 0.7 collective-permute-start.16
  60.9 0.7 collective-permute-start.17
  62.4 0.7 collective-permute-start.18
  63.8 0.7 collective-permute-start.19
  65.2 17.7 %collective-permute-start.20 = (f32[32,256]{1,0:T(8,128)S(1)}, f32[32,256]{1,0:T(8,128)S(1)}, u32[]{:S(2)}, u32[]{:S(2)}) collective-permute-start(f32[32,256]{1,0:T(8,128)S(1)} %hop.11), channel_id=1, source_target_pairs={{192,224},{193,225},{194,226},{195,227},{196,228},{197,229},{198,2... | collective-permute-start | bytes 98312 | tf_op jit(solution)/shard_map/ppermute | solution.py:428
  83.9 4.1 %collective-permute-start.21 = (f32[32,256]{1,0:T(8,128)S(1)}, f32[32,256]{1,0:T(8,128)S(1)}, u32[]{:S(2)}, u32[]{:S(2)}) collective-permute-start(f32[32,256]{1,0:T(8,128)S(1)} %get-tuple-element.55), channel_id=1, source_target_pairs={{0,2},{1,3},{2,4},{3,5},{4,6},{5,7},{6,0},{7,1},{8,10},{9,11},{10,... | collective-permute-start | bytes 98312 | tf_op jit(solution)/shard_map/ppermute | solution.py:441
  84.6 3.3 %collective-permute-start.22 = (f32[32,256]{1,0:T(8,128)S(1)}, f32[32,256]{1,0:T(8,128)S(1)}, u32[]{:S(2)}, u32[]{:S(2)}) collective-permute-start(f32[32,256]{1,0:T(8,128)S(1)} %get-tuple-element.56), channel_id=1, source_target_pairs={{0,6},{1,7},{2,0},{3,1},{4,2},{5,3},{6,4},{7,5},{8,14},{9,15},{10,... | collective-permute-start | bytes 98312 | tf_op jit(solution)/shard_map/ppermute | solution.py:441
  86.6 4.3 %collective-permute-start.23 = (f32[32,256]{1,0:T(8,128)S(1)}, f32[32,256]{1,0:T(8,128)S(1)}, u32[]{:S(2)}, u32[]{:S(2)}) collective-permute-start(f32[32,256]{1,0:T(8,128)S(1)} %get-tuple-element.57), channel_id=1, source_target_pairs={{0,4},{1,5},{2,6},{3,7},{4,0},{5,1},{6,2},{7,3},{8,12},{9,13},{10,... | collective-permute-start | bytes 98312 | tf_op jit(solution)/shard_map/ppermute | solution.py:441
  91.7 11.2 %collective-permute-start.24 = (f32[128,256]{1,0:T(8,128)S(1)}, f32[128,256]{1,0:T(8,128)S(1)}, u32[]{:S(2)}, u32[]{:S(2)}) collective-permute-start(f32[128,256]{1,0:T(8,128)S(1)} %get-tuple-element.60), channel_id=1, source_target_pairs={{0,1},{1,0},{2,3},{3,2},{4,5},{5,4},{6,7},{7,6},{8,9},{9,8},{10,11... | collective-permute-start | bytes 393224 | tf_op jit(solution)/shard_map/ppermute | solution.py:454

commit v4 on v3

--- a/solution.py
+++ b/solution.py
@@ -170,6 +170,7 @@
 
 
 def group_map_kernel(pos, a0, a1, a3, a2, prefix, ordered, through, high, low, before):
+    y = pos[1]
     x = pos[2]
     order(x, NX, ordered, (a0, a1, a3, a2))
     modes = high.shape[0]
@@ -181,11 +182,11 @@
         before[k] = total
         total = mm(split(total), split(ordered[k]))
     high[...], low[...] = split(total)
-    own = before[x]
-    through[0] = own
-    own = split(own)
-    for k in range(1, NY):
-        through[k] = mm(own, split(prefix[k - 1]))
+    through[...] = before[x]
+
+    @pl.when(y > 0)
+    def _():
+        through[...] = mm(split(before[x]), split(prefix[jnp.maximum(y - 1, 0)]))
 
 
 def pair_shift_kernel(pos, kept, got, both, first, s0, s1, s3, s2, chip):
@@ -212,8 +213,10 @@
     line[...] = total
 
 
-def group_shift_kernel(pos, b0, b1, b3, b2, maps, prefix, before, through, group, ordered, own):
-    x = pos[2]
+def group_shift_kernel(
+    pos, b0, b1, b3, b2, maps, prefix, before, s0, s1, s3, s2, group, ordered, own, chips
+):
+    x, y = pos[2], pos[1]
     order(x, NX, ordered, (b0, b1, b3, b2))
     own[0] = jnp.zeros_like(ordered[0])
     total = ordered[0]
@@ -222,10 +225,12 @@
         total = mm(split(total), split(maps[k])) + ordered[k]
     group[...] = total
     prior = own[x]
-    through[0] = prior
+    chips[0] = prior
     prior = split(prior)
     for k in range(1, NY):
-        through[k] = mm(prior, split(prefix[k - 1])) + before[k - 1]
+        chips[k] = mm(prior, split(prefix[k - 1])) + before[k - 1]
+    for s, out in zip((0,) + SHIFTS, (s0, s1, s3, s2)):
+        out[...] = chips[lax.rem(y + s, NY)]
 
 
 def released_rows(pos, initial, part):
@@ -242,27 +247,28 @@
     out[...] = mm(split(got[...]), (high[...], low[...])) + shift[...]
 
 
-def last_hop_kernel(pos, initial, *refs):
-    gots, (maps, shifts, s0, s1, s3, s2, chips) = refs[:-7], refs[-7:]
-    y = pos[1]
+def last_hop_kernel(pos, got, high, low, shift, *refs):
+    earlier, out = refs[:-1], refs[-1]
     g = pos[3]
-    state = released_rows(pos, initial, s0.shape[0])
-    for k, got in enumerate(gots):
-        state = jnp.where(g == k + 1, got[...], state)
-    group = split(state)
-    for k in range(NY):
-        chips[k] = mm(group, split(maps[k])) + shifts[k]
-    for s, out in zip((0,) + SHIFTS, (s0, s1, s3, s2)):
-        out[...] = chips[lax.rem(y + s, NY)]
-
-
-def chip_kernel(pos, e0, e1, e3, e2, both, first, kept, sent, chip):
-    c, y = pos[0], pos[1]
+    state = mm(split(got[...]), (high[...], low[...])) + shift[...]
+    for k, ref in enumerate(earlier):
+        state = jnp.where(g == k, ref[...], state)
+    out[...] = state
+
+
+def chip_kernel(
+    pos, e0, e1, e3, e2, d0, d1, d3, d2, initial, through, both, first, kept, sent, state, driven
+):
+    c, y, g = pos[0], pos[1], pos[3]
     r = e0.shape[0]
-    for s, ref in zip((0,) + SHIFTS, (e0, e1, e3, e2)):
+    for s, ref, part in zip((0,) + SHIFTS, (e0, e1, e3, e2), (d0, d1, d3, d2)):
         start = pl.multiple_of(lax.rem(y + NY - s, NY) * r, r)
-        chip[pl.ds(start, r), :] = ref[...]
-    zero = chip[...]
+        state[pl.ds(start, r), :] = ref[...]
+        driven[pl.ds(start, r), :] = part[...]
+    h = kept.shape[0]
+    released = initial[pl.ds(pl.multiple_of(c * h, h), h), :]
+    group = jnp.where(g == 0, released, state[...])
+    zero = mm(split(group), split(through[...])) + driven[...]
     one = mm(split(zero), split(both[0])) + first[...]
     kept[...] = jnp.where(c == 0, zero, one)
     sent[...] = jnp.where(c == 0, one, zero)
@@ -386,7 +392,7 @@
     x_maps, through, high, low = call(
         group_map_kernel,
         "group_map",
-        [(NX,) + mat, (NY,) + mat, half_mat, half_mat],
+        [(NX,) + mat, mat, half_mat, half_mat],
         pos,
         line,
         *lines,
@@ -406,49 +412,61 @@
         flops=cube,
     )
     got = [lax.ppermute(b_line, "tm", along_x(s)) for s in SHIFTS]
-    b_through, b_group = call(
+    *parts, b_group = call(
         group_shift_kernel,
         "group_shift",
-        [(NY,) + small, small],
+        [small] * 5,
         pos,
         b_line,
         *got,
         x_maps,
         y_before,
         b_before,
-        scratch=[vm(NX, *small), vm(NX, *small)],
+        scratch=[vm(NX, *small), vm(NX, *small), vm(NY, *small)],
         flops=2 * cube,
     )
     (e,) = call(
         first_hop_kernel, "hop0", [small], pos, initial_state, high, low, b_group, flops=cube
     )
-    carried = [lax.ppermute(e, "grp", [(0, 1)])]
+    parts[1:] = [lax.ppermute(r, "tm", along_y(s)) for r, s in zip(parts[1:], SHIFTS)]
+    ends = [e]
     for k in range(1, n_grp - 1):
-        (e,) = call(hop_kernel, "hop", [small], pos, carried[-1], high, low, b_group, flops=cube)
-        carried.append(lax.ppermute(e, "grp", [(k, k + 1)]))
-    rows = call(
-        last_hop_kernel,
-        "chips",
-        [small] * 4,
-        pos,
-        initial_state,
-        *carried,
-        through,
-        b_through,
-        scratch=[vm(NY, *small)],
-        flops=2 * cube,
-    )
-    got = [lax.ppermute(r, "tm", along_y(s)) for r, s in zip(rows[1:], SHIFTS)]
+        came = lax.ppermute(ends[-1], "grp", [(k - 1, k)])
+        last = k == n_grp - 2
+        (e,) = call(
+            last_hop_kernel if last else hop_kernel,
+            "last_hop" if last else "hop",
+            [small],
+            pos,
+            came,
+            high,
+            low,
+            b_group,
+            *(ends if last else ()),
+            flops=cube,
+            after=parts[1:] if k == 3 else (),
+        )
+        ends.append(e)
+
+    def onward(s):
+        size = len(spots)
+        return [
+            (z * size + i, (z + 1) * size + j) for z in range(n_grp - 1) for i, j in along_y(s)
+        ]
+
+    got = [lax.ppermute(ends[-1], ("grp", "tm"), onward(s)) for s in (0,) + SHIFTS]
     kept, sent = call(
         chip_kernel,
         "chip_start",
         [(half, modes)] * 2,
         pos,
-        rows[0],
         *got,
+        *parts,
+        initial_state,
+        through,
         both,
         first,
-        scratch=[vm(half, modes)],
+        scratch=[vm(half, modes), vm(half, modes)],
         flops=cube,
     )
     back = lax.ppermute(sent, "tm", swap)

time: 105 us -> 110 us (1.048)
  the two profiles are of different devices: /device:TPU:225 before, /device:TPU:97 now
where the time goes in v4:
time: 110 us; the launch traced here: 109 us
  starting transfers between devices  59.8 us (54%)
  Pallas kernels  23.8 us (22%)
  waiting for transfers between devices  23.7 us (22%)
  local copies, waits for them, and re-layouts  1.11 us (1%)
    pallas_call x17, Pallas kernels, call(): pl.pallas_call(run, out_shape=shapes, in_specs=[smem] + [vmem] * (n_args...  21.7 us
    ppermute x4, starting transfers between devices, body(): lax.ppermute(ends[-1], ('grp', 'tm'), onward(s))  18.9 us
    ppermute x2, starting transfers between devices, body(): back = lax.ppermute(sent, 'tm', swap)  8.66 us
    all_to_all x1, starting transfers between devices, body(): arrived = lax.all_to_all(packed, 'tm', split_axis=0, concat_axis=0)  7.77 us
    ppermute x3, waiting for transfers between devices, body(): lines = [lax.ppermute(line, 'tm', along_x(s)) for s in SHIFTS]  6.88 us
    ppermute x6, starting transfers between devices, body(): came = lax.ppermute(ends[-1], 'grp', [(k - 1, k)])  6.55 us
    ppermute x3, starting transfers between devices, body(): chips = [lax.ppermute(chip, 'tm', along_y(s)) for s in SHIFTS]  4.36 us
    ppermute x3, starting transfers between devices, body(): lax.ppermute(r, 'tm', along_y(s))  3.77 us
  transfers between devices with their start and end apart: 29, of which 16 were waited for; matrix products, arithmetic and copies ran while one was open for 0% of the time, Pallas kernels for 10%

profile of v4, /device:TPU:97, one launch (start us, length us, event | category | flops | bytes accessed | tf_op | source)
XLA Modules:
  0.0 109.5 jit_solution(5048612983073347073)
XLA Ops:
  0.7 2.1 %pack.1.refs_4_ = f32[32,8,640]{2,1,0:T(8,128)} custom-call(f32[32,16,256]{2,1,0:T(8,128)} %bitcast.15, s32[16,32]{1,0:T(8,128)} %bitcast.16, s32[16,32]{1,0:T(8,128)} %bitcast.17, s32[1,32]{1,0:T(1,128)} %counts.1), custom_call_target="tpu_custom_call" | custom-call | bytes 1048576 | tf_op jit(solution)/shard_map/pack/pallas_call | solution.py:323
  2.8 7.8 %all-to-all-start = ((f32[32,8,640]{2,1,0:T(8,128)}), f32[32,8,640]{2,1,0:T(8,128)S(1)}, u32[]{:S(2)}, u32[]{:S(2)}) async-start(f32[32,8,640]{2,1,0:T(8,128)} %pack.1.refs_4_), calls=%async_computation | async-start | bytes 1310720 | tf_op jit(solution)/shard_map/all_to_all | solution.py:337
  10.7 1.1 copy-done
  11.8 2.7 %compose.1 = (f32[256,256]{1,0:T(8,128)S(1)}, f32[8,256]{1,0:T(8,128)S(1)}) custom-call(s32[4]{0:T(128)S(1)} %pad_add_fusion.refs_0_, f32[8,256]{1,0:T(8,128)S(1)} %copy-done.3, f32[8,256,256]{2,1,0:T(8,128)S(1)} %copy-done.1, f32[1,256]{1,0:T(1,128)S(1)} %bitcast.13, f32[32,8,640]{2,1,0:T(8,128)S(1)} %copy-done), custom_call_target="tpu_custom_call" | custom-call | flops 738197504 | bytes 2376720 | tf_op jit(solution)/shard_map/compose/pallas_call | solution.py:43
  14.8 1.3 %collective-permute-done.refs_2_ = f32[256,256]{1,0:T(8,128)S(1)} collective-permute-done((f32[256,256]{1,0:T(8,128)S(1)}, f32[256,256]{1,0:T(8,128)S(1)}, u32[]{:S(2)}, u32[]{:S(2)}) %collective-permute-start) | collective-permute-done | bytes 262176 | tf_op jit(solution)/shard_map/ppermute | solution.py:352
  16.1 1.6 %pair_map.1 = (f32[2,256,256]{2,1,0:T(8,128)S(1)}, f32[256,256]{1,0:T(8,128)}) custom-call(s32[4]{0:T(128)S(1)} %pad_add_fusion.refs_0_, f32[256,256]{1,0:T(8,128)S(1)} %get-tuple-element.33.refs_1_.refs_3_, f32[256,256]{1,0:T(8,128)S(1)} %collective-permute-done.refs_2_), custom_call_target="tpu_custom_call" | custom-call | flops 100663296 | bytes 1310736 | tf_op jit(solution)/shard_map/pair_map/pallas_call | solution.py:43
  17.7 2.9 %collective-permute-start.3 = (f32[256,256]{1,0:T(8,128)}, f32[256,256]{1,0:T(8,128)}, u32[]{:S(2)}, u32[]{:S(2)}) collective-permute-start(f32[256,256]{1,0:T(8,128)} %get-tuple-element.34.refs_1_), channel_id=1, source_target_pairs={{0,4},{1,5},{2,6},{3,7},{4,0},{5,1},{6,2},{7,3},{8,12},{9,13},{10,... | collective-permute-start | bytes 786440 | tf_op jit(solution)/shard_map/ppermute | solution.py:354
  20.5 0.9 collective-permute-start.2
  22.0 1.5 %all-to-all-done.refs_1_ = f32[32,8,640]{2,1,0:T(8,128)S(1)} async-done(((f32[32,8,640]{2,1,0:T(8,128)}), f32[32,8,640]{2,1,0:T(8,128)S(1)}, u32[]{:S(2)}, u32[]{:S(2)}) %all-to-all-start) | async-done | bytes 655392 | tf_op jit(solution)/shard_map/all_to_all | solution.py:337
  23.6 3.2 %drive.1 = (f32[256,256]{1,0:T(8,128)S(1)}, f32[128,256]{1,0:T(8,128)S(1)}, f32[128,256]{1,0:T(8,128)S(1)}, f32[8,256]{1,0:T(8,128)S(1)}) custom-call(s32[4]{0:T(128)S(1)} %pad_add_fusion.refs_0_, f32[32,8,640]{2,1,0:T(8,128)S(1)} %all-to-all-done.refs_1_, f32[8,256]{1,0:T(8,128)S(1)} %copy-done.3, f32[8,256,256]{2,1,0:T(8,128)S(1)} %copy-done.1, ...), custom_call_target="tpu_custom_call" | custom-call | flops 2013265920 | bytes 3294224 | tf_op jit(solution)/shard_map/drive/pallas_call | solution.py:43
  26.8 1.3 %collective-permute-done.4.refs_2_ = f32[128,256]{1,0:T(8,128)S(1)} collective-permute-done((f32[128,256]{1,0:T(8,128)S(1)}, f32[128,256]{1,0:T(8,128)S(1)}, u32[]{:S(2)}, u32[]{:S(2)}) %collective-permute-start.4) | collective-permute-done | bytes 131104 | tf_op jit(solution)/shard_map/ppermute | solution.py:366
  28.2 0.8 pair_shift.1
  29.0 2.7 %collective-permute-start.6 = (f32[32,256]{1,0:T(8,128)S(1)}, f32[32,256]{1,0:T(8,128)S(1)}, u32[]{:S(2)}, u32[]{:S(2)}) collective-permute-start(f32[32,256]{1,0:T(8,128)S(1)} %get-tuple-element.39), channel_id=1, source_target_pairs={{0,6},{1,7},{2,0},{3,1},{4,2},{5,3},{6,4},{7,5},{8,14},{9,15},{10,... | collective-permute-start | bytes 98312 | tf_op jit(solution)/shard_map/ppermute | solution.py:379
  31.7 1.6 %collective-permute-done.2.refs_3_ = f32[256,256]{1,0:T(8,128)} collective-permute-done((f32[256,256]{1,0:T(8,128)}, f32[256,256]{1,0:T(8,128)}, u32[]{:S(2)}, u32[]{:S(2)}) %collective-permute-start.2) | collective-permute-done | bytes 262176 | tf_op jit(solution)/shard_map/ppermute | solution.py:354
  33.3 1.5 %collective-permute-done.1.refs_2_ = f32[256,256]{1,0:T(8,128)} collective-permute-done((f32[256,256]{1,0:T(8,128)}, f32[256,256]{1,0:T(8,128)}, u32[]{:S(2)}, u32[]{:S(2)}) %collective-permute-start.1) | collective-permute-done | bytes 262176 | tf_op jit(solution)/shard_map/ppermute | solution.py:354
  36.0 2.1 %line_map.1 = (f32[4,256,256]{2,1,0:T(8,128)S(1)}, f32[3,256,256]{2,1,0:T(8,128)S(1)}, f32[256,256]{1,0:T(8,128)S(1)}) custom-call(s32[4]{0:T(128)S(1)} %pad_add_fusion.refs_0_, f32[256,256]{1,0:T(8,128)} %get-tuple-element.34.refs_1_, f32[256,256]{1,0:T(8,128)} %collective-permute-done.1.refs_2_, f32[256,256]{1,0:T(8,128)} %collective-permute-done.2.refs_3_, ...), custom_call_target="tpu_custom_call" | custom-call | flops 301989888 | bytes 3145744 | tf_op jit(solution)/shard_map/line_map/pallas_call | solution.py:43
  38.1 2.0 %collective-permute-start.10 = (f32[256,256]{1,0:T(8,128)S(1)}, f32[256,256]{1,0:T(8,128)S(1)}, u32[]{:S(2)}, u32[]{:S(2)}) collective-permute-start(f32[256,256]{1,0:T(8,128)S(1)} %get-tuple-element.41.refs_1_), channel_id=1, source_target_pairs={{0,16},{1,17},{2,18},{3,19},{4,20},{5,21},{6,22},{7,23},{8,24},{9,... | collective-permute-start | bytes 786440 | tf_op jit(solution)/shard_map/ppermute | solution.py:390
  40.1 0.9 collective-permute-start.9
  41.6 1.1 line_shift.1
  42.7 1.1 %collective-permute-start.13 = (f32[32,256]{1,0:T(8,128)S(1)}, f32[32,256]{1,0:T(8,128)S(1)}, u32[]{:S(2)}, u32[]{:S(2)}) collective-permute-start(f32[32,256]{1,0:T(8,128)S(1)} %get-tuple-element.47.refs_1_), channel_id=1, source_target_pairs={{0,16},{1,17},{2,18},{3,19},{4,20},{5,21},{6,22},{7,23},{8,24},{9,... | collective-permute-start | bytes 98312 | tf_op jit(solution)/shard_map/ppermute | solution.py:414
  43.8 1.7 %collective-permute-start.12 = (f32[32,256]{1,0:T(8,128)S(1)}, f32[32,256]{1,0:T(8,128)S(1)}, u32[]{:S(2)}, u32[]{:S(2)}) collective-permute-start(f32[32,256]{1,0:T(8,128)S(1)} %get-tuple-element.47.refs_1_), channel_id=1, source_target_pairs={{0,24},{1,25},{2,26},{3,27},{4,28},{5,29},{6,30},{7,31},{8,0},{9,1... | collective-permute-start | bytes 98312 | tf_op jit(solution)/shard_map/ppermute | solution.py:414
  45.9 6.0 %collective-permute-done.9.refs_3_ = f32[256,256]{1,0:T(8,128)S(1)} collective-permute-done((f32[256,256]{1,0:T(8,128)S(1)}, f32[256,256]{1,0:T(8,128)S(1)}, u32[]{:S(2)}, u32[]{:S(2)}) %collective-permute-start.9) | collective-permute-done | bytes 262176 | tf_op jit(solution)/shard_map/ppermute | solution.py:390
  52.0 0.7 collective-permute-done.8.refs_2_
  52.7 1.5 %group_map.1 = (f32[4,256,256]{2,1,0:T(8,128)S(1)}, f32[256,256]{1,0:T(8,128)S(1)}, bf16[256,256]{1,0:T(8,128)(2,1)S(1)}, bf16[256,256]{1,0:T(8,128)(2,1)S(1)}) custom-call(s32[4]{0:T(128)S(1)} %pad_add_fusion.refs_0_, f32[256,256]{1,0:T(8,128)S(1)} %get-tuple-element.41.refs_1_, f32[256,256]{1,0:T(8,128)S(1)} %collective-permute-done.8.refs_2_, ...), custom_call_target="tpu_custom_call" | custom-call | flops 603979776 | bytes 3670032 | tf_op jit(solution)/shard_map/group_map/pallas_call | solution.py:43
  54.3 1.3 %group_shift.1 = (f32[32,256]{1,0:T(8,128)S(1)}, f32[32,256]{1,0:T(8,128)S(1)}, f32[32,256]{1,0:T(8,128)S(1)}, f32[32,256]{1,0:T(8,128)S(1)}, f32[32,256]{1,0:T(8,128)S(1)}) custom-call(s32[4]{0:T(128)S(1)} %pad_add_fusion.refs_0_, f32[32,256]{1,0:T(8,128)S(1)} %get-tuple-element.47.refs_1_, f32[32,256]{1,0:T(8,128)S(1)} %collective-permute-done.11.refs_2_, ...), custom_call_target="tpu_custom_call" | custom-call | flops 67108864 | bytes 2228240 | tf_op jit(solution)/shard_map/group_shift/pallas_call | solution.py:43
  55.6 0.7 hop0.1.refs_5_
  56.3 0.8 collective-permute-start.14
  57.1 0.7 hop.5.refs_6_
  58.5 1.1 collective-permute-start.17
  59.6 1.7 %collective-permute-start.18 = (f32[32,256]{1,0:T(8,128)S(1)}, f32[32,256]{1,0:T(8,128)S(1)}, u32[]{:S(2)}, u32[]{:S(2)}) collective-permute-start(f32[32,256]{1,0:T(8,128)S(1)} %get-tuple-element.52), channel_id=1, source_target_pairs={{0,6},{1,7},{2,0},{3,1},{4,2},{5,3},{6,4},{7,5},{8,14},{9,15},{10,... | collective-permute-start | bytes 98312 | tf_op jit(solution)/shard_map/ppermute | solution.py:431
  61.3 1.0 collective-permute-start.19
  63.0 1.3 %collective-permute-start.16 = (f32[32,256]{1,0:T(8,128)S(1)}, f32[32,256]{1,0:T(8,128)S(1)}, u32[]{:S(2)}, u32[]{:S(2)}) collective-permute-start(f32[32,256]{1,0:T(8,128)S(1)} %hop.6.refs_7_), channel_id=1, source_target_pairs={{64,96},{65,97},{66,98},{67,99},{68,100},{69,101},{70,102},{71,103... | collective-permute-start | bytes 98312 | tf_op jit(solution)/shard_map/ppermute | solution.py:434
  64.3 1.2 %collective-permute-done.19.refs_7_.refs_8_ = f32[32,256]{1,0:T(8,128)S(1)} collective-permute-done((f32[32,256]{1,0:T(8,128)S(1)}, f32[32,256]{1,0:T(8,128)S(1)}, u32[]{:S(2)}, u32[]{:S(2)}) %collective-permute-start.19) | collective-permute-done | bytes 32800 | tf_op jit(solution)/shard_map/ppermute | solution.py:431
  65.5 2.4 %collective-permute-done.16.refs_1_ = f32[32,256]{1,0:T(8,128)S(1)} collective-permute-done((f32[32,256]{1,0:T(8,128)S(1)}, f32[32,256]{1,0:T(8,128)S(1)}, u32[]{:S(2)}, u32[]{:S(2)}) %collective-permute-start.16) | collective-permute-done | bytes 32800 | tf_op jit(solution)/shard_map/ppermute | solution.py:434
  68.7 2.4 %collective-permute-start.20 = (f32[32,256]{1,0:T(8,128)S(1)}, f32[32,256]{1,0:T(8,128)S(1)}, u32[]{:S(2)}, u32[]{:S(2)}) collective-permute-start(f32[32,256]{1,0:T(8,128)S(1)} %hop.7.refs_8_), channel_id=1, source_target_pairs={{96,128},{97,129},{98,130},{99,131},{100,132},{101,133},{102,134},... | collective-permute-start | bytes 98312 | tf_op jit(solution)/shard_map/ppermute | solution.py:434
  71.0 1.0 collective-permute-done.20.refs_1_
  73.4 0.7 hop.9.refs_10_
  74.9 0.7 last_hop.1
  75.6 7.2 %collective-permute-start.26 = (f32[32,256]{1,0:T(8,128)S(1)}, f32[32,256]{1,0:T(8,128)S(1)}, u32[]{:S(2)}, u32[]{:S(2)}) collective-permute-start(f32[32,256]{1,0:T(8,128)S(1)} %last_hop.1), channel_id=1, source_target_pairs={{0,36},{1,37},{2,38},{3,39},{4,32},{5,33},{6,34},{7,35},{8,44},{9,... | collective-permute-start | bytes 98312 | tf_op jit(solution)/shard_map/ppermute | solution.py:457
  82.8 6.2 %collective-permute-start.25 = (f32[32,256]{1,0:T(8,128)S(1)}, f32[32,256]{1,0:T(8,128)S(1)}, u32[]{:S(2)}, u32[]{:S(2)}) collective-permute-start(f32[32,256]{1,0:T(8,128)S(1)} %last_hop.1), channel_id=1, source_target_pairs={{0,38},{1,39},{2,32},{3,33},{4,34},{5,35},{6,36},{7,37},{8,46},{9,... | collective-permute-start | bytes 98312 | tf_op jit(solution)/shard_map/ppermute | solution.py:457
  89.0 3.6 %collective-permute-start.24 = (f32[32,256]{1,0:T(8,128)S(1)}, f32[32,256]{1,0:T(8,128)S(1)}, u32[]{:S(2)}, u32[]{:S(2)}) collective-permute-start(f32[32,256]{1,0:T(8,128)S(1)} %last_hop.1), channel_id=1, source_target_pairs={{0,34},{1,35},{2,36},{3,37},{4,38},{5,39},{6,32},{7,33},{8,42},{9,... | collective-permute-start | bytes 98312 | tf_op jit(solution)/shard_map/ppermute | solution.py:457
  92.6 1.9 %collective-permute-start.23 = (f32[32,256]{1,0:T(8,128)S(1)}, f32[32,256]{1,0:T(8,128)S(1)}, u32[]{:S(2)}, u32[]{:S(2)}) collective-permute-start(f32[32,256]{1,0:T(8,128)S(1)} %last_hop.1), channel_id=1, source_target_pairs={{0,32},{1,33},{2,34},{3,35},{4,36},{5,37},{6,38},{7,39},{8,40},{9,... | collective-permute-start | bytes 98312 | tf_op jit(solution)/shard_map/ppermute | solution.py:457
  94.6 1.2 %collective-permute-done.24.refs_2_ = f32[32,256]{1,0:T(8,128)S(1)} collective-permute-done((f32[32,256]{1,0:T(8,128)S(1)}, f32[32,256]{1,0:T(8,128)S(1)}, u32[]{:S(2)}, u32[]{:S(2)}) %collective-permute-start.24) | collective-permute-done | bytes 32800 | tf_op jit(solution)/shard_map/ppermute | solution.py:457
  95.8 1.5 %collective-permute-done.23.refs_1_ = f32[32,256]{1,0:T(8,128)S(1)} collective-permute-done((f32[32,256]{1,0:T(8,128)S(1)}, f32[32,256]{1,0:T(8,128)S(1)}, u32[]{:S(2)}, u32[]{:S(2)}) %collective-permute-start.23) | collective-permute-done | bytes 32800 | tf_op jit(solution)/shard_map/ppermute | solution.py:457
  97.3 1.0 chip_start.1
  98.3 8.6 %collective-permute-start.27 = (f32[128,256]{1,0:T(8,128)S(1)}, f32[128,256]{1,0:T(8,128)S(1)}, u32[]{:S(2)}, u32[]{:S(2)}) collective-permute-start(f32[128,256]{1,0:T(8,128)S(1)} %get-tuple-element.58), channel_id=1, source_target_pairs={{0,1},{1,0},{2,3},{3,2},{4,5},{5,4},{6,7},{7,6},{8,9},{9,8},{10,11... | collective-permute-start | bytes 393224 | tf_op jit(solution)/shard_map/ppermute | solution.py:472
  106.9 1.0 collective-permute-done.27.refs_2_
  107.8 1.6 %finish.1 = (f32[8,256]{1,0:T(8,128)}, f32[256,256]{1,0:T(8,128)}) custom-call(s32[4]{0:T(128)S(1)} %pad_add_fusion.refs_0_, f32[128,256]{1,0:T(8,128)S(1)} %get-tuple-element.57.refs_1_, f32[128,256]{1,0:T(8,128)S(1)} %collective-permute-done.27.refs_2_, f32[256,256]{1,0:T(8,128)S(1)} %get-tuple-element.33.refs_1_.refs_3_, ...), custom_call_target="tpu_custom_call" | custom-call | flops 100663296 | bytes 1073168 | tf_op jit(solution)/shard_map/finish/pallas_call | solution.py:43
  (43 shorter events, 7.5 us)
Async XLA Ops:
  0.6 10.0 %copy-start.1 = (f32[8,256,256]{2,1,0:T(8,128)S(1)}, f32[8,256,256]{2,1,0:T(8,128)}, u32[]{:S(2)}) copy-start(f32[8,256,256]{2,1,0:T(8,128)} %refs_3_.1) | copy-start | bytes 6291460
  0.6 10.0 %copy-start.3 = (f32[8,256]{1,0:T(8,128)S(1)}, f32[8,256]{1,0:T(8,128)}, u32[]{:S(2)}) copy-start(f32[8,256]{1,0:T(8,128)} %refs_2_.3) | copy-start | bytes 24580
  0.7 10.0 %copy-start.6 = (f32[256]{0:T(256)S(1)}, f32[256]{0:T(256)}, u32[]{:S(2)}) copy-start(f32[256]{0:T(256)} %param.11) | copy-start | bytes 3076
  2.8 20.8 %all-to-all-start = ((f32[32,8,640]{2,1,0:T(8,128)}), f32[32,8,640]{2,1,0:T(8,128)S(1)}, u32[]{:S(2)}, u32[]{:S(2)}) async-start(f32[32,8,640]{2,1,0:T(8,128)} %pack.1.refs_4_), calls=%async_computation | async-start | bytes 1310720 | tf_op jit(solution)/shard_map/all_to_all | solution.py:337
  10.7 1.1 copy-start
  14.5 7.0 %copy-start.4 = (f32[8,256]{1,0:T(8,128)}, f32[8,256]{1,0:T(8,128)S(1)}, u32[]{:S(2)}) copy-start(f32[8,256]{1,0:T(8,128)S(1)} %get-tuple-element.60.refs_5_) | copy-start | bytes 24580
  14.5 1.6 %collective-permute-start = (f32[256,256]{1,0:T(8,128)S(1)}, f32[256,256]{1,0:T(8,128)S(1)}, u32[]{:S(2)}, u32[]{:S(2)}) collective-permute-start(f32[256,256]{1,0:T(8,128)S(1)} %get-tuple-element.33.refs_1_.refs_3_), channel_id=1, source_target_pairs={{0,1},{1,0},{2,3},{3,2},{4,5},{5,4},{6,7},{7,6},{8,9},{9,8},{10,11... | collective-permute-start | bytes 786440 | tf_op jit(solution)/shard_map/ppermute | solution.py:352
  17.7 14.0 %collective-permute-start.3 = (f32[256,256]{1,0:T(8,128)}, f32[256,256]{1,0:T(8,128)}, u32[]{:S(2)}, u32[]{:S(2)}) collective-permute-start(f32[256,256]{1,0:T(8,128)} %get-tuple-element.34.refs_1_), channel_id=1, source_target_pairs={{0,4},{1,5},{2,6},{3,7},{4,0},{5,1},{6,2},{7,3},{8,12},{9,13},{10,... | collective-permute-start | bytes 786440 | tf_op jit(solution)/shard_map/ppermute | solution.py:354
  20.5 12.8 %collective-permute-start.2 = (f32[256,256]{1,0:T(8,128)}, f32[256,256]{1,0:T(8,128)}, u32[]{:S(2)}, u32[]{:S(2)}) collective-permute-start(f32[256,256]{1,0:T(8,128)} %get-tuple-element.34.refs_1_), channel_id=1, source_target_pairs={{0,6},{1,7},{2,0},{3,1},{4,2},{5,3},{6,4},{7,5},{8,14},{9,15},{10,... | collective-permute-start | bytes 786440 | tf_op jit(solution)/shard_map/ppermute | solution.py:354
  21.4 13.4 %collective-permute-start.1 = (f32[256,256]{1,0:T(8,128)}, f32[256,256]{1,0:T(8,128)}, u32[]{:S(2)}, u32[]{:S(2)}) collective-permute-start(f32[256,256]{1,0:T(8,128)} %get-tuple-element.34.refs_1_), channel_id=1, source_target_pairs={{0,2},{1,3},{2,4},{3,5},{4,6},{5,7},{6,0},{7,1},{8,10},{9,11},{10,... | collective-permute-start | bytes 786440 | tf_op jit(solution)/shard_map/ppermute | solution.py:354
  26.7 1.4 %collective-permute-start.4 = (f32[128,256]{1,0:T(8,128)S(1)}, f32[128,256]{1,0:T(8,128)S(1)}, u32[]{:S(2)}, u32[]{:S(2)}) collective-permute-start(f32[128,256]{1,0:T(8,128)S(1)} %get-tuple-element.36), channel_id=1, source_target_pairs={{0,1},{1,0},{2,3},{3,2},{4,5},{5,4},{6,7},{7,6},{8,9},{9,8},{10,11... | collective-permute-start | bytes 393224 | tf_op jit(solution)/shard_map/ppermute | solution.py:366
  28.9 6.5 %collective-permute-start.5 = (f32[32,256]{1,0:T(8,128)S(1)}, f32[32,256]{1,0:T(8,128)S(1)}, u32[]{:S(2)}, u32[]{:S(2)}) collective-permute-start(f32[32,256]{1,0:T(8,128)S(1)} %get-tuple-element.38), channel_id=1, source_target_pairs={{0,2},{1,3},{2,4},{3,5},{4,6},{5,7},{6,0},{7,1},{8,10},{9,11},{10,... | collective-permute-start | bytes 98312 | tf_op jit(solution)/shard_map/ppermute | solution.py:379
  29.0 6.4 %collective-permute-start.6 = (f32[32,256]{1,0:T(8,128)S(1)}, f32[32,256]{1,0:T(8,128)S(1)}, u32[]{:S(2)}, u32[]{:S(2)}) collective-permute-start(f32[32,256]{1,0:T(8,128)S(1)} %get-tuple-element.39), channel_id=1, source_target_pairs={{0,6},{1,7},{2,0},{3,1},{4,2},{5,3},{6,4},{7,5},{8,14},{9,15},{10,... | collective-permute-start | bytes 98312 | tf_op jit(solution)/shard_map/ppermute | solution.py:379
  31.7 4.3 %collective-permute-start.7 = (f32[32,256]{1,0:T(8,128)S(1)}, f32[32,256]{1,0:T(8,128)S(1)}, u32[]{:S(2)}, u32[]{:S(2)}) collective-permute-start(f32[32,256]{1,0:T(8,128)S(1)} %get-tuple-element.40), channel_id=1, source_target_pairs={{0,4},{1,5},{2,6},{3,7},{4,0},{5,1},{6,2},{7,3},{8,12},{9,13},{10,... | collective-permute-start | bytes 98312 | tf_op jit(solution)/shard_map/ppermute | solution.py:379
  38.1 7.5 %collective-permute-start.10 = (f32[256,256]{1,0:T(8,128)S(1)}, f32[256,256]{1,0:T(8,128)S(1)}, u32[]{:S(2)}, u32[]{:S(2)}) collective-permute-start(f32[256,256]{1,0:T(8,128)S(1)} %get-tuple-element.41.refs_1_), channel_id=1, source_target_pairs={{0,16},{1,17},{2,18},{3,19},{4,20},{5,21},{6,22},{7,23},{8,24},{9,... | collective-permute-start | bytes 786440 | tf_op jit(solution)/shard_map/ppermute | solution.py:390
  40.1 11.8 %collective-permute-start.9 = (f32[256,256]{1,0:T(8,128)S(1)}, f32[256,256]{1,0:T(8,128)S(1)}, u32[]{:S(2)}, u32[]{:S(2)}) collective-permute-start(f32[256,256]{1,0:T(8,128)S(1)} %get-tuple-element.41.refs_1_), channel_id=1, source_target_pairs={{0,24},{1,25},{2,26},{3,27},{4,28},{5,29},{6,30},{7,31},{8,0},{9,1... | collective-permute-start | bytes 786440 | tf_op jit(solution)/shard_map/ppermute | solution.py:390
  41.0 11.7 %collective-permute-start.8 = (f32[256,256]{1,0:T(8,128)S(1)}, f32[256,256]{1,0:T(8,128)S(1)}, u32[]{:S(2)}, u32[]{:S(2)}) collective-permute-start(f32[256,256]{1,0:T(8,128)S(1)} %get-tuple-element.41.refs_1_), channel_id=1, source_target_pairs={{0,8},{1,9},{2,10},{3,11},{4,12},{5,13},{6,14},{7,15},{8,16},{9,17... | collective-permute-start | bytes 786440 | tf_op jit(solution)/shard_map/ppermute | solution.py:390
  42.7 11.6 %collective-permute-start.13 = (f32[32,256]{1,0:T(8,128)S(1)}, f32[32,256]{1,0:T(8,128)S(1)}, u32[]{:S(2)}, u32[]{:S(2)}) collective-permute-start(f32[32,256]{1,0:T(8,128)S(1)} %get-tuple-element.47.refs_1_), channel_id=1, source_target_pairs={{0,16},{1,17},{2,18},{3,19},{4,20},{5,21},{6,22},{7,23},{8,24},{9,... | collective-permute-start | bytes 98312 | tf_op jit(solution)/shard_map/ppermute | solution.py:414
  43.8 10.5 %collective-permute-start.12 = (f32[32,256]{1,0:T(8,128)S(1)}, f32[32,256]{1,0:T(8,128)S(1)}, u32[]{:S(2)}, u32[]{:S(2)}) collective-permute-start(f32[32,256]{1,0:T(8,128)S(1)} %get-tuple-element.47.refs_1_), channel_id=1, source_target_pairs={{0,24},{1,25},{2,26},{3,27},{4,28},{5,29},{6,30},{7,31},{8,0},{9,1... | collective-permute-start | bytes 98312 | tf_op jit(solution)/shard_map/ppermute | solution.py:414
  45.6 8.6 %collective-permute-start.11 = (f32[32,256]{1,0:T(8,128)S(1)}, f32[32,256]{1,0:T(8,128)S(1)}, u32[]{:S(2)}, u32[]{:S(2)}) collective-permute-start(f32[32,256]{1,0:T(8,128)S(1)} %get-tuple-element.47.refs_1_), channel_id=1, source_target_pairs={{0,8},{1,9},{2,10},{3,11},{4,12},{5,13},{6,14},{7,15},{8,16},{9,17... | collective-permute-start | bytes 98312 | tf_op jit(solution)/shard_map/ppermute | solution.py:414
  52.7 2.8 %copy-start.2 = (f32[256,256]{1,0:T(8,128)S(1)}, f32[256,256]{1,0:T(8,128)}, u32[]{:S(2)}) copy-start(f32[256,256]{1,0:T(8,128)} %refs_9_.1) | copy-start | bytes 786436
  56.3 51.6 %copy-start.5 = (f32[8,256]{1,0:T(8,128)S(1)}, f32[8,256]{1,0:T(8,128)}, u32[]{:S(2)}) copy-start(f32[8,256]{1,0:T(8,128)} %copy-done.4) | copy-start | bytes 24580
  56.3 0.8 collective-permute-start.14
  57.8 4.5 %collective-permute-start.15 = (f32[32,256]{1,0:T(8,128)S(1)}, f32[32,256]{1,0:T(8,128)S(1)}, u32[]{:S(2)}, u32[]{:S(2)}) collective-permute-start(f32[32,256]{1,0:T(8,128)S(1)} %hop.5.refs_6_), channel_id=1, source_target_pairs={{32,64},{33,65},{34,66},{35,67},{36,68},{37,69},{38,70},{39,71},{4... | collective-permute-start | bytes 98312 | tf_op jit(solution)/shard_map/ppermute | solution.py:434
  58.5 5.8 %collective-permute-start.17 = (f32[32,256]{1,0:T(8,128)S(1)}, f32[32,256]{1,0:T(8,128)S(1)}, u32[]{:S(2)}, u32[]{:S(2)}) collective-permute-start(f32[32,256]{1,0:T(8,128)S(1)} %get-tuple-element.51), channel_id=1, source_target_pairs={{0,2},{1,3},{2,4},{3,5},{4,6},{5,7},{6,0},{7,1},{8,10},{9,11},{10,... | collective-permute-start | bytes 98312 | tf_op jit(solution)/shard_map/ppermute | solution.py:431
  59.6 4.7 %collective-permute-start.18 = (f32[32,256]{1,0:T(8,128)S(1)}, f32[32,256]{1,0:T(8,128)S(1)}, u32[]{:S(2)}, u32[]{:S(2)}) collective-permute-start(f32[32,256]{1,0:T(8,128)S(1)} %get-tuple-element.52), channel_id=1, source_target_pairs={{0,6},{1,7},{2,0},{3,1},{4,2},{5,3},{6,4},{7,5},{8,14},{9,15},{10,... | collective-permute-start | bytes 98312 | tf_op jit(solution)/shard_map/ppermute | solution.py:431
  61.3 4.3 %collective-permute-start.19 = (f32[32,256]{1,0:T(8,128)S(1)}, f32[32,256]{1,0:T(8,128)S(1)}, u32[]{:S(2)}, u32[]{:S(2)}) collective-permute-start(f32[32,256]{1,0:T(8,128)S(1)} %get-tuple-element.53), channel_id=1, source_target_pairs={{0,4},{1,5},{2,6},{3,7},{4,0},{5,1},{6,2},{7,3},{8,12},{9,13},{10,... | collective-permute-start | bytes 98312 | tf_op jit(solution)/shard_map/ppermute | solution.py:431
  63.0 5.0 %collective-permute-start.16 = (f32[32,256]{1,0:T(8,128)S(1)}, f32[32,256]{1,0:T(8,128)S(1)}, u32[]{:S(2)}, u32[]{:S(2)}) collective-permute-start(f32[32,256]{1,0:T(8,128)S(1)} %hop.6.refs_7_), channel_id=1, source_target_pairs={{64,96},{65,97},{66,98},{67,99},{68,100},{69,101},{70,102},{71,103... | collective-permute-start | bytes 98312 | tf_op jit(solution)/shard_map/ppermute | solution.py:434
  68.7 3.4 %collective-permute-start.20 = (f32[32,256]{1,0:T(8,128)S(1)}, f32[32,256]{1,0:T(8,128)S(1)}, u32[]{:S(2)}, u32[]{:S(2)}) collective-permute-start(f32[32,256]{1,0:T(8,128)S(1)} %hop.7.refs_8_), channel_id=1, source_target_pairs={{96,128},{97,129},{98,130},{99,131},{100,132},{101,133},{102,134},... | collective-permute-start | bytes 98312 | tf_op jit(solution)/shard_map/ppermute | solution.py:434
  72.7 0.7 collective-permute-start.21
  74.1 0.7 collective-permute-start.22
  75.6 19.0 %collective-permute-start.26 = (f32[32,256]{1,0:T(8,128)S(1)}, f32[32,256]{1,0:T(8,128)S(1)}, u32[]{:S(2)}, u32[]{:S(2)}) collective-permute-start(f32[32,256]{1,0:T(8,128)S(1)} %last_hop.1), channel_id=1, source_target_pairs={{0,36},{1,37},{2,38},{3,39},{4,32},{5,33},{6,34},{7,35},{8,44},{9,... | collective-permute-start | bytes 98312 | tf_op jit(solution)/shard_map/ppermute | solution.py:457
  82.8 11.8 %collective-permute-start.25 = (f32[32,256]{1,0:T(8,128)S(1)}, f32[32,256]{1,0:T(8,128)S(1)}, u32[]{:S(2)}, u32[]{:S(2)}) collective-permute-start(f32[32,256]{1,0:T(8,128)S(1)} %last_hop.1), channel_id=1, source_target_pairs={{0,38},{1,39},{2,32},{3,33},{4,34},{5,35},{6,36},{7,37},{8,46},{9,... | collective-permute-start | bytes 98312 | tf_op jit(solution)/shard_map/ppermute | solution.py:457
  89.0 6.8 %collective-permute-start.24 = (f32[32,256]{1,0:T(8,128)S(1)}, f32[32,256]{1,0:T(8,128)S(1)}, u32[]{:S(2)}, u32[]{:S(2)}) collective-permute-start(f32[32,256]{1,0:T(8,128)S(1)} %last_hop.1), channel_id=1, source_target_pairs={{0,34},{1,35},{2,36},{3,37},{4,38},{5,39},{6,32},{7,33},{8,42},{9,... | collective-permute-start | bytes 98312 | tf_op jit(solution)/shard_map/ppermute | solution.py:457
  92.6 4.7 %collective-permute-start.23 = (f32[32,256]{1,0:T(8,128)S(1)}, f32[32,256]{1,0:T(8,128)S(1)}, u32[]{:S(2)}, u32[]{:S(2)}) collective-permute-start(f32[32,256]{1,0:T(8,128)S(1)} %last_hop.1), channel_id=1, source_target_pairs={{0,32},{1,33},{2,34},{3,35},{4,36},{5,37},{6,38},{7,39},{8,40},{9,... | collective-permute-start | bytes 98312 | tf_op jit(solution)/shard_map/ppermute | solution.py:457
  98.3 9.6 %collective-permute-start.27 = (f32[128,256]{1,0:T(8,128)S(1)}, f32[128,256]{1,0:T(8,128)S(1)}, u32[]{:S(2)}, u32[]{:S(2)}) collective-permute-start(f32[128,256]{1,0:T(8,128)S(1)} %get-tuple-element.58), channel_id=1, source_target_pairs={{0,1},{1,0},{2,3},{3,2},{4,5},{5,4},{6,7},{7,6},{8,9},{9,8},{10,11... | collective-permute-start | bytes 393224 | tf_op jit(solution)/shard_map/ppermute | solution.py:472

commit v5 on v3

--- a/solution.py
+++ b/solution.py
@@ -27,23 +27,31 @@
 def mm(left, right, transposed=False):
     ah, al = left
     bh, bl = right
+    rows = ah.shape[0]
+    if rows % 16 == 0 and rows <= 64:
+        both = dot(jnp.concatenate([ah, al], axis=0), bh, transposed)
+        return both[:rows] + (dot(ah, bl, transposed) + both[rows:])
     return dot(ah, bh, transposed) + (dot(ah, bl, transposed) + dot(al, bh, transposed))
+
+
+def place():
+    t = lax.axis_index("tm")
+    return lax.rem(t, 2), lax.rem(t // 2, NY), t // (2 * NY), lax.axis_index("grp")
 
 
 def call(kernel, name, outs, *args, scratch=(), flops=0, after=()):
     shapes = [s if hasattr(s, "dtype") else jax.ShapeDtypeStruct(s, F32) for s in outs]
-    smem = pl.BlockSpec(memory_space=pltpu.SMEM)
     vmem = pl.BlockSpec(memory_space=pltpu.VMEM)
     moved = sum(4 * a.size for a in args) + sum(4 * s.size for s in shapes)
     n_args, n_after = len(args), len(after)
 
     def run(*refs):
-        kernel(*refs[:n_args], *refs[n_args + n_after :])
+        kernel(place(), *refs[:n_args], *refs[n_args + n_after :])
 
     return pl.pallas_call(
         run,
         out_shape=shapes,
-        in_specs=[smem] + [vmem] * (n_args - 1) + [pl.BlockSpec(memory_space=pl.ANY)] * n_after,
+        in_specs=[vmem] * n_args + [pl.BlockSpec(memory_space=pl.ANY)] * n_after,
         out_specs=[vmem] * len(shapes),
         scratch_shapes=list(scratch),
         name=name,
@@ -296,10 +304,6 @@
     mat = (modes, modes)
     vm = lambda *s: pltpu.VMEM(s, F32)
 
-    t = lax.axis_index("tm")
-    g = lax.axis_index("grp")
-    pos = jnp.stack([t % 2, (t // 2) % NY, t // (2 * NY), g]).astype(jnp.int32)
-
     def at(x, y, c):
         return (x * NY + y) * 2 + c
 
@@ -336,7 +340,6 @@
         compose_kernel,
         "compose",
         [mat, (steps, modes)],
-        pos,
         retain,
         coupling,
         probe_row,
@@ -344,13 +347,12 @@
         after=(packed,),
     )
     other = lax.ppermute(whole, "tm", swap)
-    both, chip = call(pair_kernel, "pair_map", [(2,) + mat, mat], pos, whole, other, flops=3 * cube)
+    both, chip = call(pair_kernel, "pair_map", [(2,) + mat, mat], whole, other, flops=3 * cube)
     chips = [lax.ppermute(chip, "tm", along_y(s)) for s in SHIFTS]
     shifted, kept, sent, driven = call(
         drive_kernel,
         "drive",
         [mat, (half, modes), (half, modes), (steps, samples)],
-        pos,
         arrived,
         retain,
         coupling,
@@ -363,7 +365,6 @@
         pair_shift_kernel,
         "pair_shift",
         [(half, modes)] + [small] * 4,
-        pos,
         kept,
         back,
         both,
@@ -375,7 +376,6 @@
         line_map_kernel,
         "line_map",
         [(NY,) + mat, (NY - 1,) + mat, mat],
-        pos,
         chip,
         *chips,
         flops=9 * cube,
@@ -387,7 +387,6 @@
         group_map_kernel,
         "group_map",
         [(NX,) + mat, (NY,) + mat, half_mat, half_mat],
-        pos,
         line,
         *lines,
         y_before,
@@ -398,7 +397,6 @@
         line_shift_kernel,
         "line_shift",
         [(NY - 1,) + small, small],
-        pos,
         rows[0],
         *got,
         y_maps,
@@ -410,7 +408,6 @@
         group_shift_kernel,
         "group_shift",
         [(NY,) + small, small],
-        pos,
         b_line,
         *got,
         x_maps,
@@ -420,17 +417,16 @@
         flops=2 * cube,
     )
     (e,) = call(
-        first_hop_kernel, "hop0", [small], pos, initial_state, high, low, b_group, flops=cube
+        first_hop_kernel, "hop0", [small], initial_state, high, low, b_group, flops=cube
     )
     carried = [lax.ppermute(e, "grp", [(0, 1)])]
     for k in range(1, n_grp - 1):
-        (e,) = call(hop_kernel, "hop", [small], pos, carried[-1], high, low, b_group, flops=cube)
+        (e,) = call(hop_kernel, "hop", [small], carried[-1], high, low, b_group, flops=cube)
         carried.append(lax.ppermute(e, "grp", [(k, k + 1)]))
     rows = call(
         last_hop_kernel,
         "chips",
         [small] * 4,
-        pos,
         initial_state,
         *carried,
         through,
@@ -443,7 +439,6 @@
         chip_kernel,
         "chip_start",
         [(half, modes)] * 2,
-        pos,
         rows[0],
         *got,
         both,
@@ -456,7 +451,6 @@
         finish_kernel,
         "finish",
         [(steps, samples), mat],
-        pos,
         kept,
         back,
         whole,

time: 105 us -> 97.4 us (0.928)
  Pallas kernels: 24.8 us -> 15.3 us
  waiting for transfers between devices: 36.3 us -> 40.4 us
  starting transfers between devices: 41.2 us -> 38.6 us
    pallas_call x18, Pallas kernels: 22.7 us -> 13.2 us  [call(): pl.pallas_call(run, out_shape=shapes, in_specs=[vmem] * n_args + [pl.Bloc...]
    ppermute x3, waiting for transfers between devices: 6.88 us -> 9.28 us  [body(): lines = [lax.ppermute(line, 'tm', along_x(s)) for s in SHIFTS]]
    all_to_all x1, waiting for transfers between devices: 1.54 us -> 2.72 us  [body(): arrived = lax.all_to_all(packed, 'tm', split_axis=0, concat_axis=0)]
  transfers between devices with their start and end apart: 26 -> 26, of which waited for: 14 -> 14; matrix products, arithmetic and copies ran while one was open for 0% -> 0% of each run, Pallas kernels for 11% -> 8%
where the time goes in v5:
time: 97.4 us; the launch traced here: 97 us
  waiting for transfers between devices  40.4 us (41%)
  starting transfers between devices  38.6 us (40%)
  Pallas kernels  15.3 us (16%)
  local copies, waits for them, and re-layouts  1.81 us (2%)
  between operations  0.98 us (1%)
    ppermute x6, waiting for transfers between devices, body(): carried.append(lax.ppermute(e, 'grp', [(k, k + 1)]))  16.4 us
    pallas_call x18, Pallas kernels, call(): pl.pallas_call(run, out_shape=shapes, in_specs=[vmem] * n_args + [pl.Bloc...  13.2 us
    ppermute x2, starting transfers between devices, body(): back = lax.ppermute(sent, 'tm', swap)  9.89 us
    ppermute x3, waiting for transfers between devices, body(): lines = [lax.ppermute(line, 'tm', along_x(s)) for s in SHIFTS]  9.28 us
    all_to_all x1, starting transfers between devices, body(): arrived = lax.all_to_all(packed, 'tm', split_axis=0, concat_axis=0)  7.77 us
    ppermute x6, starting transfers between devices, body(): got = [lax.ppermute(r, 'tm', along_y(s)) for r, s in zip(rows[1:], SHIFTS)]  5.7 us
    ppermute x6, waiting for transfers between devices, body(): got = [lax.ppermute(r, 'tm', along_y(s)) for r, s in zip(rows[1:], SHIFTS)]  5.21 us
    ppermute x6, starting transfers between devices, body(): carried.append(lax.ppermute(e, 'grp', [(k, k + 1)]))  4.61 us
  transfers between devices with their start and end apart: 26, of which 14 were waited for; matrix products, arithmetic and copies ran while one was open for 0% of the time, Pallas kernels for 8%

profile of v5, /device:TPU:225, one launch (start us, length us, event | category | flops | bytes accessed | tf_op | source)
XLA Modules:
  0.0 97.0 jit_solution(17833315141479410779)
XLA Ops:
  0.7 2.1 %pack.1.refs_3_ = f32[32,8,640]{2,1,0:T(8,128)} custom-call(f32[32,16,256]{2,1,0:T(8,128)} %bitcast.11, s32[16,32]{1,0:T(8,128)} %bitcast.12, s32[16,32]{1,0:T(8,128)} %bitcast.13, s32[1,32]{1,0:T(1,128)} %counts.1), custom_call_target="tpu_custom_call" | custom-call | bytes 1048576 | tf_op jit(solution)/shard_map/pack/pallas_call | solution.py:321
  2.8 7.8 %all-to-all-start = ((f32[32,8,640]{2,1,0:T(8,128)}), f32[32,8,640]{2,1,0:T(8,128)S(1)}, u32[]{:S(2)}, u32[]{:S(2)}) async-start(f32[32,8,640]{2,1,0:T(8,128)} %pack.1.refs_3_), calls=%async_computation | async-start | bytes 1310720 | tf_op jit(solution)/shard_map/all_to_all | solution.py:335
  10.6 1.1 %copy-done = f32[32,8,640]{2,1,0:T(8,128)S(1)} copy-done((f32[32,8,640]{2,1,0:T(8,128)S(1)}, f32[32,8,640]{2,1,0:T(8,128)}, u32[]{:S(2)}) %copy-start) | copy-done | bytes 655384
  11.7 2.1 %compose.1 = (f32[256,256]{1,0:T(8,128)S(1)}, f32[8,256]{1,0:T(8,128)S(1)}) custom-call(f32[8,256]{1,0:T(8,128)S(1)} %copy-done.3, f32[8,256,256]{2,1,0:T(8,128)S(1)} %copy-done.1, f32[1,256]{1,0:T(1,128)S(1)} %bitcast.9, f32[32,8,640]{2,1,0:T(8,128)S(1)} %copy-done), custom_call_target="tpu_custom_call" | custom-call | flops 738197504 | bytes 2376704 | tf_op jit(solution)/shard_map/compose/pallas_call | solution.py:51
  13.8 0.3 collective-permute-start
  14.2 1.3 %collective-permute-done.refs_1_ = f32[256,256]{1,0:T(8,128)S(1)} collective-permute-done((f32[256,256]{1,0:T(8,128)S(1)}, f32[256,256]{1,0:T(8,128)S(1)}, u32[]{:S(2)}, u32[]{:S(2)}) %collective-permute-start) | collective-permute-done | bytes 262176 | tf_op jit(solution)/shard_map/ppermute | solution.py:349
  15.5 1.0 %pair_map.1 = (f32[2,256,256]{2,1,0:T(8,128)S(1)}, f32[256,256]{1,0:T(8,128)}) custom-call(f32[256,256]{1,0:T(8,128)S(1)} %get-tuple-element.34.refs_0_.refs_2_, f32[256,256]{1,0:T(8,128)S(1)} %collective-permute-done.refs_1_), custom_call_target="tpu_custom_call" | custom-call | flops 100663296 | bytes 1310720 | tf_op jit(solution)/shard_map/pair_map/pallas_call | solution.py:51
  16.5 2.9 %collective-permute-start.3 = (f32[256,256]{1,0:T(8,128)}, f32[256,256]{1,0:T(8,128)}, u32[]{:S(2)}, u32[]{:S(2)}) collective-permute-start(f32[256,256]{1,0:T(8,128)} %get-tuple-element.35.refs_0_), channel_id=1, source_target_pairs={{0,4},{1,5},{2,6},{3,7},{4,0},{5,1},{6,2},{7,3},{8,12},{9,13},{10,... | collective-permute-start | bytes 786440 | tf_op jit(solution)/shard_map/ppermute | solution.py:351
  19.4 0.9 collective-permute-start.2
  20.3 0.6 collective-permute-start.1
  20.8 2.7 %all-to-all-done.refs_0_ = f32[32,8,640]{2,1,0:T(8,128)S(1)} async-done(((f32[32,8,640]{2,1,0:T(8,128)}), f32[32,8,640]{2,1,0:T(8,128)S(1)}, u32[]{:S(2)}, u32[]{:S(2)}) %all-to-all-start) | async-done | bytes 655392 | tf_op jit(solution)/shard_map/all_to_all | solution.py:335
  23.6 0.7 copy-done.5
  24.2 2.6 %drive.1 = (f32[256,256]{1,0:T(8,128)S(1)}, f32[128,256]{1,0:T(8,128)S(1)}, f32[128,256]{1,0:T(8,128)S(1)}, f32[8,256]{1,0:T(8,128)S(1)}) custom-call(f32[32,8,640]{2,1,0:T(8,128)S(1)} %all-to-all-done.refs_0_, f32[8,256]{1,0:T(8,128)S(1)} %copy-done.3, f32[8,256,256]{2,1,0:T(8,128)S(1)} %copy-done.1, f32[1,256]{1,0:T(1,128)S(1)} %bitcast.10), custom_call_target="tpu_custom_call" | custom-call | flops 2013265920 | bytes 3294208 | tf_op jit(solution)/shard_map/drive/pallas_call | solution.py:51
  26.9 1.3 %collective-permute-done.4.refs_1_ = f32[128,256]{1,0:T(8,128)S(1)} collective-permute-done((f32[128,256]{1,0:T(8,128)S(1)}, f32[128,256]{1,0:T(8,128)S(1)}, u32[]{:S(2)}, u32[]{:S(2)}) %collective-permute-start.4) | collective-permute-done | bytes 131104 | tf_op jit(solution)/shard_map/ppermute | solution.py:362
  28.3 0.2 pair_shift.1
  28.6 2.7 %collective-permute-start.6 = (f32[32,256]{1,0:T(8,128)S(1)}, f32[32,256]{1,0:T(8,128)S(1)}, u32[]{:S(2)}, u32[]{:S(2)}) collective-permute-start(f32[32,256]{1,0:T(8,128)S(1)} %get-tuple-element.40), channel_id=1, source_target_pairs={{0,6},{1,7},{2,0},{3,1},{4,2},{5,3},{6,4},{7,5},{8,14},{9,15},{10,... | collective-permute-start | bytes 98312 | tf_op jit(solution)/shard_map/ppermute | solution.py:374
  31.3 1.3 %collective-permute-done.2.refs_2_ = f32[256,256]{1,0:T(8,128)} collective-permute-done((f32[256,256]{1,0:T(8,128)}, f32[256,256]{1,0:T(8,128)}, u32[]{:S(2)}, u32[]{:S(2)}) %collective-permute-start.2) | collective-permute-done | bytes 262176 | tf_op jit(solution)/shard_map/ppermute | solution.py:351
  32.6 1.9 %collective-permute-done.1.refs_1_ = f32[256,256]{1,0:T(8,128)} collective-permute-done((f32[256,256]{1,0:T(8,128)}, f32[256,256]{1,0:T(8,128)}, u32[]{:S(2)}, u32[]{:S(2)}) %collective-permute-start.1) | collective-permute-done | bytes 262176 | tf_op jit(solution)/shard_map/ppermute | solution.py:351
  34.4 0.6 collective-permute-done.5.refs_4_.refs_1_
  35.0 0.5 collective-permute-done.7.refs_6_.refs_3_
  35.5 2.1 %line_map.1 = (f32[4,256,256]{2,1,0:T(8,128)S(1)}, f32[3,256,256]{2,1,0:T(8,128)S(1)}, f32[256,256]{1,0:T(8,128)S(1)}) custom-call(f32[256,256]{1,0:T(8,128)} %get-tuple-element.35.refs_0_, f32[256,256]{1,0:T(8,128)} %collective-permute-done.1.refs_1_, f32[256,256]{1,0:T(8,128)} %collective-permute-done.2.refs_2_, ...), custom_call_target="tpu_custom_call" | custom-call | flops 301989888 | bytes 3145728 | tf_op jit(solution)/shard_map/line_map/pallas_call | solution.py:51
  37.7 1.3 %collective-permute-start.10 = (f32[256,256]{1,0:T(8,128)S(1)}, f32[256,256]{1,0:T(8,128)S(1)}, u32[]{:S(2)}, u32[]{:S(2)}) collective-permute-start(f32[256,256]{1,0:T(8,128)S(1)} %get-tuple-element.42.refs_0_), channel_id=1, source_target_pairs={{0,16},{1,17},{2,18},{3,19},{4,20},{5,21},{6,22},{7,23},{8,24},{9,... | collective-permute-start | bytes 786440 | tf_op jit(solution)/shard_map/ppermute | solution.py:384
  38.9 1.1 %collective-permute-start.9 = (f32[256,256]{1,0:T(8,128)S(1)}, f32[256,256]{1,0:T(8,128)S(1)}, u32[]{:S(2)}, u32[]{:S(2)}) collective-permute-start(f32[256,256]{1,0:T(8,128)S(1)} %get-tuple-element.42.refs_0_), channel_id=1, source_target_pairs={{0,24},{1,25},{2,26},{3,27},{4,28},{5,29},{6,30},{7,31},{8,0},{9,1... | collective-permute-start | bytes 786440 | tf_op jit(solution)/shard_map/ppermute | solution.py:384
  40.0 0.4 collective-permute-start.8
  40.4 0.5 line_shift.1
  40.8 1.8 %collective-permute-start.13 = (f32[32,256]{1,0:T(8,128)S(1)}, f32[32,256]{1,0:T(8,128)S(1)}, u32[]{:S(2)}, u32[]{:S(2)}) collective-permute-start(f32[32,256]{1,0:T(8,128)S(1)} %get-tuple-element.48.refs_0_), channel_id=1, source_target_pairs={{0,16},{1,17},{2,18},{3,19},{4,20},{5,21},{6,22},{7,23},{8,24},{9,... | collective-permute-start | bytes 98312 | tf_op jit(solution)/shard_map/ppermute | solution.py:406
  42.7 0.7 collective-permute-start.12
  43.4 1.8 %collective-permute-done.10.refs_3_ = f32[256,256]{1,0:T(8,128)S(1)} collective-permute-done((f32[256,256]{1,0:T(8,128)S(1)}, f32[256,256]{1,0:T(8,128)S(1)}, u32[]{:S(2)}, u32[]{:S(2)}) %collective-permute-start.10) | collective-permute-done | bytes 262176 | tf_op jit(solution)/shard_map/ppermute | solution.py:384
  45.2 5.2 %collective-permute-done.9.refs_2_ = f32[256,256]{1,0:T(8,128)S(1)} collective-permute-done((f32[256,256]{1,0:T(8,128)S(1)}, f32[256,256]{1,0:T(8,128)S(1)}, u32[]{:S(2)}, u32[]{:S(2)}) %collective-permute-start.9) | collective-permute-done | bytes 262176 | tf_op jit(solution)/shard_map/ppermute | solution.py:384
  50.4 2.2 %collective-permute-done.8.refs_1_ = f32[256,256]{1,0:T(8,128)S(1)} collective-permute-done((f32[256,256]{1,0:T(8,128)S(1)}, f32[256,256]{1,0:T(8,128)S(1)}, u32[]{:S(2)}, u32[]{:S(2)}) %collective-permute-start.8) | collective-permute-done | bytes 262176 | tf_op jit(solution)/shard_map/ppermute | solution.py:384
  52.7 1.3 %group_map.1 = (f32[4,256,256]{2,1,0:T(8,128)S(1)}, f32[4,256,256]{2,1,0:T(8,128)S(1)}, bf16[256,256]{1,0:T(8,128)(2,1)S(1)}, bf16[256,256]{1,0:T(8,128)(2,1)S(1)}) custom-call(f32[256,256]{1,0:T(8,128)S(1)} %get-tuple-element.42.refs_0_, f32[256,256]{1,0:T(8,128)S(1)} %collective-permute-done.8.refs_1_, f32[256,256]{1,0:T(8,128)S(1)} %collective-permute-done.9.refs_2_, ...), custom_call_target="tpu_custom_call" | custom-call | flops 603979776 | bytes 4456448 | tf_op jit(solution)/shard_map/group_map/pallas_call | solution.py:51
  54.0 0.6 group_shift.1
  54.8 0.7 collective-permute-start.14
  55.6 0.7 collective-permute-start.15
  56.5 0.7 collective-permute-start.16
  57.3 0.7 collective-permute-start.17
  58.2 0.7 collective-permute-start.18
  59.0 0.7 collective-permute-start.19
  59.9 1.3 %collective-permute-start.20 = (f32[32,256]{1,0:T(8,128)S(1)}, f32[32,256]{1,0:T(8,128)S(1)}, u32[]{:S(2)}, u32[]{:S(2)}) collective-permute-start(f32[32,256]{1,0:T(8,128)S(1)} %hop.11), channel_id=1, source_target_pairs={{192,224},{193,225},{194,226},{195,227},{196,228},{197,229},{198,2... | collective-permute-start | bytes 98312 | tf_op jit(solution)/shard_map/ppermute | solution.py:425
  61.2 16.4 %collective-permute-done.20.refs_7_ = f32[32,256]{1,0:T(8,128)S(1)} collective-permute-done((f32[32,256]{1,0:T(8,128)S(1)}, f32[32,256]{1,0:T(8,128)S(1)}, u32[]{:S(2)}, u32[]{:S(2)}) %collective-permute-start.20) | collective-permute-done | bytes 32800 | tf_op jit(solution)/shard_map/ppermute | solution.py:425
  77.6 0.3 chips.1
  77.9 1.1 %collective-permute-start.21 = (f32[32,256]{1,0:T(8,128)S(1)}, f32[32,256]{1,0:T(8,128)S(1)}, u32[]{:S(2)}, u32[]{:S(2)}) collective-permute-start(f32[32,256]{1,0:T(8,128)S(1)} %get-tuple-element.55), channel_id=1, source_target_pairs={{0,2},{1,3},{2,4},{3,5},{4,6},{5,7},{6,0},{7,1},{8,10},{9,11},{10,... | collective-permute-start | bytes 98312 | tf_op jit(solution)/shard_map/ppermute | solution.py:437
  79.0 1.7 %collective-permute-start.22 = (f32[32,256]{1,0:T(8,128)S(1)}, f32[32,256]{1,0:T(8,128)S(1)}, u32[]{:S(2)}, u32[]{:S(2)}) collective-permute-start(f32[32,256]{1,0:T(8,128)S(1)} %get-tuple-element.56), channel_id=1, source_target_pairs={{0,6},{1,7},{2,0},{3,1},{4,2},{5,3},{6,4},{7,5},{8,14},{9,15},{10,... | collective-permute-start | bytes 98312 | tf_op jit(solution)/shard_map/ppermute | solution.py:437
  80.9 1.1 %collective-permute-done.21.refs_1_ = f32[32,256]{1,0:T(8,128)S(1)} collective-permute-done((f32[32,256]{1,0:T(8,128)S(1)}, f32[32,256]{1,0:T(8,128)S(1)}, u32[]{:S(2)}, u32[]{:S(2)}) %collective-permute-start.21) | collective-permute-done | bytes 32800 | tf_op jit(solution)/shard_map/ppermute | solution.py:437
  82.0 3.0 %collective-permute-done.23.refs_3_ = f32[32,256]{1,0:T(8,128)S(1)} collective-permute-done((f32[32,256]{1,0:T(8,128)S(1)}, f32[32,256]{1,0:T(8,128)S(1)}, u32[]{:S(2)}, u32[]{:S(2)}) %collective-permute-start.23) | collective-permute-done | bytes 32800 | tf_op jit(solution)/shard_map/ppermute | solution.py:437
  85.2 9.8 %collective-permute-start.24 = (f32[128,256]{1,0:T(8,128)S(1)}, f32[128,256]{1,0:T(8,128)S(1)}, u32[]{:S(2)}, u32[]{:S(2)}) collective-permute-start(f32[128,256]{1,0:T(8,128)S(1)} %get-tuple-element.60), channel_id=1, source_target_pairs={{0,1},{1,0},{2,3},{3,2},{4,5},{5,4},{6,7},{7,6},{8,9},{9,8},{10,11... | collective-permute-start | bytes 393224 | tf_op jit(solution)/shard_map/ppermute | solution.py:449
  95.0 1.0 %collective-permute-done.24.refs_1_ = f32[128,256]{1,0:T(8,128)S(1)} collective-permute-done((f32[128,256]{1,0:T(8,128)S(1)}, f32[128,256]{1,0:T(8,128)S(1)}, u32[]{:S(2)}, u32[]{:S(2)}) %collective-permute-start.24) | collective-permute-done | bytes 131104 | tf_op jit(solution)/shard_map/ppermute | solution.py:449
  95.9 1.1 %finish.1 = (f32[8,256]{1,0:T(8,128)}, f32[256,256]{1,0:T(8,128)}) custom-call(f32[128,256]{1,0:T(8,128)S(1)} %get-tuple-element.59.refs_0_, f32[128,256]{1,0:T(8,128)S(1)} %collective-permute-done.24.refs_1_, f32[256,256]{1,0:T(8,128)S(1)} %get-tuple-element.34.refs_0_.refs_2_, f32[256,256]{1,0:T(8,128)S(1)} %get-tuple-element.61.refs_3_, ...), custom_call_target="tpu_custom_call" | custom-call | flops 100663296 | bytes 1073152 | tf_op jit(solution)/shard_map/finish/pallas_call | solution.py:51
  (35 shorter events, 1.8 us)
Async XLA Ops:
  0.6 9.9 %copy-start.1 = (f32[8,256,256]{2,1,0:T(8,128)S(1)}, f32[8,256,256]{2,1,0:T(8,128)}, u32[]{:S(2)}) copy-start(f32[8,256,256]{2,1,0:T(8,128)} %refs_2_.1) | copy-start | bytes 6291460
  0.6 9.9 %copy-start.3 = (f32[8,256]{1,0:T(8,128)S(1)}, f32[8,256]{1,0:T(8,128)}, u32[]{:S(2)}) copy-start(f32[8,256]{1,0:T(8,128)} %refs_1_.3) | copy-start | bytes 24580
  0.7 9.9 %copy-start.4 = (f32[256]{0:T(256)S(1)}, f32[256]{0:T(256)}, u32[]{:S(2)}) copy-start(f32[256]{0:T(256)} %param.11) | copy-start | bytes 3076
  2.8 20.8 %all-to-all-start = ((f32[32,8,640]{2,1,0:T(8,128)}), f32[32,8,640]{2,1,0:T(8,128)S(1)}, u32[]{:S(2)}, u32[]{:S(2)}) async-start(f32[32,8,640]{2,1,0:T(8,128)} %pack.1.refs_3_), calls=%async_computation | async-start | bytes 1310720 | tf_op jit(solution)/shard_map/all_to_all | solution.py:335
  10.6 1.1 %copy-start = (f32[32,8,640]{2,1,0:T(8,128)S(1)}, f32[32,8,640]{2,1,0:T(8,128)}, u32[]{:S(2)}) copy-start(f32[32,8,640]{2,1,0:T(8,128)} %pack.1.refs_3_) | copy-start | bytes 1966084
  13.8 1.6 %collective-permute-start = (f32[256,256]{1,0:T(8,128)S(1)}, f32[256,256]{1,0:T(8,128)S(1)}, u32[]{:S(2)}, u32[]{:S(2)}) collective-permute-start(f32[256,256]{1,0:T(8,128)S(1)} %get-tuple-element.34.refs_0_.refs_2_), channel_id=1, source_target_pairs={{0,1},{1,0},{2,3},{3,2},{4,5},{5,4},{6,7},{7,6},{8,9},{9,8},{10,11... | collective-permute-start | bytes 786440 | tf_op jit(solution)/shard_map/ppermute | solution.py:349
  16.5 14.8 %collective-permute-start.3 = (f32[256,256]{1,0:T(8,128)}, f32[256,256]{1,0:T(8,128)}, u32[]{:S(2)}, u32[]{:S(2)}) collective-permute-start(f32[256,256]{1,0:T(8,128)} %get-tuple-element.35.refs_0_), channel_id=1, source_target_pairs={{0,4},{1,5},{2,6},{3,7},{4,0},{5,1},{6,2},{7,3},{8,12},{9,13},{10,... | collective-permute-start | bytes 786440 | tf_op jit(solution)/shard_map/ppermute | solution.py:351
  19.4 13.2 %collective-permute-start.2 = (f32[256,256]{1,0:T(8,128)}, f32[256,256]{1,0:T(8,128)}, u32[]{:S(2)}, u32[]{:S(2)}) collective-permute-start(f32[256,256]{1,0:T(8,128)} %get-tuple-element.35.refs_0_), channel_id=1, source_target_pairs={{0,6},{1,7},{2,0},{3,1},{4,2},{5,3},{6,4},{7,5},{8,14},{9,15},{10,... | collective-permute-start | bytes 786440 | tf_op jit(solution)/shard_map/ppermute | solution.py:351
  20.3 14.2 %collective-permute-start.1 = (f32[256,256]{1,0:T(8,128)}, f32[256,256]{1,0:T(8,128)}, u32[]{:S(2)}, u32[]{:S(2)}) collective-permute-start(f32[256,256]{1,0:T(8,128)} %get-tuple-element.35.refs_0_), channel_id=1, source_target_pairs={{0,2},{1,3},{2,4},{3,5},{4,6},{5,7},{6,0},{7,1},{8,10},{9,11},{10,... | collective-permute-start | bytes 786440 | tf_op jit(solution)/shard_map/ppermute | solution.py:351
  23.6 0.7 copy-start.5
  26.8 1.4 %collective-permute-start.4 = (f32[128,256]{1,0:T(8,128)S(1)}, f32[128,256]{1,0:T(8,128)S(1)}, u32[]{:S(2)}, u32[]{:S(2)}) collective-permute-start(f32[128,256]{1,0:T(8,128)S(1)} %get-tuple-element.37), channel_id=1, source_target_pairs={{0,1},{1,0},{2,3},{3,2},{4,5},{5,4},{6,7},{7,6},{8,9},{9,8},{10,11... | collective-permute-start | bytes 393224 | tf_op jit(solution)/shard_map/ppermute | solution.py:362
  28.5 6.5 %collective-permute-start.5 = (f32[32,256]{1,0:T(8,128)S(1)}, f32[32,256]{1,0:T(8,128)S(1)}, u32[]{:S(2)}, u32[]{:S(2)}) collective-permute-start(f32[32,256]{1,0:T(8,128)S(1)} %get-tuple-element.39), channel_id=1, source_target_pairs={{0,2},{1,3},{2,4},{3,5},{4,6},{5,7},{6,0},{7,1},{8,10},{9,11},{10,... | collective-permute-start | bytes 98312 | tf_op jit(solution)/shard_map/ppermute | solution.py:374
  28.6 6.4 %collective-permute-start.6 = (f32[32,256]{1,0:T(8,128)S(1)}, f32[32,256]{1,0:T(8,128)S(1)}, u32[]{:S(2)}, u32[]{:S(2)}) collective-permute-start(f32[32,256]{1,0:T(8,128)S(1)} %get-tuple-element.40), channel_id=1, source_target_pairs={{0,6},{1,7},{2,0},{3,1},{4,2},{5,3},{6,4},{7,5},{8,14},{9,15},{10,... | collective-permute-start | bytes 98312 | tf_op jit(solution)/shard_map/ppermute | solution.py:374
  31.3 4.3 %collective-permute-start.7 = (f32[32,256]{1,0:T(8,128)S(1)}, f32[32,256]{1,0:T(8,128)S(1)}, u32[]{:S(2)}, u32[]{:S(2)}) collective-permute-start(f32[32,256]{1,0:T(8,128)S(1)} %get-tuple-element.41), channel_id=1, source_target_pairs={{0,4},{1,5},{2,6},{3,7},{4,0},{5,1},{6,2},{7,3},{8,12},{9,13},{10,... | collective-permute-start | bytes 98312 | tf_op jit(solution)/shard_map/ppermute | solution.py:374
  37.7 7.5 %collective-permute-start.10 = (f32[256,256]{1,0:T(8,128)S(1)}, f32[256,256]{1,0:T(8,128)S(1)}, u32[]{:S(2)}, u32[]{:S(2)}) collective-permute-start(f32[256,256]{1,0:T(8,128)S(1)} %get-tuple-element.42.refs_0_), channel_id=1, source_target_pairs={{0,16},{1,17},{2,18},{3,19},{4,20},{5,21},{6,22},{7,23},{8,24},{9,... | collective-permute-start | bytes 786440 | tf_op jit(solution)/shard_map/ppermute | solution.py:384
  38.9 11.5 %collective-permute-start.9 = (f32[256,256]{1,0:T(8,128)S(1)}, f32[256,256]{1,0:T(8,128)S(1)}, u32[]{:S(2)}, u32[]{:S(2)}) collective-permute-start(f32[256,256]{1,0:T(8,128)S(1)} %get-tuple-element.42.refs_0_), channel_id=1, source_target_pairs={{0,24},{1,25},{2,26},{3,27},{4,28},{5,29},{6,30},{7,31},{8,0},{9,1... | collective-permute-start | bytes 786440 | tf_op jit(solution)/shard_map/ppermute | solution.py:384
  40.0 12.6 %collective-permute-start.8 = (f32[256,256]{1,0:T(8,128)S(1)}, f32[256,256]{1,0:T(8,128)S(1)}, u32[]{:S(2)}, u32[]{:S(2)}) collective-permute-start(f32[256,256]{1,0:T(8,128)S(1)} %get-tuple-element.42.refs_0_), channel_id=1, source_target_pairs={{0,8},{1,9},{2,10},{3,11},{4,12},{5,13},{6,14},{7,15},{8,16},{9,17... | collective-permute-start | bytes 786440 | tf_op jit(solution)/shard_map/ppermute | solution.py:384
  40.8 13.1 %collective-permute-start.13 = (f32[32,256]{1,0:T(8,128)S(1)}, f32[32,256]{1,0:T(8,128)S(1)}, u32[]{:S(2)}, u32[]{:S(2)}) collective-permute-start(f32[32,256]{1,0:T(8,128)S(1)} %get-tuple-element.48.refs_0_), channel_id=1, source_target_pairs={{0,16},{1,17},{2,18},{3,19},{4,20},{5,21},{6,22},{7,23},{8,24},{9,... | collective-permute-start | bytes 98312 | tf_op jit(solution)/shard_map/ppermute | solution.py:406
  42.7 11.3 %collective-permute-start.12 = (f32[32,256]{1,0:T(8,128)S(1)}, f32[32,256]{1,0:T(8,128)S(1)}, u32[]{:S(2)}, u32[]{:S(2)}) collective-permute-start(f32[32,256]{1,0:T(8,128)S(1)} %get-tuple-element.48.refs_0_), channel_id=1, source_target_pairs={{0,24},{1,25},{2,26},{3,27},{4,28},{5,29},{6,30},{7,31},{8,0},{9,1... | collective-permute-start | bytes 98312 | tf_op jit(solution)/shard_map/ppermute | solution.py:406
  45.2 8.8 %collective-permute-start.11 = (f32[32,256]{1,0:T(8,128)S(1)}, f32[32,256]{1,0:T(8,128)S(1)}, u32[]{:S(2)}, u32[]{:S(2)}) collective-permute-start(f32[32,256]{1,0:T(8,128)S(1)} %get-tuple-element.48.refs_0_), channel_id=1, source_target_pairs={{0,8},{1,9},{2,10},{3,11},{4,12},{5,13},{6,14},{7,15},{8,16},{9,17... | collective-permute-start | bytes 98312 | tf_op jit(solution)/shard_map/ppermute | solution.py:406
  52.6 1.9 %copy-start.2 = (f32[256,256]{1,0:T(8,128)S(1)}, f32[256,256]{1,0:T(8,128)}, u32[]{:S(2)}) copy-start(f32[256,256]{1,0:T(8,128)} %refs_0_.5) | copy-start | bytes 786436
  54.8 0.7 collective-permute-start.14
  55.6 0.7 collective-permute-start.15
  56.5 0.7 collective-permute-start.16
  57.3 0.7 collective-permute-start.17
  58.2 0.7 collective-permute-start.18
  59.0 0.7 collective-permute-start.19
  59.9 17.7 %collective-permute-start.20 = (f32[32,256]{1,0:T(8,128)S(1)}, f32[32,256]{1,0:T(8,128)S(1)}, u32[]{:S(2)}, u32[]{:S(2)}) collective-permute-start(f32[32,256]{1,0:T(8,128)S(1)} %hop.11), channel_id=1, source_target_pairs={{192,224},{193,225},{194,226},{195,227},{196,228},{197,229},{198,2... | collective-permute-start | bytes 98312 | tf_op jit(solution)/shard_map/ppermute | solution.py:425
  77.9 4.1 %collective-permute-start.21 = (f32[32,256]{1,0:T(8,128)S(1)}, f32[32,256]{1,0:T(8,128)S(1)}, u32[]{:S(2)}, u32[]{:S(2)}) collective-permute-start(f32[32,256]{1,0:T(8,128)S(1)} %get-tuple-element.55), channel_id=1, source_target_pairs={{0,2},{1,3},{2,4},{3,5},{4,6},{5,7},{6,0},{7,1},{8,10},{9,11},{10,... | collective-permute-start | bytes 98312 | tf_op jit(solution)/shard_map/ppermute | solution.py:437
  79.0 3.0 %collective-permute-start.22 = (f32[32,256]{1,0:T(8,128)S(1)}, f32[32,256]{1,0:T(8,128)S(1)}, u32[]{:S(2)}, u32[]{:S(2)}) collective-permute-start(f32[32,256]{1,0:T(8,128)S(1)} %get-tuple-element.56), channel_id=1, source_target_pairs={{0,6},{1,7},{2,0},{3,1},{4,2},{5,3},{6,4},{7,5},{8,14},{9,15},{10,... | collective-permute-start | bytes 98312 | tf_op jit(solution)/shard_map/ppermute | solution.py:437
  80.7 4.3 %collective-permute-start.23 = (f32[32,256]{1,0:T(8,128)S(1)}, f32[32,256]{1,0:T(8,128)S(1)}, u32[]{:S(2)}, u32[]{:S(2)}) collective-permute-start(f32[32,256]{1,0:T(8,128)S(1)} %get-tuple-element.57), channel_id=1, source_target_pairs={{0,4},{1,5},{2,6},{3,7},{4,0},{5,1},{6,2},{7,3},{8,12},{9,13},{10,... | collective-permute-start | bytes 98312 | tf_op jit(solution)/shard_map/ppermute | solution.py:437
  85.2 10.8 %collective-permute-start.24 = (f32[128,256]{1,0:T(8,128)S(1)}, f32[128,256]{1,0:T(8,128)S(1)}, u32[]{:S(2)}, u32[]{:S(2)}) collective-permute-start(f32[128,256]{1,0:T(8,128)S(1)} %get-tuple-element.60), channel_id=1, source_target_pairs={{0,1},{1,0},{2,3},{3,2},{4,5},{5,4},{6,7},{7,6},{8,9},{9,8},{10,11... | collective-permute-start | bytes 393224 | tf_op jit(solution)/shard_map/ppermute | solution.py:449

commit v6 on v5

--- a/solution.py
+++ b/solution.py
@@ -168,32 +168,81 @@
         ordered[lax.rem(place + count - s, count)] = ref[...]
 
 
-def line_map_kernel(pos, a0, a1, a3, a2, ordered, prefix, line):
-    order(pos[1], NY, ordered, (a0, a1, a3, a2))
-    total = ordered[0]
+def line_kernel(
+    pos, a0, a1, a3, a2, b0, b1, b3, b2, prefix, line, before, packet, maps, shifts
+):
+    order(pos[1], NY, maps, (a0, a1, a3, a2))
+    order(pos[1], NY, shifts, (b0, b1, b3, b2))
+    total, moved = maps[0], shifts[0]
     for k in range(1, NY):
         prefix[k - 1] = total
-        total = mm(split(total), split(ordered[k]))
+        before[k - 1] = moved
+        right = split(maps[k])
+        total = mm(split(total), right)
+        moved = mm(split(moved), right) + shifts[k]
     line[...] = total
-
-
-def group_map_kernel(pos, a0, a1, a3, a2, prefix, ordered, through, high, low, before):
+    h = line.shape[0] // 2
+    packet[:h] = line[pl.ds(pl.multiple_of(pos[0] * h, h), h), :]
+    packet[h:] = moved
+
+
+def stack_kernel(pos, p1, p3, p2, out):
+    for i, ref in enumerate((p1, p3, p2)):
+        out[i] = ref[: out.shape[1]]
+
+
+def group_kernel(
+    pos,
+    line,
+    p0,
+    p1,
+    p3,
+    p2,
+    theirs,
+    prefix,
+    before,
+    through,
+    high,
+    low,
+    b_through,
+    b_group,
+    maps,
+    shifts,
+    a_before,
+    own,
+):
     x = pos[2]
-    order(x, NX, ordered, (a0, a1, a3, a2))
     modes = high.shape[0]
+    h = theirs.shape[1]
+    here = pl.ds(pl.multiple_of(pos[0] * h, h), h)
+    there = pl.ds(pl.multiple_of((1 - pos[0]) * h, h), h)
+    maps[x] = line[...]
+    shifts[x] = p0[h:]
+    for i, (s, ref) in enumerate(zip(SHIFTS, (p1, p3, p2))):
+        spot = lax.rem(x + NX - s, NX)
+        maps[spot, here, :] = ref[:h]
+        maps[spot, there, :] = theirs[i]
+        shifts[spot] = ref[h:]
     rows = lax.broadcasted_iota(jnp.int32, (modes, modes), 0)
     cols = lax.broadcasted_iota(jnp.int32, (modes, modes), 1)
-    before[0] = jnp.where(rows == cols, 1.0, 0.0)
-    total = ordered[0]
+    a_before[0] = jnp.where(rows == cols, 1.0, 0.0)
+    own[0] = jnp.zeros_like(shifts[0])
+    total, moved = maps[0], shifts[0]
     for k in range(1, NX):
-        before[k] = total
-        total = mm(split(total), split(ordered[k]))
+        a_before[k] = total
+        own[k] = moved
+        right = split(maps[k])
+        total = mm(split(total), right)
+        moved = mm(split(moved), right) + shifts[k]
     high[...], low[...] = split(total)
-    own = before[x]
-    through[0] = own
-    own = split(own)
+    b_group[...] = moved
+    through[0] = a_before[x]
+    b_through[0] = own[x]
+    a_own, b_own = split(a_before[x]), split(own[x])
     for k in range(1, NY):
-        through[k] = mm(own, split(prefix[k - 1]))
+        right = split(prefix[k - 1])
+        through[k] = mm(a_own, right)
+        b_through[k] = mm(b_own, right) + before[k - 1]
 
 
 def pair_shift_kernel(pos, kept, got, both, first, s0, s1, s3, s2, chip):
@@ -211,31 +260,6 @@
         out[...] = chip[pl.ds(start, r), :]
 
 
-def line_shift_kernel(pos, b0, b1, b3, b2, maps, before, line, ordered):
-    order(pos[1], NY, ordered, (b0, b1, b3, b2))
-    total = ordered[0]
-    for k in range(1, NY):
-        before[k - 1] = total
-        total = mm(split(total), split(maps[k])) + ordered[k]
-    line[...] = total
-
-
-def group_shift_kernel(pos, b0, b1, b3, b2, maps, prefix, before, through, group, ordered, own):
-    x = pos[2]
-    order(x, NX, ordered, (b0, b1, b3, b2))
-    own[0] = jnp.zeros_like(ordered[0])
-    total = ordered[0]
-    for k in range(1, NX):
-        own[k] = total
-        total = mm(split(total), split(maps[k])) + ordered[k]
-    group[...] = total
-    prior = own[x]
-    through[0] = prior
-    prior = split(prior)
-    for k in range(1, NY):
-        through[k] = mm(prior, split(prefix[k - 1])) + before[k - 1]
-
-
 def released_rows(pos, initial, part):
     start = pl.multiple_of(pos[0] * (NY * part) + pos[1] * part, part)
     return initial[pl.ds(start, part), :]
@@ -330,7 +354,7 @@
             pltpu.SemaphoreType.DMA((5,)),
         ],
         name="pack",
-        cost_estimate=pl.CostEstimate(flops=0, bytes_accessed=2**20, transcendentals=0),
+        cost_estimate=pl.CostEstimate(flops=3000000000, bytes_accessed=2**20, transcendentals=0),
     )(rec_load[0], rec_sample[0].T, rec_step[0].T, rec_count)
     arrived = lax.all_to_all(packed, "tm", split_axis=0, concat_axis=0)
 
@@ -372,49 +396,32 @@
         flops=cube,
     )
     got = [lax.ppermute(r, "tm", along_y(s)) for r, s in zip(rows[1:], SHIFTS)]
-    y_maps, y_before, line = call(
-        line_map_kernel,
-        "line_map",
-        [(NY,) + mat, (NY - 1,) + mat, mat],
+    y_before, line, b_before, packet = call(
+        line_kernel,
+        "line",
+        [(NY - 1,) + mat, mat, (NY - 1,) + small, (half + part, modes)],
         chip,
         *chips,
-        flops=9 * cube,
-        after=got,
-    )
-    lines = [lax.ppermute(line, "tm", along_x(s)) for s in SHIFTS]
-    half_mat = jax.ShapeDtypeStruct(mat, BF16)
-    x_maps, through, high, low = call(
-        group_map_kernel,
-        "group_map",
-        [(NX,) + mat, (NY,) + mat, half_mat, half_mat],
-        line,
-        *lines,
-        y_before,
-        scratch=[vm(NX, *mat)],
-        flops=18 * cube,
-    )
-    b_before, b_line = call(
-        line_shift_kernel,
-        "line_shift",
-        [(NY - 1,) + small, small],
         rows[0],
         *got,
-        y_maps,
-        scratch=[vm(NY, *small)],
-        flops=cube,
-    )
-    got = [lax.ppermute(b_line, "tm", along_x(s)) for s in SHIFTS]
-    b_through, b_group = call(
-        group_shift_kernel,
-        "group_shift",
-        [(NY,) + small, small],
-        b_line,
-        *got,
-        x_maps,
+        scratch=[vm(NY, *mat), vm(NY, *small)],
+        flops=10 * cube,
+    )
+    packets = [lax.ppermute(packet, "tm", along_x(s)) for s in SHIFTS]
+    (halves,) = call(stack_kernel, "stack", [(NX - 1, half, modes)], *packets)
+    half_mat = jax.ShapeDtypeStruct(mat, BF16)
+    through, high, low, b_through, b_group = call(
+        group_kernel,
+        "group",
+        [(NY,) + mat, half_mat, half_mat, (NY,) + small, small],
+        line,
+        packet,
+        *packets,
+        lax.ppermute(halves, "tm", swap),
         y_before,
         b_before,
-        scratch=[vm(NX, *small), vm(NX, *small)],
-        flops=2 * cube,
+        scratch=[vm(NX, *mat), vm(NX, *small), vm(NX, *mat), vm(NX, *small)],
+        flops=20 * cube,
     )
     (e,) = call(
         first_hop_kernel, "hop0", [small], initial_state, high, low, b_group, flops=cube

time: 97.4 us -> 94.1 us (0.966)
  starting transfers between devices: 38.6 us -> 36.8 us
    ppermute x2, starting transfers between devices: 9.89 us -> 8.64 us  [body(): back = lax.ppermute(sent, 'tm', swap)]
    pallas_call x18 -> x17, Pallas kernels: 13.2 us -> 12.3 us  [call(): pl.pallas_call(run, out_shape=shapes, in_specs=[vmem] * n_args + [pl.Bloc...]
    ppermute x6 -> x4, waiting for transfers between devices: 9.29 us -> 8.45 us  [the longest x3 7.1 us: body(): packets = [lax.ppermute(packet, 'tm', along_x(s)) for s in SHIFTS]]
    ppermute x6 -> x4, starting transfers between devices: 5.26 us -> 4.91 us  [the longest x3 2.73 us: body(): packets = [lax.ppermute(packet, 'tm', along_x(s)) for s in SHIFTS]]
  transfers between devices with their start and end apart: 26 -> 24, of which waited for: 14 -> 15; matrix products, arithmetic and copies ran while one was open for 0% -> 0% of each run, Pallas kernels for 8% -> 6%
where the time goes in v6:
time: 94.1 us; the launch traced here: 93.7 us
  waiting for transfers between devices  39.7 us (42%)
  starting transfers between devices  36.8 us (39%)
  Pallas kernels  14.4 us (15%)
  local copies, waits for them, and re-layouts  1.81 us (2%)
  between operations  0.96 us (1%)
    ppermute x6, waiting for transfers between devices, body(): carried.append(lax.ppermute(e, 'grp', [(k, k + 1)]))  16.4 us
    pallas_call x17, Pallas kernels, call(): pl.pallas_call(run, out_shape=shapes, in_specs=[vmem] * n_args + [pl.Bloc...  12.3 us
    ppermute x2, starting transfers between devices, body(): back = lax.ppermute(sent, 'tm', swap)  8.64 us
    all_to_all x1, starting transfers between devices, body(): arrived = lax.all_to_all(packed, 'tm', split_axis=0, concat_axis=0)  7.77 us
    ppermute x3, waiting for transfers between devices, body(): packets = [lax.ppermute(packet, 'tm', along_x(s)) for s in SHIFTS]  7.1 us
    ppermute x6, starting transfers between devices, body(): got = [lax.ppermute(r, 'tm', along_y(s)) for r, s in zip(rows[1:], SHIFTS)]  5.5 us
    ppermute x6, waiting for transfers between devices, body(): got = [lax.ppermute(r, 'tm', along_y(s)) for r, s in zip(rows[1:], SHIFTS)]  5.4 us
    ppermute x6, starting transfers between devices, body(): carried.append(lax.ppermute(e, 'grp', [(k, k + 1)]))  4.61 us
  transfers between devices with their start and end apart: 24, of which 15 were waited for; matrix products, arithmetic and copies ran while one was open for 0% of the time, Pallas kernels for 6%

profile of v6, /device:TPU:225, one launch (start us, length us, event | category | flops | bytes accessed | tf_op | source)
XLA Modules:
  0.0 93.7 jit_solution(1053441835813257409)
XLA Ops:
  0.7 2.1 %pack.1.refs_3_ = f32[32,8,640]{2,1,0:T(8,128)} custom-call(f32[32,16,256]{2,1,0:T(8,128)} %bitcast.11, s32[16,32]{1,0:T(8,128)} %bitcast.13, s32[16,32]{1,0:T(8,128)} %bitcast.14, s32[1,32]{1,0:T(1,128)} %counts.1), custom_call_target="tpu_custom_call" | custom-call | flops 3000000000 | bytes 1048576 | tf_op jit(solution)/shard_map/pack/pallas_call | solution.py:345
  2.8 7.8 %all-to-all-start = ((f32[32,8,640]{2,1,0:T(8,128)}), f32[32,8,640]{2,1,0:T(8,128)S(1)}, u32[]{:S(2)}, u32[]{:S(2)}) async-start(f32[32,8,640]{2,1,0:T(8,128)} %pack.1.refs_3_), calls=%async_computation | async-start | bytes 1310720 | tf_op jit(solution)/shard_map/all_to_all | solution.py:359
  10.6 1.1 %copy-done = f32[32,8,640]{2,1,0:T(8,128)S(1)} copy-done((f32[32,8,640]{2,1,0:T(8,128)S(1)}, f32[32,8,640]{2,1,0:T(8,128)}, u32[]{:S(2)}) %copy-start) | copy-done | bytes 655384
  11.7 2.1 %compose.1 = (f32[256,256]{1,0:T(8,128)S(1)}, f32[8,256]{1,0:T(8,128)S(1)}) custom-call(f32[8,256]{1,0:T(8,128)S(1)} %copy-done.3, f32[8,256,256]{2,1,0:T(8,128)S(1)} %copy-done.1, f32[1,256]{1,0:T(1,128)S(1)} %bitcast.9, f32[32,8,640]{2,1,0:T(8,128)S(1)} %copy-done), custom_call_target="tpu_custom_call" | custom-call | flops 738197504 | bytes 2376704 | tf_op jit(solution)/shard_map/compose/pallas_call | solution.py:51
  13.9 0.3 collective-permute-start
  14.2 1.3 %collective-permute-done.refs_1_ = f32[256,256]{1,0:T(8,128)S(1)} collective-permute-done((f32[256,256]{1,0:T(8,128)S(1)}, f32[256,256]{1,0:T(8,128)S(1)}, u32[]{:S(2)}, u32[]{:S(2)}) %collective-permute-start) | collective-permute-done | bytes 262176 | tf_op jit(solution)/shard_map/ppermute | solution.py:373
  15.5 1.0 %pair_map.1 = (f32[2,256,256]{2,1,0:T(8,128)S(1)}, f32[256,256]{1,0:T(8,128)}) custom-call(f32[256,256]{1,0:T(8,128)S(1)} %get-tuple-element.32.refs_0_.refs_2_, f32[256,256]{1,0:T(8,128)S(1)} %collective-permute-done.refs_1_), custom_call_target="tpu_custom_call" | custom-call | flops 100663296 | bytes 1310720 | tf_op jit(solution)/shard_map/pair_map/pallas_call | solution.py:51
  16.5 2.9 %collective-permute-start.3 = (f32[256,256]{1,0:T(8,128)}, f32[256,256]{1,0:T(8,128)}, u32[]{:S(2)}, u32[]{:S(2)}) collective-permute-start(f32[256,256]{1,0:T(8,128)} %get-tuple-element.33.refs_0_), channel_id=1, source_target_pairs={{0,4},{1,5},{2,6},{3,7},{4,0},{5,1},{6,2},{7,3},{8,12},{9,13},{10,... | collective-permute-start | bytes 786440 | tf_op jit(solution)/shard_map/ppermute | solution.py:375
  19.4 0.9 collective-permute-start.2
  20.3 0.6 collective-permute-start.1
  20.9 2.7 %all-to-all-done.refs_0_ = f32[32,8,640]{2,1,0:T(8,128)S(1)} async-done(((f32[32,8,640]{2,1,0:T(8,128)}), f32[32,8,640]{2,1,0:T(8,128)S(1)}, u32[]{:S(2)}, u32[]{:S(2)}) %all-to-all-start) | async-done | bytes 655392 | tf_op jit(solution)/shard_map/all_to_all | solution.py:359
  23.6 0.7 copy-done.5
  24.3 2.6 %drive.1 = (f32[256,256]{1,0:T(8,128)S(1)}, f32[128,256]{1,0:T(8,128)S(1)}, f32[128,256]{1,0:T(8,128)S(1)}, f32[8,256]{1,0:T(8,128)S(1)}) custom-call(f32[32,8,640]{2,1,0:T(8,128)S(1)} %all-to-all-done.refs_0_, f32[8,256]{1,0:T(8,128)S(1)} %copy-done.3, f32[8,256,256]{2,1,0:T(8,128)S(1)} %copy-done.1, f32[1,256]{1,0:T(1,128)S(1)} %bitcast.10), custom_call_target="tpu_custom_call" | custom-call | flops 2013265920 | bytes 3294208 | tf_op jit(solution)/shard_map/drive/pallas_call | solution.py:51
  27.0 1.3 %collective-permute-done.4.refs_1_ = f32[128,256]{1,0:T(8,128)S(1)} collective-permute-done((f32[128,256]{1,0:T(8,128)S(1)}, f32[128,256]{1,0:T(8,128)S(1)}, u32[]{:S(2)}, u32[]{:S(2)}) %collective-permute-start.4) | collective-permute-done | bytes 131104 | tf_op jit(solution)/shard_map/ppermute | solution.py:386
  28.3 0.2 pair_shift.1
  28.6 2.7 %collective-permute-start.6 = (f32[32,256]{1,0:T(8,128)S(1)}, f32[32,256]{1,0:T(8,128)S(1)}, u32[]{:S(2)}, u32[]{:S(2)}) collective-permute-start(f32[32,256]{1,0:T(8,128)S(1)} %get-tuple-element.39), channel_id=1, source_target_pairs={{0,6},{1,7},{2,0},{3,1},{4,2},{5,3},{6,4},{7,5},{8,14},{9,15},{10,... | collective-permute-start | bytes 98312 | tf_op jit(solution)/shard_map/ppermute | solution.py:398
  31.3 1.3 %collective-permute-done.2.refs_2_ = f32[256,256]{1,0:T(8,128)} collective-permute-done((f32[256,256]{1,0:T(8,128)}, f32[256,256]{1,0:T(8,128)}, u32[]{:S(2)}, u32[]{:S(2)}) %collective-permute-start.2) | collective-permute-done | bytes 262176 | tf_op jit(solution)/shard_map/ppermute | solution.py:375
  32.6 1.9 %collective-permute-done.1.refs_1_ = f32[256,256]{1,0:T(8,128)} collective-permute-done((f32[256,256]{1,0:T(8,128)}, f32[256,256]{1,0:T(8,128)}, u32[]{:S(2)}, u32[]{:S(2)}) %collective-permute-start.1) | collective-permute-done | bytes 262176 | tf_op jit(solution)/shard_map/ppermute | solution.py:375
  34.4 0.6 collective-permute-done.5.refs_5_
  35.0 0.5 collective-permute-done.7.refs_7_
  35.6 2.2 %line.1 = (f32[3,256,256]{2,1,0:T(8,128)S(1)}, f32[256,256]{1,0:T(8,128)S(1)}, f32[3,32,256]{2,1,0:T(8,128)S(1)}, f32[160,256]{1,0:T(8,128)S(1)}) custom-call(f32[256,256]{1,0:T(8,128)} %get-tuple-element.33.refs_0_, f32[256,256]{1,0:T(8,128)} %collective-permute-done.1.refs_1_, f32[256,256]{1,0:T(8,128)} %collective-permute-done.2.refs_2_, ...), custom_call_target="tpu_custom_call" | custom-call | flops 335544320 | bytes 2490368 | tf_op jit(solution)/shard_map/line/pallas_call | solution.py:51
  37.8 1.3 %collective-permute-start.10 = (f32[160,256]{1,0:T(8,128)S(1)}, f32[160,256]{1,0:T(8,128)S(1)}, u32[]{:S(2)}, u32[]{:S(2)}) collective-permute-start(f32[160,256]{1,0:T(8,128)S(1)} %get-tuple-element.42.refs_1_), channel_id=1, source_target_pairs={{0,16},{1,17},{2,18},{3,19},{4,20},{5,21},{6,22},{7,23},{8,24},{9,... | collective-permute-start | bytes 491528 | tf_op jit(solution)/shard_map/ppermute | solution.py:410
  39.0 1.1 %collective-permute-start.9 = (f32[160,256]{1,0:T(8,128)S(1)}, f32[160,256]{1,0:T(8,128)S(1)}, u32[]{:S(2)}, u32[]{:S(2)}) collective-permute-start(f32[160,256]{1,0:T(8,128)S(1)} %get-tuple-element.42.refs_1_), channel_id=1, source_target_pairs={{0,24},{1,25},{2,26},{3,27},{4,28},{5,29},{6,30},{7,31},{8,0},{9,1... | collective-permute-start | bytes 491528 | tf_op jit(solution)/shard_map/ppermute | solution.py:410
  40.1 0.4 collective-permute-start.8
  40.5 3.0 %collective-permute-done.10.refs_2_.refs_4_ = f32[160,256]{1,0:T(8,128)S(1)} collective-permute-done((f32[160,256]{1,0:T(8,128)S(1)}, f32[160,256]{1,0:T(8,128)S(1)}, u32[]{:S(2)}, u32[]{:S(2)}) %collective-permute-start.10) | collective-permute-done | bytes 163872 | tf_op jit(solution)/shard_map/ppermute | solution.py:410
  43.5 1.5 %collective-permute-done.9.refs_1_.refs_3_ = f32[160,256]{1,0:T(8,128)S(1)} collective-permute-done((f32[160,256]{1,0:T(8,128)S(1)}, f32[160,256]{1,0:T(8,128)S(1)}, u32[]{:S(2)}, u32[]{:S(2)}) %collective-permute-start.9) | collective-permute-done | bytes 163872 | tf_op jit(solution)/shard_map/ppermute | solution.py:410
  45.0 2.6 %collective-permute-done.8.refs_0_.refs_2_ = f32[160,256]{1,0:T(8,128)S(1)} collective-permute-done((f32[160,256]{1,0:T(8,128)S(1)}, f32[160,256]{1,0:T(8,128)S(1)}, u32[]{:S(2)}, u32[]{:S(2)}) %collective-permute-start.8) | collective-permute-done | bytes 163872 | tf_op jit(solution)/shard_map/ppermute | solution.py:410
  47.6 2.2 %collective-permute-start.11 = (f32[3,128,256]{2,1,0:T(8,128)S(1)}, f32[3,128,256]{2,1,0:T(8,128)S(1)}, u32[]{:S(2)}, u32[]{:S(2)}) collective-permute-start(f32[3,128,256]{2,1,0:T(8,128)S(1)} %stack.1), channel_id=1, source_target_pairs={{0,1},{1,0},{2,3},{3,2},{4,5},{5,4},{6,7},{7,6},{8,9},{9,8},{10,11... | collective-permute-start | bytes 1179656 | tf_op jit(solution)/shard_map/ppermute | solution.py:420
  49.8 1.3 %collective-permute-done.11.refs_5_ = f32[3,128,256]{2,1,0:T(8,128)S(1)} collective-permute-done((f32[3,128,256]{2,1,0:T(8,128)S(1)}, f32[3,128,256]{2,1,0:T(8,128)S(1)}, u32[]{:S(2)}, u32[]{:S(2)}) %collective-permute-start.11) | collective-permute-done | bytes 393248 | tf_op jit(solution)/shard_map/ppermute | solution.py:420
  51.2 1.3 %group.1 = (f32[4,256,256]{2,1,0:T(8,128)S(1)}, bf16[256,256]{1,0:T(8,128)(2,1)S(1)}, bf16[256,256]{1,0:T(8,128)(2,1)S(1)}, f32[4,32,256]{2,1,0:T(8,128)S(1)}, f32[32,256]{1,0:T(8,128)S(1)}) custom-call(f32[256,256]{1,0:T(8,128)S(1)} %get-tuple-element.41.refs_0_, f32[160,256]{1,0:T(8,128)S(1)} %get-tuple-element.42.refs_1_, ...), custom_call_target="tpu_custom_call" | custom-call | flops 671088640 | bytes 3932160 | tf_op jit(solution)/shard_map/group/pallas_call | solution.py:51
  52.5 0.2 hop0.1
  52.7 0.7 collective-permute-start.12
  53.6 0.7 collective-permute-start.13
  54.4 0.7 collective-permute-start.14
  55.1 0.2 hop.8
  55.3 0.7 collective-permute-start.15
  56.1 0.7 collective-permute-start.16
  57.0 0.7 collective-permute-start.17
  57.8 1.3 %collective-permute-start.18 = (f32[32,256]{1,0:T(8,128)S(1)}, f32[32,256]{1,0:T(8,128)S(1)}, u32[]{:S(2)}, u32[]{:S(2)}) collective-permute-start(f32[32,256]{1,0:T(8,128)S(1)} %hop.11), channel_id=1, source_target_pairs={{192,224},{193,225},{194,226},{195,227},{196,228},{197,229},{198,2... | collective-permute-start | bytes 98312 | tf_op jit(solution)/shard_map/ppermute | solution.py:432
  59.1 16.4 %collective-permute-done.18.refs_7_ = f32[32,256]{1,0:T(8,128)S(1)} collective-permute-done((f32[32,256]{1,0:T(8,128)S(1)}, f32[32,256]{1,0:T(8,128)S(1)}, u32[]{:S(2)}, u32[]{:S(2)}) %collective-permute-start.18) | collective-permute-done | bytes 32800 | tf_op jit(solution)/shard_map/ppermute | solution.py:432
  75.5 0.3 chips.1
  75.9 2.7 %collective-permute-start.20 = (f32[32,256]{1,0:T(8,128)S(1)}, f32[32,256]{1,0:T(8,128)S(1)}, u32[]{:S(2)}, u32[]{:S(2)}) collective-permute-start(f32[32,256]{1,0:T(8,128)S(1)} %get-tuple-element.52), channel_id=1, source_target_pairs={{0,6},{1,7},{2,0},{3,1},{4,2},{5,3},{6,4},{7,5},{8,14},{9,15},{10,... | collective-permute-start | bytes 98312 | tf_op jit(solution)/shard_map/ppermute | solution.py:444
  78.6 1.3 %collective-permute-done.19.refs_1_ = f32[32,256]{1,0:T(8,128)S(1)} collective-permute-done((f32[32,256]{1,0:T(8,128)S(1)}, f32[32,256]{1,0:T(8,128)S(1)}, u32[]{:S(2)}, u32[]{:S(2)}) %collective-permute-start.19) | collective-permute-done | bytes 32800 | tf_op jit(solution)/shard_map/ppermute | solution.py:444
  79.9 3.0 %collective-permute-done.21.refs_3_ = f32[32,256]{1,0:T(8,128)S(1)} collective-permute-done((f32[32,256]{1,0:T(8,128)S(1)}, f32[32,256]{1,0:T(8,128)S(1)}, u32[]{:S(2)}, u32[]{:S(2)}) %collective-permute-start.21) | collective-permute-done | bytes 32800 | tf_op jit(solution)/shard_map/ppermute | solution.py:444
  82.9 0.2 chip_start.1
  83.1 8.5 %collective-permute-start.22 = (f32[128,256]{1,0:T(8,128)S(1)}, f32[128,256]{1,0:T(8,128)S(1)}, u32[]{:S(2)}, u32[]{:S(2)}) collective-permute-start(f32[128,256]{1,0:T(8,128)S(1)} %get-tuple-element.56), channel_id=1, source_target_pairs={{0,1},{1,0},{2,3},{3,2},{4,5},{5,4},{6,7},{7,6},{8,9},{9,8},{10,11... | collective-permute-start | bytes 393224 | tf_op jit(solution)/shard_map/ppermute | solution.py:456
  91.6 1.0 %collective-permute-done.22.refs_1_ = f32[128,256]{1,0:T(8,128)S(1)} collective-permute-done((f32[128,256]{1,0:T(8,128)S(1)}, f32[128,256]{1,0:T(8,128)S(1)}, u32[]{:S(2)}, u32[]{:S(2)}) %collective-permute-start.22) | collective-permute-done | bytes 131104 | tf_op jit(solution)/shard_map/ppermute | solution.py:456
  92.6 1.1 %finish.1 = (f32[8,256]{1,0:T(8,128)}, f32[256,256]{1,0:T(8,128)}) custom-call(f32[128,256]{1,0:T(8,128)S(1)} %get-tuple-element.55.refs_0_, f32[128,256]{1,0:T(8,128)S(1)} %collective-permute-done.22.refs_1_, f32[256,256]{1,0:T(8,128)S(1)} %get-tuple-element.32.refs_0_.refs_2_, f32[256,256]{1,0:T(8,128)S(1)} %get-tuple-element.57.refs_3_, ...), custom_call_target="tpu_custom_call" | custom-call | flops 100663296 | bytes 1073152 | tf_op jit(solution)/shard_map/finish/pallas_call | solution.py:51
  (30 shorter events, 1.1 us)
Async XLA Ops:
  0.6 9.9 %copy-start.1 = (f32[8,256,256]{2,1,0:T(8,128)S(1)}, f32[8,256,256]{2,1,0:T(8,128)}, u32[]{:S(2)}) copy-start(f32[8,256,256]{2,1,0:T(8,128)} %refs_2_.1) | copy-start | bytes 6291460
  0.6 9.9 %copy-start.3 = (f32[8,256]{1,0:T(8,128)S(1)}, f32[8,256]{1,0:T(8,128)}, u32[]{:S(2)}) copy-start(f32[8,256]{1,0:T(8,128)} %refs_1_.3) | copy-start | bytes 24580
  0.7 9.9 %copy-start.4 = (f32[256]{0:T(256)S(1)}, f32[256]{0:T(256)}, u32[]{:S(2)}) copy-start(f32[256]{0:T(256)} %param.11) | copy-start | bytes 3076
  2.8 20.8 %all-to-all-start = ((f32[32,8,640]{2,1,0:T(8,128)}), f32[32,8,640]{2,1,0:T(8,128)S(1)}, u32[]{:S(2)}, u32[]{:S(2)}) async-start(f32[32,8,640]{2,1,0:T(8,128)} %pack.1.refs_3_), calls=%async_computation | async-start | bytes 1310720 | tf_op jit(solution)/shard_map/all_to_all | solution.py:359
  10.6 1.1 %copy-start = (f32[32,8,640]{2,1,0:T(8,128)S(1)}, f32[32,8,640]{2,1,0:T(8,128)}, u32[]{:S(2)}) copy-start(f32[32,8,640]{2,1,0:T(8,128)} %pack.1.refs_3_) | copy-start | bytes 1966084
  13.9 1.6 %collective-permute-start = (f32[256,256]{1,0:T(8,128)S(1)}, f32[256,256]{1,0:T(8,128)S(1)}, u32[]{:S(2)}, u32[]{:S(2)}) collective-permute-start(f32[256,256]{1,0:T(8,128)S(1)} %get-tuple-element.32.refs_0_.refs_2_), channel_id=1, source_target_pairs={{0,1},{1,0},{2,3},{3,2},{4,5},{5,4},{6,7},{7,6},{8,9},{9,8},{10,11... | collective-permute-start | bytes 786440 | tf_op jit(solution)/shard_map/ppermute | solution.py:373
  16.5 14.8 %collective-permute-start.3 = (f32[256,256]{1,0:T(8,128)}, f32[256,256]{1,0:T(8,128)}, u32[]{:S(2)}, u32[]{:S(2)}) collective-permute-start(f32[256,256]{1,0:T(8,128)} %get-tuple-element.33.refs_0_), channel_id=1, source_target_pairs={{0,4},{1,5},{2,6},{3,7},{4,0},{5,1},{6,2},{7,3},{8,12},{9,13},{10,... | collective-permute-start | bytes 786440 | tf_op jit(solution)/shard_map/ppermute | solution.py:375
  19.4 13.2 %collective-permute-start.2 = (f32[256,256]{1,0:T(8,128)}, f32[256,256]{1,0:T(8,128)}, u32[]{:S(2)}, u32[]{:S(2)}) collective-permute-start(f32[256,256]{1,0:T(8,128)} %get-tuple-element.33.refs_0_), channel_id=1, source_target_pairs={{0,6},{1,7},{2,0},{3,1},{4,2},{5,3},{6,4},{7,5},{8,14},{9,15},{10,... | collective-permute-start | bytes 786440 | tf_op jit(solution)/shard_map/ppermute | solution.py:375
  20.3 14.2 %collective-permute-start.1 = (f32[256,256]{1,0:T(8,128)}, f32[256,256]{1,0:T(8,128)}, u32[]{:S(2)}, u32[]{:S(2)}) collective-permute-start(f32[256,256]{1,0:T(8,128)} %get-tuple-element.33.refs_0_), channel_id=1, source_target_pairs={{0,2},{1,3},{2,4},{3,5},{4,6},{5,7},{6,0},{7,1},{8,10},{9,11},{10,... | collective-permute-start | bytes 786440 | tf_op jit(solution)/shard_map/ppermute | solution.py:375
  23.6 0.7 copy-start.5
  26.9 1.4 %collective-permute-start.4 = (f32[128,256]{1,0:T(8,128)S(1)}, f32[128,256]{1,0:T(8,128)S(1)}, u32[]{:S(2)}, u32[]{:S(2)}) collective-permute-start(f32[128,256]{1,0:T(8,128)S(1)} %get-tuple-element.35), channel_id=1, source_target_pairs={{0,1},{1,0},{2,3},{3,2},{4,5},{5,4},{6,7},{7,6},{8,9},{9,8},{10,11... | collective-permute-start | bytes 393224 | tf_op jit(solution)/shard_map/ppermute | solution.py:386
  28.5 6.5 %collective-permute-start.5 = (f32[32,256]{1,0:T(8,128)S(1)}, f32[32,256]{1,0:T(8,128)S(1)}, u32[]{:S(2)}, u32[]{:S(2)}) collective-permute-start(f32[32,256]{1,0:T(8,128)S(1)} %get-tuple-element.38), channel_id=1, source_target_pairs={{0,2},{1,3},{2,4},{3,5},{4,6},{5,7},{6,0},{7,1},{8,10},{9,11},{10,... | collective-permute-start | bytes 98312 | tf_op jit(solution)/shard_map/ppermute | solution.py:398
  28.6 6.4 %collective-permute-start.6 = (f32[32,256]{1,0:T(8,128)S(1)}, f32[32,256]{1,0:T(8,128)S(1)}, u32[]{:S(2)}, u32[]{:S(2)}) collective-permute-start(f32[32,256]{1,0:T(8,128)S(1)} %get-tuple-element.39), channel_id=1, source_target_pairs={{0,6},{1,7},{2,0},{3,1},{4,2},{5,3},{6,4},{7,5},{8,14},{9,15},{10,... | collective-permute-start | bytes 98312 | tf_op jit(solution)/shard_map/ppermute | solution.py:398
  31.3 4.3 %collective-permute-start.7 = (f32[32,256]{1,0:T(8,128)S(1)}, f32[32,256]{1,0:T(8,128)S(1)}, u32[]{:S(2)}, u32[]{:S(2)}) collective-permute-start(f32[32,256]{1,0:T(8,128)S(1)} %get-tuple-element.40), channel_id=1, source_target_pairs={{0,4},{1,5},{2,6},{3,7},{4,0},{5,1},{6,2},{7,3},{8,12},{9,13},{10,... | collective-permute-start | bytes 98312 | tf_op jit(solution)/shard_map/ppermute | solution.py:398
  35.6 17.0 %copy-start.2 = (f32[256,256]{1,0:T(8,128)S(1)}, f32[256,256]{1,0:T(8,128)}, u32[]{:S(2)}) copy-start(f32[256,256]{1,0:T(8,128)} %refs_0_.5) | copy-start | bytes 786436
  37.8 5.8 %collective-permute-start.10 = (f32[160,256]{1,0:T(8,128)S(1)}, f32[160,256]{1,0:T(8,128)S(1)}, u32[]{:S(2)}, u32[]{:S(2)}) collective-permute-start(f32[160,256]{1,0:T(8,128)S(1)} %get-tuple-element.42.refs_1_), channel_id=1, source_target_pairs={{0,16},{1,17},{2,18},{3,19},{4,20},{5,21},{6,22},{7,23},{8,24},{9,... | collective-permute-start | bytes 491528 | tf_op jit(solution)/shard_map/ppermute | solution.py:410
  39.0 6.0 %collective-permute-start.9 = (f32[160,256]{1,0:T(8,128)S(1)}, f32[160,256]{1,0:T(8,128)S(1)}, u32[]{:S(2)}, u32[]{:S(2)}) collective-permute-start(f32[160,256]{1,0:T(8,128)S(1)} %get-tuple-element.42.refs_1_), channel_id=1, source_target_pairs={{0,24},{1,25},{2,26},{3,27},{4,28},{5,29},{6,30},{7,31},{8,0},{9,1... | collective-permute-start | bytes 491528 | tf_op jit(solution)/shard_map/ppermute | solution.py:410
  40.1 7.5 %collective-permute-start.8 = (f32[160,256]{1,0:T(8,128)S(1)}, f32[160,256]{1,0:T(8,128)S(1)}, u32[]{:S(2)}, u32[]{:S(2)}) collective-permute-start(f32[160,256]{1,0:T(8,128)S(1)} %get-tuple-element.42.refs_1_), channel_id=1, source_target_pairs={{0,8},{1,9},{2,10},{3,11},{4,12},{5,13},{6,14},{7,15},{8,16},{9,17... | collective-permute-start | bytes 491528 | tf_op jit(solution)/shard_map/ppermute | solution.py:410
  47.6 3.5 %collective-permute-start.11 = (f32[3,128,256]{2,1,0:T(8,128)S(1)}, f32[3,128,256]{2,1,0:T(8,128)S(1)}, u32[]{:S(2)}, u32[]{:S(2)}) collective-permute-start(f32[3,128,256]{2,1,0:T(8,128)S(1)} %stack.1), channel_id=1, source_target_pairs={{0,1},{1,0},{2,3},{3,2},{4,5},{5,4},{6,7},{7,6},{8,9},{9,8},{10,11... | collective-permute-start | bytes 1179656 | tf_op jit(solution)/shard_map/ppermute | solution.py:420
  52.7 0.7 collective-permute-start.12
  53.6 0.7 collective-permute-start.13
  54.4 0.7 collective-permute-start.14
  55.3 0.7 collective-permute-start.15
  56.1 0.7 collective-permute-start.16
  57.0 0.7 collective-permute-start.17
  57.8 17.7 %collective-permute-start.18 = (f32[32,256]{1,0:T(8,128)S(1)}, f32[32,256]{1,0:T(8,128)S(1)}, u32[]{:S(2)}, u32[]{:S(2)}) collective-permute-start(f32[32,256]{1,0:T(8,128)S(1)} %hop.11), channel_id=1, source_target_pairs={{192,224},{193,225},{194,226},{195,227},{196,228},{197,229},{198,2... | collective-permute-start | bytes 98312 | tf_op jit(solution)/shard_map/ppermute | solution.py:432
  75.8 4.1 %collective-permute-start.19 = (f32[32,256]{1,0:T(8,128)S(1)}, f32[32,256]{1,0:T(8,128)S(1)}, u32[]{:S(2)}, u32[]{:S(2)}) collective-permute-start(f32[32,256]{1,0:T(8,128)S(1)} %get-tuple-element.51), channel_id=1, source_target_pairs={{0,2},{1,3},{2,4},{3,5},{4,6},{5,7},{6,0},{7,1},{8,10},{9,11},{10,... | collective-permute-start | bytes 98312 | tf_op jit(solution)/shard_map/ppermute | solution.py:444
  75.9 4.0 %collective-permute-start.20 = (f32[32,256]{1,0:T(8,128)S(1)}, f32[32,256]{1,0:T(8,128)S(1)}, u32[]{:S(2)}, u32[]{:S(2)}) collective-permute-start(f32[32,256]{1,0:T(8,128)S(1)} %get-tuple-element.52), channel_id=1, source_target_pairs={{0,6},{1,7},{2,0},{3,1},{4,2},{5,3},{6,4},{7,5},{8,14},{9,15},{10,... | collective-permute-start | bytes 98312 | tf_op jit(solution)/shard_map/ppermute | solution.py:444
  78.6 4.3 %collective-permute-start.21 = (f32[32,256]{1,0:T(8,128)S(1)}, f32[32,256]{1,0:T(8,128)S(1)}, u32[]{:S(2)}, u32[]{:S(2)}) collective-permute-start(f32[32,256]{1,0:T(8,128)S(1)} %get-tuple-element.53), channel_id=1, source_target_pairs={{0,4},{1,5},{2,6},{3,7},{4,0},{5,1},{6,2},{7,3},{8,12},{9,13},{10,... | collective-permute-start | bytes 98312 | tf_op jit(solution)/shard_map/ppermute | solution.py:444
  83.1 9.5 %collective-permute-start.22 = (f32[128,256]{1,0:T(8,128)S(1)}, f32[128,256]{1,0:T(8,128)S(1)}, u32[]{:S(2)}, u32[]{:S(2)}) collective-permute-start(f32[128,256]{1,0:T(8,128)S(1)} %get-tuple-element.56), channel_id=1, source_target_pairs={{0,1},{1,0},{2,3},{3,2},{4,5},{5,4},{6,7},{7,6},{8,9},{9,8},{10,11... | collective-permute-start | bytes 393224 | tf_op jit(solution)/shard_map/ppermute | solution.py:456

commit v7 on v6

--- a/solution.py
+++ b/solution.py
@@ -186,11 +186,6 @@
     packet[h:] = moved
 
 
-def stack_kernel(pos, p1, p3, p2, out):
-    for i, ref in enumerate((p1, p3, p2)):
-        out[i] = ref[: out.shape[1]]
-
-
 def group_kernel(
     pos,
     line,
@@ -198,7 +193,9 @@
     p1,
     p3,
     p2,
-    theirs,
+    t1,
+    t3,
+    t2,
     prefix,
     before,
     through,
@@ -213,15 +210,15 @@
 ):
     x = pos[2]
     modes = high.shape[0]
-    h = theirs.shape[1]
+    h = modes // 2
     here = pl.ds(pl.multiple_of(pos[0] * h, h), h)
     there = pl.ds(pl.multiple_of((1 - pos[0]) * h, h), h)
     maps[x] = line[...]
     shifts[x] = p0[h:]
-    for i, (s, ref) in enumerate(zip(SHIFTS, (p1, p3, p2))):
+    for s, ref, theirs in zip(SHIFTS, (p1, p3, p2), (t1, t3, t2)):
         spot = lax.rem(x + NX - s, NX)
         maps[spot, here, :] = ref[:h]
-        maps[spot, there, :] = theirs[i]
+        maps[spot, there, :] = theirs[:h]
         shifts[spot] = ref[h:]
     rows = lax.broadcasted_iota(jnp.int32, (modes, modes), 0)
     cols = lax.broadcasted_iota(jnp.int32, (modes, modes), 1)
@@ -408,7 +405,7 @@
         flops=10 * cube,
     )
     packets = [lax.ppermute(packet, "tm", along_x(s)) for s in SHIFTS]
-    (halves,) = call(stack_kernel, "stack", [(NX - 1, half, modes)], *packets)
+    swapped = [lax.ppermute(p, "tm", swap) for p in packets]
     half_mat = jax.ShapeDtypeStruct(mat, BF16)
     through, high, low, b_through, b_group = call(
         group_kernel,
@@ -417,7 +414,7 @@
         line,
         packet,
         *packets,
-        lax.ppermute(halves, "tm", swap),
+        *swapped,
         y_before,
         b_before,
         scratch=[vm(NX, *mat), vm(NX, *small), vm(NX, *mat), vm(NX, *small)],

time: 94.1 us -> 93.6 us (level)
  waiting for transfers between devices: 39.7 us -> 35.4 us
  starting transfers between devices: 36.8 us -> 40.7 us
    ppermute x3, waiting for transfers between devices: 7.1 us -> 3.04 us  [body(): packets = [lax.ppermute(packet, 'tm', along_x(s)) for s in SHIFTS]]
    ppermute x1 -> x3, starting transfers between devices: 2.19 us -> 6.16 us  [body(): swapped = [lax.ppermute(p, 'tm', swap) for p in packets]]
    pallas_call x17 -> x16, Pallas kernels: 12.3 us -> 12.3 us  [call(): pl.pallas_call(run, out_shape=shapes, in_specs=[vmem] * n_args + [pl.Bloc...]
  transfers between devices with their start and end apart: 24 -> 26, of which waited for: 15 -> 13; matrix products, arithmetic and copies ran while one was open for 0% -> 0% of each run, Pallas kernels for 6% -> 6%
where the time goes in v7:
time: 93.6 us; the launch traced here: 93.2 us
  starting transfers between devices  40.7 us (43%)
  waiting for transfers between devices  35.4 us (38%)
  Pallas kernels  14.4 us (15%)
  local copies, waits for them, and re-layouts  1.81 us (2%)
  between operations  0.96 us (1%)
    ppermute x6, waiting for transfers between devices, body(): carried.append(lax.ppermute(e, 'grp', [(k, k + 1)]))  16.4 us
    pallas_call x16, Pallas kernels, call(): pl.pallas_call(run, out_shape=shapes, in_specs=[vmem] * n_args + [pl.Bloc...  12.3 us
    ppermute x2, starting transfers between devices, body(): back = lax.ppermute(sent, 'tm', swap)  8.62 us
    all_to_all x1, starting transfers between devices, body(): arrived = lax.all_to_all(packed, 'tm', split_axis=0, concat_axis=0)  7.77 us
    ppermute x3, starting transfers between devices, body(): swapped = [lax.ppermute(p, 'tm', swap) for p in packets]  6.16 us
    ppermute x6, starting transfers between devices, body(): got = [lax.ppermute(r, 'tm', along_y(s)) for r, s in zip(rows[1:], SHIFTS)]  5.5 us
    ppermute x6, waiting for transfers between devices, body(): got = [lax.ppermute(r, 'tm', along_y(s)) for r, s in zip(rows[1:], SHIFTS)]  5.4 us
    ppermute x6, starting transfers between devices, body(): carried.append(lax.ppermute(e, 'grp', [(k, k + 1)]))  4.61 us
  transfers between devices with their start and end apart: 26, of which 13 were waited for; matrix products, arithmetic and copies ran while one was open for 0% of the time, Pallas kernels for 6%

profile of v7, /device:TPU:225, one launch (start us, length us, event | category | flops | bytes accessed | tf_op | source)
XLA Modules:
  0.0 93.2 jit_solution(574147092131801637)
XLA Ops:
  0.7 2.1 %pack.1.refs_3_ = f32[32,8,640]{2,1,0:T(8,128)} custom-call(f32[32,16,256]{2,1,0:T(8,128)} %bitcast.11, s32[16,32]{1,0:T(8,128)} %bitcast.13, s32[16,32]{1,0:T(8,128)} %bitcast.14, s32[1,32]{1,0:T(1,128)} %counts.1), custom_call_target="tpu_custom_call" | custom-call | flops 3000000000 | bytes 1048576 | tf_op jit(solution)/shard_map/pack/pallas_call | solution.py:342
  2.8 7.8 %all-to-all-start = ((f32[32,8,640]{2,1,0:T(8,128)}), f32[32,8,640]{2,1,0:T(8,128)S(1)}, u32[]{:S(2)}, u32[]{:S(2)}) async-start(f32[32,8,640]{2,1,0:T(8,128)} %pack.1.refs_3_), calls=%async_computation | async-start | bytes 1310720 | tf_op jit(solution)/shard_map/all_to_all | solution.py:356
  10.6 1.1 %copy-done = f32[32,8,640]{2,1,0:T(8,128)S(1)} copy-done((f32[32,8,640]{2,1,0:T(8,128)S(1)}, f32[32,8,640]{2,1,0:T(8,128)}, u32[]{:S(2)}) %copy-start) | copy-done | bytes 655384
  11.7 2.1 %compose.1 = (f32[256,256]{1,0:T(8,128)S(1)}, f32[8,256]{1,0:T(8,128)S(1)}) custom-call(f32[8,256]{1,0:T(8,128)S(1)} %copy-done.3, f32[8,256,256]{2,1,0:T(8,128)S(1)} %copy-done.1, f32[1,256]{1,0:T(1,128)S(1)} %bitcast.9, f32[32,8,640]{2,1,0:T(8,128)S(1)} %copy-done), custom_call_target="tpu_custom_call" | custom-call | flops 738197504 | bytes 2376704 | tf_op jit(solution)/shard_map/compose/pallas_call | solution.py:51
  13.9 0.3 collective-permute-start
  14.2 1.3 %collective-permute-done.refs_1_ = f32[256,256]{1,0:T(8,128)S(1)} collective-permute-done((f32[256,256]{1,0:T(8,128)S(1)}, f32[256,256]{1,0:T(8,128)S(1)}, u32[]{:S(2)}, u32[]{:S(2)}) %collective-permute-start) | collective-permute-done | bytes 262176 | tf_op jit(solution)/shard_map/ppermute | solution.py:370
  15.5 1.0 %pair_map.1 = (f32[2,256,256]{2,1,0:T(8,128)S(1)}, f32[256,256]{1,0:T(8,128)}) custom-call(f32[256,256]{1,0:T(8,128)S(1)} %get-tuple-element.32.refs_0_.refs_2_, f32[256,256]{1,0:T(8,128)S(1)} %collective-permute-done.refs_1_), custom_call_target="tpu_custom_call" | custom-call | flops 100663296 | bytes 1310720 | tf_op jit(solution)/shard_map/pair_map/pallas_call | solution.py:51
  16.5 2.9 %collective-permute-start.3 = (f32[256,256]{1,0:T(8,128)}, f32[256,256]{1,0:T(8,128)}, u32[]{:S(2)}, u32[]{:S(2)}) collective-permute-start(f32[256,256]{1,0:T(8,128)} %get-tuple-element.33.refs_0_), channel_id=1, source_target_pairs={{0,4},{1,5},{2,6},{3,7},{4,0},{5,1},{6,2},{7,3},{8,12},{9,13},{10,... | collective-permute-start | bytes 786440 | tf_op jit(solution)/shard_map/ppermute | solution.py:372
  19.4 0.9 collective-permute-start.2
  20.3 0.6 collective-permute-start.1
  20.8 2.7 %all-to-all-done.refs_0_ = f32[32,8,640]{2,1,0:T(8,128)S(1)} async-done(((f32[32,8,640]{2,1,0:T(8,128)}), f32[32,8,640]{2,1,0:T(8,128)S(1)}, u32[]{:S(2)}, u32[]{:S(2)}) %all-to-all-start) | async-done | bytes 655392 | tf_op jit(solution)/shard_map/all_to_all | solution.py:356
  23.6 0.7 copy-done.5
  24.2 2.6 %drive.1 = (f32[256,256]{1,0:T(8,128)S(1)}, f32[128,256]{1,0:T(8,128)S(1)}, f32[128,256]{1,0:T(8,128)S(1)}, f32[8,256]{1,0:T(8,128)S(1)}) custom-call(f32[32,8,640]{2,1,0:T(8,128)S(1)} %all-to-all-done.refs_0_, f32[8,256]{1,0:T(8,128)S(1)} %copy-done.3, f32[8,256,256]{2,1,0:T(8,128)S(1)} %copy-done.1, f32[1,256]{1,0:T(1,128)S(1)} %bitcast.10), custom_call_target="tpu_custom_call" | custom-call | flops 2013265920 | bytes 3294208 | tf_op jit(solution)/shard_map/drive/pallas_call | solution.py:51
  27.0 1.3 %collective-permute-done.4.refs_1_ = f32[128,256]{1,0:T(8,128)S(1)} collective-permute-done((f32[128,256]{1,0:T(8,128)S(1)}, f32[128,256]{1,0:T(8,128)S(1)}, u32[]{:S(2)}, u32[]{:S(2)}) %collective-permute-start.4) | collective-permute-done | bytes 131104 | tf_op jit(solution)/shard_map/ppermute | solution.py:383
  28.3 0.2 pair_shift.1
  28.6 2.7 %collective-permute-start.6 = (f32[32,256]{1,0:T(8,128)S(1)}, f32[32,256]{1,0:T(8,128)S(1)}, u32[]{:S(2)}, u32[]{:S(2)}) collective-permute-start(f32[32,256]{1,0:T(8,128)S(1)} %get-tuple-element.39), channel_id=1, source_target_pairs={{0,6},{1,7},{2,0},{3,1},{4,2},{5,3},{6,4},{7,5},{8,14},{9,15},{10,... | collective-permute-start | bytes 98312 | tf_op jit(solution)/shard_map/ppermute | solution.py:395
  31.3 1.3 %collective-permute-done.2.refs_2_ = f32[256,256]{1,0:T(8,128)} collective-permute-done((f32[256,256]{1,0:T(8,128)}, f32[256,256]{1,0:T(8,128)}, u32[]{:S(2)}, u32[]{:S(2)}) %collective-permute-start.2) | collective-permute-done | bytes 262176 | tf_op jit(solution)/shard_map/ppermute | solution.py:372
  32.6 1.9 %collective-permute-done.1.refs_1_ = f32[256,256]{1,0:T(8,128)} collective-permute-done((f32[256,256]{1,0:T(8,128)}, f32[256,256]{1,0:T(8,128)}, u32[]{:S(2)}, u32[]{:S(2)}) %collective-permute-start.1) | collective-permute-done | bytes 262176 | tf_op jit(solution)/shard_map/ppermute | solution.py:372
  34.4 0.6 collective-permute-done.5.refs_5_
  35.0 0.5 collective-permute-done.7.refs_7_
  35.6 2.2 %line.1 = (f32[3,256,256]{2,1,0:T(8,128)S(1)}, f32[256,256]{1,0:T(8,128)S(1)}, f32[3,32,256]{2,1,0:T(8,128)S(1)}, f32[160,256]{1,0:T(8,128)S(1)}) custom-call(f32[256,256]{1,0:T(8,128)} %get-tuple-element.33.refs_0_, f32[256,256]{1,0:T(8,128)} %collective-permute-done.1.refs_1_, f32[256,256]{1,0:T(8,128)} %collective-permute-done.2.refs_2_, ...), custom_call_target="tpu_custom_call" | custom-call | flops 335544320 | bytes 2490368 | tf_op jit(solution)/shard_map/line/pallas_call | solution.py:51
  37.7 1.3 %collective-permute-start.10 = (f32[160,256]{1,0:T(8,128)S(1)}, f32[160,256]{1,0:T(8,128)S(1)}, u32[]{:S(2)}, u32[]{:S(2)}) collective-permute-start(f32[160,256]{1,0:T(8,128)S(1)} %get-tuple-element.42.refs_1_), channel_id=1, source_target_pairs={{0,16},{1,17},{2,18},{3,19},{4,20},{5,21},{6,22},{7,23},{8,24},{9,... | collective-permute-start | bytes 491528 | tf_op jit(solution)/shard_map/ppermute | solution.py:407
  39.0 1.1 %collective-permute-start.9 = (f32[160,256]{1,0:T(8,128)S(1)}, f32[160,256]{1,0:T(8,128)S(1)}, u32[]{:S(2)}, u32[]{:S(2)}) collective-permute-start(f32[160,256]{1,0:T(8,128)S(1)} %get-tuple-element.42.refs_1_), channel_id=1, source_target_pairs={{0,24},{1,25},{2,26},{3,27},{4,28},{5,29},{6,30},{7,31},{8,0},{9,1... | collective-permute-start | bytes 491528 | tf_op jit(solution)/shard_map/ppermute | solution.py:407
  40.1 0.4 collective-permute-start.8
  40.5 3.0 %collective-permute-done.10.refs_4_ = f32[160,256]{1,0:T(8,128)S(1)} collective-permute-done((f32[160,256]{1,0:T(8,128)S(1)}, f32[160,256]{1,0:T(8,128)S(1)}, u32[]{:S(2)}, u32[]{:S(2)}) %collective-permute-start.10) | collective-permute-done | bytes 163872 | tf_op jit(solution)/shard_map/ppermute | solution.py:407
  43.5 4.3 %collective-permute-start.13 = (f32[160,256]{1,0:T(8,128)S(1)}, f32[160,256]{1,0:T(8,128)S(1)}, u32[]{:S(2)}, u32[]{:S(2)}) collective-permute-start(f32[160,256]{1,0:T(8,128)S(1)} %collective-permute-done.10.refs_4_), channel_id=1, source_target_pairs={{0,1},{1,0},{2,3},{3,2},{4,5},{5,4},{6,7},{7,6},{8,9},{9,8},{10,11... | collective-permute-start | bytes 491528 | tf_op jit(solution)/shard_map/ppermute | solution.py:408
  47.8 1.9 %collective-permute-start.11 = (f32[160,256]{1,0:T(8,128)S(1)}, f32[160,256]{1,0:T(8,128)S(1)}, u32[]{:S(2)}, u32[]{:S(2)}) collective-permute-start(f32[160,256]{1,0:T(8,128)S(1)} %collective-permute-done.8.refs_2_), channel_id=1, source_target_pairs={{0,1},{1,0},{2,3},{3,2},{4,5},{5,4},{6,7},{7,6},{8,9},{9,8},{10,11... | collective-permute-start | bytes 491528 | tf_op jit(solution)/shard_map/ppermute | solution.py:408
  49.7 1.0 %collective-permute-done.11.refs_5_ = f32[160,256]{1,0:T(8,128)S(1)} collective-permute-done((f32[160,256]{1,0:T(8,128)S(1)}, f32[160,256]{1,0:T(8,128)S(1)}, u32[]{:S(2)}, u32[]{:S(2)}) %collective-permute-start.11) | collective-permute-done | bytes 163872 | tf_op jit(solution)/shard_map/ppermute | solution.py:408
  50.7 1.4 %group.1 = (f32[4,256,256]{2,1,0:T(8,128)S(1)}, bf16[256,256]{1,0:T(8,128)(2,1)S(1)}, bf16[256,256]{1,0:T(8,128)(2,1)S(1)}, f32[4,32,256]{2,1,0:T(8,128)S(1)}, f32[32,256]{1,0:T(8,128)S(1)}) custom-call(f32[256,256]{1,0:T(8,128)S(1)} %get-tuple-element.41.refs_0_, f32[160,256]{1,0:T(8,128)S(1)} %get-tuple-element.42.refs_1_, ...), custom_call_target="tpu_custom_call" | custom-call | flops 671088640 | bytes 4030464 | tf_op jit(solution)/shard_map/group/pallas_call | solution.py:51
  52.2 0.7 collective-permute-start.14
  52.9 0.2 hop.6
  53.1 0.7 collective-permute-start.15
  53.8 0.2 hop.7
  53.9 0.7 collective-permute-start.16
  54.8 0.7 collective-permute-start.17
  55.5 0.2 hop.9
  55.6 0.7 collective-permute-start.18
  56.5 0.7 collective-permute-start.19
  57.3 1.3 %collective-permute-start.20 = (f32[32,256]{1,0:T(8,128)S(1)}, f32[32,256]{1,0:T(8,128)S(1)}, u32[]{:S(2)}, u32[]{:S(2)}) collective-permute-start(f32[32,256]{1,0:T(8,128)S(1)} %hop.11), channel_id=1, source_target_pairs={{192,224},{193,225},{194,226},{195,227},{196,228},{197,229},{198,2... | collective-permute-start | bytes 98312 | tf_op jit(solution)/shard_map/ppermute | solution.py:429
  58.6 16.4 %collective-permute-done.20.refs_7_ = f32[32,256]{1,0:T(8,128)S(1)} collective-permute-done((f32[32,256]{1,0:T(8,128)S(1)}, f32[32,256]{1,0:T(8,128)S(1)}, u32[]{:S(2)}, u32[]{:S(2)}) %collective-permute-start.20) | collective-permute-done | bytes 32800 | tf_op jit(solution)/shard_map/ppermute | solution.py:429
  75.1 0.3 chips.1
  75.5 2.7 %collective-permute-start.22 = (f32[32,256]{1,0:T(8,128)S(1)}, f32[32,256]{1,0:T(8,128)S(1)}, u32[]{:S(2)}, u32[]{:S(2)}) collective-permute-start(f32[32,256]{1,0:T(8,128)S(1)} %get-tuple-element.52), channel_id=1, source_target_pairs={{0,6},{1,7},{2,0},{3,1},{4,2},{5,3},{6,4},{7,5},{8,14},{9,15},{10,... | collective-permute-start | bytes 98312 | tf_op jit(solution)/shard_map/ppermute | solution.py:441
  78.1 1.3 %collective-permute-done.21.refs_1_ = f32[32,256]{1,0:T(8,128)S(1)} collective-permute-done((f32[32,256]{1,0:T(8,128)S(1)}, f32[32,256]{1,0:T(8,128)S(1)}, u32[]{:S(2)}, u32[]{:S(2)}) %collective-permute-start.21) | collective-permute-done | bytes 32800 | tf_op jit(solution)/shard_map/ppermute | solution.py:441
  79.4 3.0 %collective-permute-done.23.refs_3_ = f32[32,256]{1,0:T(8,128)S(1)} collective-permute-done((f32[32,256]{1,0:T(8,128)S(1)}, f32[32,256]{1,0:T(8,128)S(1)}, u32[]{:S(2)}, u32[]{:S(2)}) %collective-permute-start.23) | collective-permute-done | bytes 32800 | tf_op jit(solution)/shard_map/ppermute | solution.py:441
  82.4 0.2 chip_start.1
  82.6 8.5 %collective-permute-start.24 = (f32[128,256]{1,0:T(8,128)S(1)}, f32[128,256]{1,0:T(8,128)S(1)}, u32[]{:S(2)}, u32[]{:S(2)}) collective-permute-start(f32[128,256]{1,0:T(8,128)S(1)} %get-tuple-element.56), channel_id=1, source_target_pairs={{0,1},{1,0},{2,3},{3,2},{4,5},{5,4},{6,7},{7,6},{8,9},{9,8},{10,11... | collective-permute-start | bytes 393224 | tf_op jit(solution)/shard_map/ppermute | solution.py:453
  91.2 1.0 %collective-permute-done.24.refs_1_ = f32[128,256]{1,0:T(8,128)S(1)} collective-permute-done((f32[128,256]{1,0:T(8,128)S(1)}, f32[128,256]{1,0:T(8,128)S(1)}, u32[]{:S(2)}, u32[]{:S(2)}) %collective-permute-start.24) | collective-permute-done | bytes 131104 | tf_op jit(solution)/shard_map/ppermute | solution.py:453
  92.2 1.1 %finish.1 = (f32[8,256]{1,0:T(8,128)}, f32[256,256]{1,0:T(8,128)}) custom-call(f32[128,256]{1,0:T(8,128)S(1)} %get-tuple-element.55.refs_0_, f32[128,256]{1,0:T(8,128)S(1)} %collective-permute-done.24.refs_1_, f32[256,256]{1,0:T(8,128)S(1)} %get-tuple-element.32.refs_0_.refs_2_, f32[256,256]{1,0:T(8,128)S(1)} %get-tuple-element.57.refs_3_, ...), custom_call_target="tpu_custom_call" | custom-call | flops 100663296 | bytes 1073152 | tf_op jit(solution)/shard_map/finish/pallas_call | solution.py:51
  (33 shorter events, 1.0 us)
Async XLA Ops:
  0.6 9.9 %copy-start.1 = (f32[8,256,256]{2,1,0:T(8,128)S(1)}, f32[8,256,256]{2,1,0:T(8,128)}, u32[]{:S(2)}) copy-start(f32[8,256,256]{2,1,0:T(8,128)} %refs_2_.1) | copy-start | bytes 6291460
  0.6 9.9 %copy-start.3 = (f32[8,256]{1,0:T(8,128)S(1)}, f32[8,256]{1,0:T(8,128)}, u32[]{:S(2)}) copy-start(f32[8,256]{1,0:T(8,128)} %refs_1_.3) | copy-start | bytes 24580
  0.7 9.9 %copy-start.4 = (f32[256]{0:T(256)S(1)}, f32[256]{0:T(256)}, u32[]{:S(2)}) copy-start(f32[256]{0:T(256)} %param.11) | copy-start | bytes 3076
  2.8 20.8 %all-to-all-start = ((f32[32,8,640]{2,1,0:T(8,128)}), f32[32,8,640]{2,1,0:T(8,128)S(1)}, u32[]{:S(2)}, u32[]{:S(2)}) async-start(f32[32,8,640]{2,1,0:T(8,128)} %pack.1.refs_3_), calls=%async_computation | async-start | bytes 1310720 | tf_op jit(solution)/shard_map/all_to_all | solution.py:356
  10.6 1.1 %copy-start = (f32[32,8,640]{2,1,0:T(8,128)S(1)}, f32[32,8,640]{2,1,0:T(8,128)}, u32[]{:S(2)}) copy-start(f32[32,8,640]{2,1,0:T(8,128)} %pack.1.refs_3_) | copy-start | bytes 1966084
  13.9 1.6 %collective-permute-start = (f32[256,256]{1,0:T(8,128)S(1)}, f32[256,256]{1,0:T(8,128)S(1)}, u32[]{:S(2)}, u32[]{:S(2)}) collective-permute-start(f32[256,256]{1,0:T(8,128)S(1)} %get-tuple-element.32.refs_0_.refs_2_), channel_id=1, source_target_pairs={{0,1},{1,0},{2,3},{3,2},{4,5},{5,4},{6,7},{7,6},{8,9},{9,8},{10,11... | collective-permute-start | bytes 786440 | tf_op jit(solution)/shard_map/ppermute | solution.py:370
  16.5 14.8 %collective-permute-start.3 = (f32[256,256]{1,0:T(8,128)}, f32[256,256]{1,0:T(8,128)}, u32[]{:S(2)}, u32[]{:S(2)}) collective-permute-start(f32[256,256]{1,0:T(8,128)} %get-tuple-element.33.refs_0_), channel_id=1, source_target_pairs={{0,4},{1,5},{2,6},{3,7},{4,0},{5,1},{6,2},{7,3},{8,12},{9,13},{10,... | collective-permute-start | bytes 786440 | tf_op jit(solution)/shard_map/ppermute | solution.py:372
  19.4 13.2 %collective-permute-start.2 = (f32[256,256]{1,0:T(8,128)}, f32[256,256]{1,0:T(8,128)}, u32[]{:S(2)}, u32[]{:S(2)}) collective-permute-start(f32[256,256]{1,0:T(8,128)} %get-tuple-element.33.refs_0_), channel_id=1, source_target_pairs={{0,6},{1,7},{2,0},{3,1},{4,2},{5,3},{6,4},{7,5},{8,14},{9,15},{10,... | collective-permute-start | bytes 786440 | tf_op jit(solution)/shard_map/ppermute | solution.py:372
  20.3 14.2 %collective-permute-start.1 = (f32[256,256]{1,0:T(8,128)}, f32[256,256]{1,0:T(8,128)}, u32[]{:S(2)}, u32[]{:S(2)}) collective-permute-start(f32[256,256]{1,0:T(8,128)} %get-tuple-element.33.refs_0_), channel_id=1, source_target_pairs={{0,2},{1,3},{2,4},{3,5},{4,6},{5,7},{6,0},{7,1},{8,10},{9,11},{10,... | collective-permute-start | bytes 786440 | tf_op jit(solution)/shard_map/ppermute | solution.py:372
  23.6 0.7 copy-start.5
  26.9 1.4 %collective-permute-start.4 = (f32[128,256]{1,0:T(8,128)S(1)}, f32[128,256]{1,0:T(8,128)S(1)}, u32[]{:S(2)}, u32[]{:S(2)}) collective-permute-start(f32[128,256]{1,0:T(8,128)S(1)} %get-tuple-element.35), channel_id=1, source_target_pairs={{0,1},{1,0},{2,3},{3,2},{4,5},{5,4},{6,7},{7,6},{8,9},{9,8},{10,11... | collective-permute-start | bytes 393224 | tf_op jit(solution)/shard_map/ppermute | solution.py:383
  28.3 23.8 %copy-start.2 = (f32[256,256]{1,0:T(8,128)S(1)}, f32[256,256]{1,0:T(8,128)}, u32[]{:S(2)}) copy-start(f32[256,256]{1,0:T(8,128)} %refs_0_.5) | copy-start | bytes 786436
  28.5 6.5 %collective-permute-start.5 = (f32[32,256]{1,0:T(8,128)S(1)}, f32[32,256]{1,0:T(8,128)S(1)}, u32[]{:S(2)}, u32[]{:S(2)}) collective-permute-start(f32[32,256]{1,0:T(8,128)S(1)} %get-tuple-element.38), channel_id=1, source_target_pairs={{0,2},{1,3},{2,4},{3,5},{4,6},{5,7},{6,0},{7,1},{8,10},{9,11},{10,... | collective-permute-start | bytes 98312 | tf_op jit(solution)/shard_map/ppermute | solution.py:395
  28.6 6.4 %collective-permute-start.6 = (f32[32,256]{1,0:T(8,128)S(1)}, f32[32,256]{1,0:T(8,128)S(1)}, u32[]{:S(2)}, u32[]{:S(2)}) collective-permute-start(f32[32,256]{1,0:T(8,128)S(1)} %get-tuple-element.39), channel_id=1, source_target_pairs={{0,6},{1,7},{2,0},{3,1},{4,2},{5,3},{6,4},{7,5},{8,14},{9,15},{10,... | collective-permute-start | bytes 98312 | tf_op jit(solution)/shard_map/ppermute | solution.py:395
  31.3 4.3 %collective-permute-start.7 = (f32[32,256]{1,0:T(8,128)S(1)}, f32[32,256]{1,0:T(8,128)S(1)}, u32[]{:S(2)}, u32[]{:S(2)}) collective-permute-start(f32[32,256]{1,0:T(8,128)S(1)} %get-tuple-element.40), channel_id=1, source_target_pairs={{0,4},{1,5},{2,6},{3,7},{4,0},{5,1},{6,2},{7,3},{8,12},{9,13},{10,... | collective-permute-start | bytes 98312 | tf_op jit(solution)/shard_map/ppermute | solution.py:395
  37.7 5.8 %collective-permute-start.10 = (f32[160,256]{1,0:T(8,128)S(1)}, f32[160,256]{1,0:T(8,128)S(1)}, u32[]{:S(2)}, u32[]{:S(2)}) collective-permute-start(f32[160,256]{1,0:T(8,128)S(1)} %get-tuple-element.42.refs_1_), channel_id=1, source_target_pairs={{0,16},{1,17},{2,18},{3,19},{4,20},{5,21},{6,22},{7,23},{8,24},{9,... | collective-permute-start | bytes 491528 | tf_op jit(solution)/shard_map/ppermute | solution.py:407
  39.0 8.8 %collective-permute-start.9 = (f32[160,256]{1,0:T(8,128)S(1)}, f32[160,256]{1,0:T(8,128)S(1)}, u32[]{:S(2)}, u32[]{:S(2)}) collective-permute-start(f32[160,256]{1,0:T(8,128)S(1)} %get-tuple-element.42.refs_1_), channel_id=1, source_target_pairs={{0,24},{1,25},{2,26},{3,27},{4,28},{5,29},{6,30},{7,31},{8,0},{9,1... | collective-permute-start | bytes 491528 | tf_op jit(solution)/shard_map/ppermute | solution.py:407
  40.1 7.7 %collective-permute-start.8 = (f32[160,256]{1,0:T(8,128)S(1)}, f32[160,256]{1,0:T(8,128)S(1)}, u32[]{:S(2)}, u32[]{:S(2)}) collective-permute-start(f32[160,256]{1,0:T(8,128)S(1)} %get-tuple-element.42.refs_1_), channel_id=1, source_target_pairs={{0,8},{1,9},{2,10},{3,11},{4,12},{5,13},{6,14},{7,15},{8,16},{9,17... | collective-permute-start | bytes 491528 | tf_op jit(solution)/shard_map/ppermute | solution.py:407
  43.5 6.2 %collective-permute-start.13 = (f32[160,256]{1,0:T(8,128)S(1)}, f32[160,256]{1,0:T(8,128)S(1)}, u32[]{:S(2)}, u32[]{:S(2)}) collective-permute-start(f32[160,256]{1,0:T(8,128)S(1)} %collective-permute-done.10.refs_4_), channel_id=1, source_target_pairs={{0,1},{1,0},{2,3},{3,2},{4,5},{5,4},{6,7},{7,6},{8,9},{9,8},{10,11... | collective-permute-start | bytes 491528 | tf_op jit(solution)/shard_map/ppermute | solution.py:408
  47.8 1.9 %collective-permute-start.12 = (f32[160,256]{1,0:T(8,128)S(1)}, f32[160,256]{1,0:T(8,128)S(1)}, u32[]{:S(2)}, u32[]{:S(2)}) collective-permute-start(f32[160,256]{1,0:T(8,128)S(1)} %collective-permute-done.9.refs_3_), channel_id=1, source_target_pairs={{0,1},{1,0},{2,3},{3,2},{4,5},{5,4},{6,7},{7,6},{8,9},{9,8},{10,11... | collective-permute-start | bytes 491528 | tf_op jit(solution)/shard_map/ppermute | solution.py:408
  47.8 2.9 %collective-permute-start.11 = (f32[160,256]{1,0:T(8,128)S(1)}, f32[160,256]{1,0:T(8,128)S(1)}, u32[]{:S(2)}, u32[]{:S(2)}) collective-permute-start(f32[160,256]{1,0:T(8,128)S(1)} %collective-permute-done.8.refs_2_), channel_id=1, source_target_pairs={{0,1},{1,0},{2,3},{3,2},{4,5},{5,4},{6,7},{7,6},{8,9},{9,8},{10,11... | collective-permute-start | bytes 491528 | tf_op jit(solution)/shard_map/ppermute | solution.py:408
  52.2 0.7 collective-permute-start.14
  53.1 0.7 collective-permute-start.15
  53.9 0.7 collective-permute-start.16
  54.8 0.7 collective-permute-start.17
  55.6 0.7 collective-permute-start.18
  56.5 0.7 collective-permute-start.19
  57.3 17.7 %collective-permute-start.20 = (f32[32,256]{1,0:T(8,128)S(1)}, f32[32,256]{1,0:T(8,128)S(1)}, u32[]{:S(2)}, u32[]{:S(2)}) collective-permute-start(f32[32,256]{1,0:T(8,128)S(1)} %hop.11), channel_id=1, source_target_pairs={{192,224},{193,225},{194,226},{195,227},{196,228},{197,229},{198,2... | collective-permute-start | bytes 98312 | tf_op jit(solution)/shard_map/ppermute | solution.py:429
  75.4 4.1 %collective-permute-start.21 = (f32[32,256]{1,0:T(8,128)S(1)}, f32[32,256]{1,0:T(8,128)S(1)}, u32[]{:S(2)}, u32[]{:S(2)}) collective-permute-start(f32[32,256]{1,0:T(8,128)S(1)} %get-tuple-element.51), channel_id=1, source_target_pairs={{0,2},{1,3},{2,4},{3,5},{4,6},{5,7},{6,0},{7,1},{8,10},{9,11},{10,... | collective-permute-start | bytes 98312 | tf_op jit(solution)/shard_map/ppermute | solution.py:441
  75.5 4.0 %collective-permute-start.22 = (f32[32,256]{1,0:T(8,128)S(1)}, f32[32,256]{1,0:T(8,128)S(1)}, u32[]{:S(2)}, u32[]{:S(2)}) collective-permute-start(f32[32,256]{1,0:T(8,128)S(1)} %get-tuple-element.52), channel_id=1, source_target_pairs={{0,6},{1,7},{2,0},{3,1},{4,2},{5,3},{6,4},{7,5},{8,14},{9,15},{10,... | collective-permute-start | bytes 98312 | tf_op jit(solution)/shard_map/ppermute | solution.py:441
  78.1 4.3 %collective-permute-start.23 = (f32[32,256]{1,0:T(8,128)S(1)}, f32[32,256]{1,0:T(8,128)S(1)}, u32[]{:S(2)}, u32[]{:S(2)}) collective-permute-start(f32[32,256]{1,0:T(8,128)S(1)} %get-tuple-element.53), channel_id=1, source_target_pairs={{0,4},{1,5},{2,6},{3,7},{4,0},{5,1},{6,2},{7,3},{8,12},{9,13},{10,... | collective-permute-start | bytes 98312 | tf_op jit(solution)/shard_map/ppermute | solution.py:441
  82.6 9.5 %collective-permute-start.24 = (f32[128,256]{1,0:T(8,128)S(1)}, f32[128,256]{1,0:T(8,128)S(1)}, u32[]{:S(2)}, u32[]{:S(2)}) collective-permute-start(f32[128,256]{1,0:T(8,128)S(1)} %get-tuple-element.56), channel_id=1, source_target_pairs={{0,1},{1,0},{2,3},{3,2},{4,5},{5,4},{6,7},{7,6},{8,9},{9,8},{10,11... | collective-permute-start | bytes 393224 | tf_op jit(solution)/shard_map/ppermute | solution.py:453

commit v8 on v7

--- a/solution.py
+++ b/solution.py
@@ -169,7 +169,7 @@
 
 
 def line_kernel(
-    pos, a0, a1, a3, a2, b0, b1, b3, b2, prefix, line, before, packet, maps, shifts
+    pos, a0, a1, a3, a2, b0, b2, b1, b3, prefix, line, before, packet, maps, shifts
 ):
     order(pos[1], NY, maps, (a0, a1, a3, a2))
     order(pos[1], NY, shifts, (b0, b1, b3, b2))
@@ -285,7 +285,7 @@
         out[...] = chips[lax.rem(y + s, NY)]
 
 
-def chip_kernel(pos, e0, e1, e3, e2, both, first, kept, sent, chip):
+def chip_kernel(pos, e0, e2, e1, e3, both, first, kept, sent, chip):
     c, y = pos[0], pos[1]
     r = e0.shape[0]
     for s, ref in zip((0,) + SHIFTS, (e0, e1, e3, e2)):
@@ -400,7 +400,9 @@
         chip,
         *chips,
         rows[0],
-        *got,
+        got[2],
+        got[0],
+        got[1],
         scratch=[vm(NY, *mat), vm(NY, *small)],
         flops=10 * cube,
     )
@@ -444,7 +446,9 @@
         "chip_start",
         [(half, modes)] * 2,
         rows[0],
-        *got,
+        got[2],
+        got[0],
+        got[1],
         both,
         first,
         scratch=[vm(half, modes)],

time: 93.6 us -> 91.6 us (0.979)
  waiting for transfers between devices: 35.4 us -> 32.9 us
    ppermute x6, waiting for transfers between devices: 5.4 us -> 2.33 us  [body(): got = [lax.ppermute(r, 'tm', along_y(s)) for r, s in zip(rows[1:], SHIFTS)]]
    ppermute x6, starting transfers between devices: 5.5 us -> 7.62 us  [body(): got = [lax.ppermute(r, 'tm', along_y(s)) for r, s in zip(rows[1:], SHIFTS)]]
    ppermute x3, starting transfers between devices: 6.16 us -> 4.25 us  [body(): swapped = [lax.ppermute(p, 'tm', swap) for p in packets]]
    ppermute x3, waiting for transfers between devices: 3.04 us -> 4.43 us  [body(): packets = [lax.ppermute(packet, 'tm', along_x(s)) for s in SHIFTS]]
  transfers between devices with their start and end apart: 26 -> 26, of which waited for: 13 -> 14; matrix products, arithmetic and copies ran while one was open for 0% -> 0% of each run, Pallas kernels for 6% -> 7%
where the time goes in v8:
time: 91.6 us; the launch traced here: 91 us
  starting transfers between devices  41 us (45%)
  waiting for transfers between devices  32.9 us (36%)
  Pallas kernels  14.4 us (16%)
  local copies, waits for them, and re-layouts  1.81 us (2%)
  between operations  0.94 us (1%)
    ppermute x6, waiting for transfers between devices, body(): carried.append(lax.ppermute(e, 'grp', [(k, k + 1)]))  16.4 us
    pallas_call x16, Pallas kernels, call(): pl.pallas_call(run, out_shape=shapes, in_specs=[vmem] * n_args + [pl.Bloc...  12.3 us
    ppermute x2, starting transfers between devices, body(): back = lax.ppermute(sent, 'tm', swap)  8.34 us
    all_to_all x1, starting transfers between devices, body(): arrived = lax.all_to_all(packed, 'tm', split_axis=0, concat_axis=0)  7.77 us
    ppermute x6, starting transfers between devices, body(): got = [lax.ppermute(r, 'tm', along_y(s)) for r, s in zip(rows[1:], SHIFTS)]  7.62 us
    ppermute x6, starting transfers between devices, body(): carried.append(lax.ppermute(e, 'grp', [(k, k + 1)]))  4.61 us
    ppermute x3, waiting for transfers between devices, body(): packets = [lax.ppermute(packet, 'tm', along_x(s)) for s in SHIFTS]  4.43 us
    ppermute x3, starting transfers between devices, body(): chips = [lax.ppermute(chip, 'tm', along_y(s)) for s in SHIFTS]  4.36 us
  transfers between devices with their start and end apart: 26, of which 14 were waited for; matrix products, arithmetic and copies ran while one was open for 0% of the time, Pallas kernels for 7%

profile of v8, /device:TPU:225, one launch (start us, length us, event | category | flops | bytes accessed | tf_op | source)
XLA Modules:
  0.0 91.0 jit_solution(16979603069702004781)
XLA Ops:
  0.7 2.1 %pack.1.refs_3_ = f32[32,8,640]{2,1,0:T(8,128)} custom-call(f32[32,16,256]{2,1,0:T(8,128)} %bitcast.11, s32[16,32]{1,0:T(8,128)} %bitcast.13, s32[16,32]{1,0:T(8,128)} %bitcast.14, s32[1,32]{1,0:T(1,128)} %counts.1), custom_call_target="tpu_custom_call" | custom-call | flops 3000000000 | bytes 1048576 | tf_op jit(solution)/shard_map/pack/pallas_call | solution.py:342
  2.8 7.8 %all-to-all-start = ((f32[32,8,640]{2,1,0:T(8,128)}), f32[32,8,640]{2,1,0:T(8,128)S(1)}, u32[]{:S(2)}, u32[]{:S(2)}) async-start(f32[32,8,640]{2,1,0:T(8,128)} %pack.1.refs_3_), calls=%async_computation | async-start | bytes 1310720 | tf_op jit(solution)/shard_map/all_to_all | solution.py:356
  10.6 1.1 %copy-done = f32[32,8,640]{2,1,0:T(8,128)S(1)} copy-done((f32[32,8,640]{2,1,0:T(8,128)S(1)}, f32[32,8,640]{2,1,0:T(8,128)}, u32[]{:S(2)}) %copy-start) | copy-done | bytes 655384
  11.7 2.1 %compose.1 = (f32[256,256]{1,0:T(8,128)S(1)}, f32[8,256]{1,0:T(8,128)S(1)}) custom-call(f32[8,256]{1,0:T(8,128)S(1)} %copy-done.3, f32[8,256,256]{2,1,0:T(8,128)S(1)} %copy-done.1, f32[1,256]{1,0:T(1,128)S(1)} %bitcast.9, f32[32,8,640]{2,1,0:T(8,128)S(1)} %copy-done), custom_call_target="tpu_custom_call" | custom-call | flops 738197504 | bytes 2376704 | tf_op jit(solution)/shard_map/compose/pallas_call | solution.py:51
  13.9 0.3 collective-permute-start
  14.2 1.3 %collective-permute-done.refs_1_ = f32[256,256]{1,0:T(8,128)S(1)} collective-permute-done((f32[256,256]{1,0:T(8,128)S(1)}, f32[256,256]{1,0:T(8,128)S(1)}, u32[]{:S(2)}, u32[]{:S(2)}) %collective-permute-start) | collective-permute-done | bytes 262176 | tf_op jit(solution)/shard_map/ppermute | solution.py:370
  15.5 1.0 %pair_map.1 = (f32[2,256,256]{2,1,0:T(8,128)S(1)}, f32[256,256]{1,0:T(8,128)}) custom-call(f32[256,256]{1,0:T(8,128)S(1)} %get-tuple-element.32.refs_0_.refs_2_, f32[256,256]{1,0:T(8,128)S(1)} %collective-permute-done.refs_1_), custom_call_target="tpu_custom_call" | custom-call | flops 100663296 | bytes 1310720 | tf_op jit(solution)/shard_map/pair_map/pallas_call | solution.py:51
  16.5 2.9 %collective-permute-start.3 = (f32[256,256]{1,0:T(8,128)}, f32[256,256]{1,0:T(8,128)}, u32[]{:S(2)}, u32[]{:S(2)}) collective-permute-start(f32[256,256]{1,0:T(8,128)} %get-tuple-element.33.refs_0_), channel_id=1, source_target_pairs={{0,4},{1,5},{2,6},{3,7},{4,0},{5,1},{6,2},{7,3},{8,12},{9,13},{10,... | collective-permute-start | bytes 786440 | tf_op jit(solution)/shard_map/ppermute | solution.py:372
  19.4 0.9 collective-permute-start.2
  20.3 0.6 collective-permute-start.1
  20.8 2.7 %all-to-all-done.refs_0_ = f32[32,8,640]{2,1,0:T(8,128)S(1)} async-done(((f32[32,8,640]{2,1,0:T(8,128)}), f32[32,8,640]{2,1,0:T(8,128)S(1)}, u32[]{:S(2)}, u32[]{:S(2)}) %all-to-all-start) | async-done | bytes 655392 | tf_op jit(solution)/shard_map/all_to_all | solution.py:356
  23.6 0.7 copy-done.5
  24.2 2.6 %drive.1 = (f32[256,256]{1,0:T(8,128)S(1)}, f32[128,256]{1,0:T(8,128)S(1)}, f32[128,256]{1,0:T(8,128)S(1)}, f32[8,256]{1,0:T(8,128)S(1)}) custom-call(f32[32,8,640]{2,1,0:T(8,128)S(1)} %all-to-all-done.refs_0_, f32[8,256]{1,0:T(8,128)S(1)} %copy-done.3, f32[8,256,256]{2,1,0:T(8,128)S(1)} %copy-done.1, f32[1,256]{1,0:T(1,128)S(1)} %bitcast.10), custom_call_target="tpu_custom_call" | custom-call | flops 2013265920 | bytes 3294208 | tf_op jit(solution)/shard_map/drive/pallas_call | solution.py:51
  27.0 1.3 %collective-permute-done.4.refs_1_ = f32[128,256]{1,0:T(8,128)S(1)} collective-permute-done((f32[128,256]{1,0:T(8,128)S(1)}, f32[128,256]{1,0:T(8,128)S(1)}, u32[]{:S(2)}, u32[]{:S(2)}) %collective-permute-start.4) | collective-permute-done | bytes 131104 | tf_op jit(solution)/shard_map/ppermute | solution.py:383
  28.5 1.0 %collective-permute-start.5 = (f32[32,256]{1,0:T(8,128)S(1)}, f32[32,256]{1,0:T(8,128)S(1)}, u32[]{:S(2)}, u32[]{:S(2)}) collective-permute-start(f32[32,256]{1,0:T(8,128)S(1)} %get-tuple-element.38), channel_id=1, source_target_pairs={{0,4},{1,5},{2,6},{3,7},{4,0},{5,1},{6,2},{7,3},{8,12},{9,13},{10,... | collective-permute-start | bytes 98312 | tf_op jit(solution)/shard_map/ppermute | solution.py:395
  29.6 0.8 collective-permute-start.6
  30.4 1.8 %collective-permute-start.7 = (f32[32,256]{1,0:T(8,128)S(1)}, f32[32,256]{1,0:T(8,128)S(1)}, u32[]{:S(2)}, u32[]{:S(2)}) collective-permute-start(f32[32,256]{1,0:T(8,128)S(1)} %get-tuple-element.40), channel_id=1, source_target_pairs={{0,6},{1,7},{2,0},{3,1},{4,2},{5,3},{6,4},{7,5},{8,14},{9,15},{10,... | collective-permute-start | bytes 98312 | tf_op jit(solution)/shard_map/ppermute | solution.py:395
  32.2 0.3 collective-permute-done.2.refs_2_
  32.6 2.1 %collective-permute-done.1.refs_1_ = f32[256,256]{1,0:T(8,128)} collective-permute-done((f32[256,256]{1,0:T(8,128)}, f32[256,256]{1,0:T(8,128)}, u32[]{:S(2)}, u32[]{:S(2)}) %collective-permute-start.1) | collective-permute-done | bytes 262176 | tf_op jit(solution)/shard_map/ppermute | solution.py:372
  34.7 1.0 %collective-permute-done.6.refs_6_ = f32[32,256]{1,0:T(8,128)S(1)} collective-permute-done((f32[32,256]{1,0:T(8,128)S(1)}, f32[32,256]{1,0:T(8,128)S(1)}, u32[]{:S(2)}, u32[]{:S(2)}) %collective-permute-start.6) | collective-permute-done | bytes 32800 | tf_op jit(solution)/shard_map/ppermute | solution.py:395
  35.7 2.2 %line.1 = (f32[3,256,256]{2,1,0:T(8,128)S(1)}, f32[256,256]{1,0:T(8,128)S(1)}, f32[3,32,256]{2,1,0:T(8,128)S(1)}, f32[160,256]{1,0:T(8,128)S(1)}) custom-call(f32[256,256]{1,0:T(8,128)} %get-tuple-element.33.refs_0_, f32[256,256]{1,0:T(8,128)} %collective-permute-done.1.refs_1_, f32[256,256]{1,0:T(8,128)} %collective-permute-done.2.refs_2_, ...), custom_call_target="tpu_custom_call" | custom-call | flops 335544320 | bytes 2490368 | tf_op jit(solution)/shard_map/line/pallas_call | solution.py:51
  37.9 1.6 %collective-permute-start.10 = (f32[160,256]{1,0:T(8,128)S(1)}, f32[160,256]{1,0:T(8,128)S(1)}, u32[]{:S(2)}, u32[]{:S(2)}) collective-permute-start(f32[160,256]{1,0:T(8,128)S(1)} %get-tuple-element.42.refs_1_), channel_id=1, source_target_pairs={{0,16},{1,17},{2,18},{3,19},{4,20},{5,21},{6,22},{7,23},{8,24},{9,... | collective-permute-start | bytes 491528 | tf_op jit(solution)/shard_map/ppermute | solution.py:409
  39.5 0.9 collective-permute-start.9
  40.3 0.6 collective-permute-start.8
  40.9 4.0 %collective-permute-done.10.refs_4_ = f32[160,256]{1,0:T(8,128)S(1)} collective-permute-done((f32[160,256]{1,0:T(8,128)S(1)}, f32[160,256]{1,0:T(8,128)S(1)}, u32[]{:S(2)}, u32[]{:S(2)}) %collective-permute-start.10) | collective-permute-done | bytes 163872 | tf_op jit(solution)/shard_map/ppermute | solution.py:409
  44.9 2.0 %collective-permute-start.13 = (f32[160,256]{1,0:T(8,128)S(1)}, f32[160,256]{1,0:T(8,128)S(1)}, u32[]{:S(2)}, u32[]{:S(2)}) collective-permute-start(f32[160,256]{1,0:T(8,128)S(1)} %collective-permute-done.10.refs_4_), channel_id=1, source_target_pairs={{0,1},{1,0},{2,3},{3,2},{4,5},{5,4},{6,7},{7,6},{8,9},{9,8},{10,11... | collective-permute-start | bytes 491528 | tf_op jit(solution)/shard_map/ppermute | solution.py:410
  47.1 1.3 %collective-permute-start.12 = (f32[160,256]{1,0:T(8,128)S(1)}, f32[160,256]{1,0:T(8,128)S(1)}, u32[]{:S(2)}, u32[]{:S(2)}) collective-permute-start(f32[160,256]{1,0:T(8,128)S(1)} %collective-permute-done.9.refs_3_), channel_id=1, source_target_pairs={{0,1},{1,0},{2,3},{3,2},{4,5},{5,4},{6,7},{7,6},{8,9},{9,8},{10,11... | collective-permute-start | bytes 491528 | tf_op jit(solution)/shard_map/ppermute | solution.py:410
  48.4 0.3 collective-permute-done.8.refs_2_
  48.7 0.9 %collective-permute-start.11 = (f32[160,256]{1,0:T(8,128)S(1)}, f32[160,256]{1,0:T(8,128)S(1)}, u32[]{:S(2)}, u32[]{:S(2)}) collective-permute-start(f32[160,256]{1,0:T(8,128)S(1)} %collective-permute-done.8.refs_2_), channel_id=1, source_target_pairs={{0,1},{1,0},{2,3},{3,2},{4,5},{5,4},{6,7},{7,6},{8,9},{9,8},{10,11... | collective-permute-start | bytes 491528 | tf_op jit(solution)/shard_map/ppermute | solution.py:410
  49.6 1.0 %collective-permute-done.11.refs_5_ = f32[160,256]{1,0:T(8,128)S(1)} collective-permute-done((f32[160,256]{1,0:T(8,128)S(1)}, f32[160,256]{1,0:T(8,128)S(1)}, u32[]{:S(2)}, u32[]{:S(2)}) %collective-permute-start.11) | collective-permute-done | bytes 163872 | tf_op jit(solution)/shard_map/ppermute | solution.py:410
  50.7 1.4 %group.1 = (f32[4,256,256]{2,1,0:T(8,128)S(1)}, bf16[256,256]{1,0:T(8,128)(2,1)S(1)}, bf16[256,256]{1,0:T(8,128)(2,1)S(1)}, f32[4,32,256]{2,1,0:T(8,128)S(1)}, f32[32,256]{1,0:T(8,128)S(1)}) custom-call(f32[256,256]{1,0:T(8,128)S(1)} %get-tuple-element.41.refs_0_, f32[160,256]{1,0:T(8,128)S(1)} %get-tuple-element.42.refs_1_, ...), custom_call_target="tpu_custom_call" | custom-call | flops 671088640 | bytes 4030464 | tf_op jit(solution)/shard_map/group/pallas_call | solution.py:51
  52.2 0.7 collective-permute-start.14
  53.0 0.7 collective-permute-start.15
  53.9 0.7 collective-permute-start.16
  54.7 0.7 collective-permute-start.17
  55.6 0.7 collective-permute-start.18
  56.4 0.7 collective-permute-start.19
  57.3 1.3 %collective-permute-start.20 = (f32[32,256]{1,0:T(8,128)S(1)}, f32[32,256]{1,0:T(8,128)S(1)}, u32[]{:S(2)}, u32[]{:S(2)}) collective-permute-start(f32[32,256]{1,0:T(8,128)S(1)} %hop.11), channel_id=1, source_target_pairs={{192,224},{193,225},{194,226},{195,227},{196,228},{197,229},{198,2... | collective-permute-start | bytes 98312 | tf_op jit(solution)/shard_map/ppermute | solution.py:431
  58.6 16.3 %collective-permute-done.20.refs_7_ = f32[32,256]{1,0:T(8,128)S(1)} collective-permute-done((f32[32,256]{1,0:T(8,128)S(1)}, f32[32,256]{1,0:T(8,128)S(1)}, u32[]{:S(2)}, u32[]{:S(2)}) %collective-permute-start.20) | collective-permute-done | bytes 32800 | tf_op jit(solution)/shard_map/ppermute | solution.py:431
  74.9 0.3 chips.1
  75.3 1.2 %collective-permute-start.21 = (f32[32,256]{1,0:T(8,128)S(1)}, f32[32,256]{1,0:T(8,128)S(1)}, u32[]{:S(2)}, u32[]{:S(2)}) collective-permute-start(f32[32,256]{1,0:T(8,128)S(1)} %get-tuple-element.51), channel_id=1, source_target_pairs={{0,4},{1,5},{2,6},{3,7},{4,0},{5,1},{6,2},{7,3},{8,12},{9,13},{10,... | collective-permute-start | bytes 98312 | tf_op jit(solution)/shard_map/ppermute | solution.py:443
  76.5 0.9 %collective-permute-start.22 = (f32[32,256]{1,0:T(8,128)S(1)}, f32[32,256]{1,0:T(8,128)S(1)}, u32[]{:S(2)}, u32[]{:S(2)}) collective-permute-start(f32[32,256]{1,0:T(8,128)S(1)} %get-tuple-element.52), channel_id=1, source_target_pairs={{0,2},{1,3},{2,4},{3,5},{4,6},{5,7},{6,0},{7,1},{8,10},{9,11},{10,... | collective-permute-start | bytes 98312 | tf_op jit(solution)/shard_map/ppermute | solution.py:443
  77.4 1.7 %collective-permute-start.23 = (f32[32,256]{1,0:T(8,128)S(1)}, f32[32,256]{1,0:T(8,128)S(1)}, u32[]{:S(2)}, u32[]{:S(2)}) collective-permute-start(f32[32,256]{1,0:T(8,128)S(1)} %get-tuple-element.53), channel_id=1, source_target_pairs={{0,6},{1,7},{2,0},{3,1},{4,2},{5,3},{6,4},{7,5},{8,14},{9,15},{10,... | collective-permute-start | bytes 98312 | tf_op jit(solution)/shard_map/ppermute | solution.py:443
  79.2 0.4 collective-permute-done.21.refs_1_
  79.6 0.9 collective-permute-done.22.refs_2_
  80.7 8.2 %collective-permute-start.24 = (f32[128,256]{1,0:T(8,128)S(1)}, f32[128,256]{1,0:T(8,128)S(1)}, u32[]{:S(2)}, u32[]{:S(2)}) collective-permute-start(f32[128,256]{1,0:T(8,128)S(1)} %get-tuple-element.56), channel_id=1, source_target_pairs={{0,1},{1,0},{2,3},{3,2},{4,5},{5,4},{6,7},{7,6},{8,9},{9,8},{10,11... | collective-permute-start | bytes 393224 | tf_op jit(solution)/shard_map/ppermute | solution.py:457
  89.0 1.0 %collective-permute-done.24.refs_1_ = f32[128,256]{1,0:T(8,128)S(1)} collective-permute-done((f32[128,256]{1,0:T(8,128)S(1)}, f32[128,256]{1,0:T(8,128)S(1)}, u32[]{:S(2)}, u32[]{:S(2)}) %collective-permute-start.24) | collective-permute-done | bytes 131104 | tf_op jit(solution)/shard_map/ppermute | solution.py:457
  89.9 1.1 %finish.1 = (f32[8,256]{1,0:T(8,128)}, f32[256,256]{1,0:T(8,128)}) custom-call(f32[128,256]{1,0:T(8,128)S(1)} %get-tuple-element.55.refs_0_, f32[128,256]{1,0:T(8,128)S(1)} %collective-permute-done.24.refs_1_, f32[256,256]{1,0:T(8,128)S(1)} %get-tuple-element.32.refs_0_.refs_2_, f32[256,256]{1,0:T(8,128)S(1)} %get-tuple-element.57.refs_3_, ...), custom_call_target="tpu_custom_call" | custom-call | flops 100663296 | bytes 1073152 | tf_op jit(solution)/shard_map/finish/pallas_call | solution.py:51
  (33 shorter events, 1.9 us)
Async XLA Ops:
  0.6 9.9 %copy-start.1 = (f32[8,256,256]{2,1,0:T(8,128)S(1)}, f32[8,256,256]{2,1,0:T(8,128)}, u32[]{:S(2)}) copy-start(f32[8,256,256]{2,1,0:T(8,128)} %refs_2_.1) | copy-start | bytes 6291460
  0.6 9.9 %copy-start.3 = (f32[8,256]{1,0:T(8,128)S(1)}, f32[8,256]{1,0:T(8,128)}, u32[]{:S(2)}) copy-start(f32[8,256]{1,0:T(8,128)} %refs_1_.3) | copy-start | bytes 24580
  0.7 9.9 %copy-start.4 = (f32[256]{0:T(256)S(1)}, f32[256]{0:T(256)}, u32[]{:S(2)}) copy-start(f32[256]{0:T(256)} %param.11) | copy-start | bytes 3076
  2.8 20.8 %all-to-all-start = ((f32[32,8,640]{2,1,0:T(8,128)}), f32[32,8,640]{2,1,0:T(8,128)S(1)}, u32[]{:S(2)}, u32[]{:S(2)}) async-start(f32[32,8,640]{2,1,0:T(8,128)} %pack.1.refs_3_), calls=%async_computation | async-start | bytes 1310720 | tf_op jit(solution)/shard_map/all_to_all | solution.py:356
  10.6 1.1 %copy-start = (f32[32,8,640]{2,1,0:T(8,128)S(1)}, f32[32,8,640]{2,1,0:T(8,128)}, u32[]{:S(2)}) copy-start(f32[32,8,640]{2,1,0:T(8,128)} %pack.1.refs_3_) | copy-start | bytes 1966084
  13.9 1.6 %collective-permute-start = (f32[256,256]{1,0:T(8,128)S(1)}, f32[256,256]{1,0:T(8,128)S(1)}, u32[]{:S(2)}, u32[]{:S(2)}) collective-permute-start(f32[256,256]{1,0:T(8,128)S(1)} %get-tuple-element.32.refs_0_.refs_2_), channel_id=1, source_target_pairs={{0,1},{1,0},{2,3},{3,2},{4,5},{5,4},{6,7},{7,6},{8,9},{9,8},{10,11... | collective-permute-start | bytes 786440 | tf_op jit(solution)/shard_map/ppermute | solution.py:370
  16.5 13.9 %collective-permute-start.3 = (f32[256,256]{1,0:T(8,128)}, f32[256,256]{1,0:T(8,128)}, u32[]{:S(2)}, u32[]{:S(2)}) collective-permute-start(f32[256,256]{1,0:T(8,128)} %get-tuple-element.33.refs_0_), channel_id=1, source_target_pairs={{0,4},{1,5},{2,6},{3,7},{4,0},{5,1},{6,2},{7,3},{8,12},{9,13},{10,... | collective-permute-start | bytes 786440 | tf_op jit(solution)/shard_map/ppermute | solution.py:372
  19.4 13.2 %collective-permute-start.2 = (f32[256,256]{1,0:T(8,128)}, f32[256,256]{1,0:T(8,128)}, u32[]{:S(2)}, u32[]{:S(2)}) collective-permute-start(f32[256,256]{1,0:T(8,128)} %get-tuple-element.33.refs_0_), channel_id=1, source_target_pairs={{0,6},{1,7},{2,0},{3,1},{4,2},{5,3},{6,4},{7,5},{8,14},{9,15},{10,... | collective-permute-start | bytes 786440 | tf_op jit(solution)/shard_map/ppermute | solution.py:372
  20.3 14.4 %collective-permute-start.1 = (f32[256,256]{1,0:T(8,128)}, f32[256,256]{1,0:T(8,128)}, u32[]{:S(2)}, u32[]{:S(2)}) collective-permute-start(f32[256,256]{1,0:T(8,128)} %get-tuple-element.33.refs_0_), channel_id=1, source_target_pairs={{0,2},{1,3},{2,4},{3,5},{4,6},{5,7},{6,0},{7,1},{8,10},{9,11},{10,... | collective-permute-start | bytes 786440 | tf_op jit(solution)/shard_map/ppermute | solution.py:372
  23.6 0.7 copy-start.5
  26.9 1.4 %collective-permute-start.4 = (f32[128,256]{1,0:T(8,128)S(1)}, f32[128,256]{1,0:T(8,128)S(1)}, u32[]{:S(2)}, u32[]{:S(2)}) collective-permute-start(f32[128,256]{1,0:T(8,128)S(1)} %get-tuple-element.35), channel_id=1, source_target_pairs={{0,1},{1,0},{2,3},{3,2},{4,5},{5,4},{6,7},{7,6},{8,9},{9,8},{10,11... | collective-permute-start | bytes 393224 | tf_op jit(solution)/shard_map/ppermute | solution.py:383
  28.3 23.7 %copy-start.2 = (f32[256,256]{1,0:T(8,128)S(1)}, f32[256,256]{1,0:T(8,128)}, u32[]{:S(2)}) copy-start(f32[256,256]{1,0:T(8,128)} %refs_0_.5) | copy-start | bytes 786436
  28.5 6.2 %collective-permute-start.5 = (f32[32,256]{1,0:T(8,128)S(1)}, f32[32,256]{1,0:T(8,128)S(1)}, u32[]{:S(2)}, u32[]{:S(2)}) collective-permute-start(f32[32,256]{1,0:T(8,128)S(1)} %get-tuple-element.38), channel_id=1, source_target_pairs={{0,4},{1,5},{2,6},{3,7},{4,0},{5,1},{6,2},{7,3},{8,12},{9,13},{10,... | collective-permute-start | bytes 98312 | tf_op jit(solution)/shard_map/ppermute | solution.py:395
  29.6 6.2 %collective-permute-start.6 = (f32[32,256]{1,0:T(8,128)S(1)}, f32[32,256]{1,0:T(8,128)S(1)}, u32[]{:S(2)}, u32[]{:S(2)}) collective-permute-start(f32[32,256]{1,0:T(8,128)S(1)} %get-tuple-element.39), channel_id=1, source_target_pairs={{0,2},{1,3},{2,4},{3,5},{4,6},{5,7},{6,0},{7,1},{8,10},{9,11},{10,... | collective-permute-start | bytes 98312 | tf_op jit(solution)/shard_map/ppermute | solution.py:395
  30.4 5.3 %collective-permute-start.7 = (f32[32,256]{1,0:T(8,128)S(1)}, f32[32,256]{1,0:T(8,128)S(1)}, u32[]{:S(2)}, u32[]{:S(2)}) collective-permute-start(f32[32,256]{1,0:T(8,128)S(1)} %get-tuple-element.40), channel_id=1, source_target_pairs={{0,6},{1,7},{2,0},{3,1},{4,2},{5,3},{6,4},{7,5},{8,14},{9,15},{10,... | collective-permute-start | bytes 98312 | tf_op jit(solution)/shard_map/ppermute | solution.py:395
  37.9 7.0 %collective-permute-start.10 = (f32[160,256]{1,0:T(8,128)S(1)}, f32[160,256]{1,0:T(8,128)S(1)}, u32[]{:S(2)}, u32[]{:S(2)}) collective-permute-start(f32[160,256]{1,0:T(8,128)S(1)} %get-tuple-element.42.refs_1_), channel_id=1, source_target_pairs={{0,16},{1,17},{2,18},{3,19},{4,20},{5,21},{6,22},{7,23},{8,24},{9,... | collective-permute-start | bytes 491528 | tf_op jit(solution)/shard_map/ppermute | solution.py:409
  39.5 7.7 %collective-permute-start.9 = (f32[160,256]{1,0:T(8,128)S(1)}, f32[160,256]{1,0:T(8,128)S(1)}, u32[]{:S(2)}, u32[]{:S(2)}) collective-permute-start(f32[160,256]{1,0:T(8,128)S(1)} %get-tuple-element.42.refs_1_), channel_id=1, source_target_pairs={{0,24},{1,25},{2,26},{3,27},{4,28},{5,29},{6,30},{7,31},{8,0},{9,1... | collective-permute-start | bytes 491528 | tf_op jit(solution)/shard_map/ppermute | solution.py:409
  40.3 8.4 %collective-permute-start.8 = (f32[160,256]{1,0:T(8,128)S(1)}, f32[160,256]{1,0:T(8,128)S(1)}, u32[]{:S(2)}, u32[]{:S(2)}) collective-permute-start(f32[160,256]{1,0:T(8,128)S(1)} %get-tuple-element.42.refs_1_), channel_id=1, source_target_pairs={{0,8},{1,9},{2,10},{3,11},{4,12},{5,13},{6,14},{7,15},{8,16},{9,17... | collective-permute-start | bytes 491528 | tf_op jit(solution)/shard_map/ppermute | solution.py:409
  44.9 4.7 %collective-permute-start.13 = (f32[160,256]{1,0:T(8,128)S(1)}, f32[160,256]{1,0:T(8,128)S(1)}, u32[]{:S(2)}, u32[]{:S(2)}) collective-permute-start(f32[160,256]{1,0:T(8,128)S(1)} %collective-permute-done.10.refs_4_), channel_id=1, source_target_pairs={{0,1},{1,0},{2,3},{3,2},{4,5},{5,4},{6,7},{7,6},{8,9},{9,8},{10,11... | collective-permute-start | bytes 491528 | tf_op jit(solution)/shard_map/ppermute | solution.py:410
  47.1 2.5 %collective-permute-start.12 = (f32[160,256]{1,0:T(8,128)S(1)}, f32[160,256]{1,0:T(8,128)S(1)}, u32[]{:S(2)}, u32[]{:S(2)}) collective-permute-start(f32[160,256]{1,0:T(8,128)S(1)} %collective-permute-done.9.refs_3_), channel_id=1, source_target_pairs={{0,1},{1,0},{2,3},{3,2},{4,5},{5,4},{6,7},{7,6},{8,9},{9,8},{10,11... | collective-permute-start | bytes 491528 | tf_op jit(solution)/shard_map/ppermute | solution.py:410
  48.7 2.0 %collective-permute-start.11 = (f32[160,256]{1,0:T(8,128)S(1)}, f32[160,256]{1,0:T(8,128)S(1)}, u32[]{:S(2)}, u32[]{:S(2)}) collective-permute-start(f32[160,256]{1,0:T(8,128)S(1)} %collective-permute-done.8.refs_2_), channel_id=1, source_target_pairs={{0,1},{1,0},{2,3},{3,2},{4,5},{5,4},{6,7},{7,6},{8,9},{9,8},{10,11... | collective-permute-start | bytes 491528 | tf_op jit(solution)/shard_map/ppermute | solution.py:410
  52.2 0.7 collective-permute-start.14
  53.0 0.7 collective-permute-start.15
  53.9 0.7 collective-permute-start.16
  54.7 0.7 collective-permute-start.17
  55.6 0.7 collective-permute-start.18
  56.4 0.7 collective-permute-start.19
  57.3 17.6 %collective-permute-start.20 = (f32[32,256]{1,0:T(8,128)S(1)}, f32[32,256]{1,0:T(8,128)S(1)}, u32[]{:S(2)}, u32[]{:S(2)}) collective-permute-start(f32[32,256]{1,0:T(8,128)S(1)} %hop.11), channel_id=1, source_target_pairs={{192,224},{193,225},{194,226},{195,227},{196,228},{197,229},{198,2... | collective-permute-start | bytes 98312 | tf_op jit(solution)/shard_map/ppermute | solution.py:431
  75.3 4.4 %collective-permute-start.21 = (f32[32,256]{1,0:T(8,128)S(1)}, f32[32,256]{1,0:T(8,128)S(1)}, u32[]{:S(2)}, u32[]{:S(2)}) collective-permute-start(f32[32,256]{1,0:T(8,128)S(1)} %get-tuple-element.51), channel_id=1, source_target_pairs={{0,4},{1,5},{2,6},{3,7},{4,0},{5,1},{6,2},{7,3},{8,12},{9,13},{10,... | collective-permute-start | bytes 98312 | tf_op jit(solution)/shard_map/ppermute | solution.py:443
  76.5 4.0 %collective-permute-start.22 = (f32[32,256]{1,0:T(8,128)S(1)}, f32[32,256]{1,0:T(8,128)S(1)}, u32[]{:S(2)}, u32[]{:S(2)}) collective-permute-start(f32[32,256]{1,0:T(8,128)S(1)} %get-tuple-element.52), channel_id=1, source_target_pairs={{0,2},{1,3},{2,4},{3,5},{4,6},{5,7},{6,0},{7,1},{8,10},{9,11},{10,... | collective-permute-start | bytes 98312 | tf_op jit(solution)/shard_map/ppermute | solution.py:443
  77.4 3.0 %collective-permute-start.23 = (f32[32,256]{1,0:T(8,128)S(1)}, f32[32,256]{1,0:T(8,128)S(1)}, u32[]{:S(2)}, u32[]{:S(2)}) collective-permute-start(f32[32,256]{1,0:T(8,128)S(1)} %get-tuple-element.53), channel_id=1, source_target_pairs={{0,6},{1,7},{2,0},{3,1},{4,2},{5,3},{6,4},{7,5},{8,14},{9,15},{10,... | collective-permute-start | bytes 98312 | tf_op jit(solution)/shard_map/ppermute | solution.py:443
  80.7 9.2 %collective-permute-start.24 = (f32[128,256]{1,0:T(8,128)S(1)}, f32[128,256]{1,0:T(8,128)S(1)}, u32[]{:S(2)}, u32[]{:S(2)}) collective-permute-start(f32[128,256]{1,0:T(8,128)S(1)} %get-tuple-element.56), channel_id=1, source_target_pairs={{0,1},{1,0},{2,3},{3,2},{4,5},{5,4},{6,7},{7,6},{8,9},{9,8},{10,11... | collective-permute-start | bytes 393224 | tf_op jit(solution)/shard_map/ppermute | solution.py:457
